TPU v7x, 32 devices: a whole 2x2x4 slice. The times are simulated.
32 devices in a mesh: ctx: 8 (over y, x, core), img: 4 (over z).
Axes of the slice: x: 2, y: 2, z: 4, core: 2. Of those that a mesh axis runs over, the one named last changes fastest.
Arguments:
- text: bfloat16 [1024, 4096], P('ctx'), may hold values from -6 to 6
- input_gain: float32 [4096], replicated, may hold values from 0.5 to 2
- q_weight: bfloat16 [4096, 4096], P('ctx', 'img'), may hold values from -0.09375 to 0.09375
- kv_weight: bfloat16 [4096, 2048], P('ctx'), may hold values from -0.09375 to 0.09375
- o_weight: bfloat16 [4096, 4096], P('img', 'ctx'), may hold values from -0.5 to 0.5
- q_gain: float32 [128], replicated, may hold values from 0.5 to 12, as said below
- k_gain: float32 [128], replicated, may hold values from 0.5 to 12, as said below
- attn_gate: float32 [1], replicated, may hold values from 0.3 to 1.5
- vision: bfloat16 [8, 64, 4096], P('img', 'ctx'), may hold values from -6 to 6
- segment_ids: int32 [1024], P('ctx'), may hold values from 0 to 31, as said below
- seg_images: int32 [32, 2], replicated, may hold values from 0 to 7, as said below
- image_slot: int32 [8], replicated, may hold values from 0 to 7, each once
Outputs:
- mixed: bfloat16 [1024, 4096], P('ctx', 'img')
Inputs may be any that keep to these rules, and one draw needn't show every extreme that they name: `segment_ids`: numbers never fall along the tokens; block c of 128 tokens uses numbers from c * 4 on, 1 to 4 segments a block, and some block has 4. `seg_images`: each row names 2 different images; the tokens of one block of 128 see at most 8 different images, and some block sees exactly 8. `image_slot`: A permutation. `q_gain`: Positive. `k_gain`: Positive.
All inputs are finite; a program needn't handle non-finite values.
Results may differ from a plain program's by a relative error of at most 0.022.
The roundings to bfloat16 on the way count: a program that leaves them out, or rounds other values in their place, can miss the bound.
Values may be sent and summed in bfloat16 or wider, within the bound.
No kernel may reach another device: no remote copies, remote signals or barrier semaphores. Data moves between devices by JAX's collectives and lax.ppermute only.
A program may use at most 64 MiB of HBM per device.

v0:
```python
import jax
import jax.numpy as jnp
from jax import lax
from jax.experimental import pallas as pl
from jax.experimental.pallas import tpu as pltpu
from jax.sharding import PartitionSpec as P

KVH = 8


EPS = 1e-05
NEG = -1e30


def head_norm(values, gain):
    mean_sq = jnp.mean(values * values, axis=-1, keepdims=True)
    return values * lax.rsqrt(mean_sq + EPS) * gain


def attend(query, keys, values, mask):
    scale = query.shape[-1] ** (-0.5)
    scores = jnp.einsum("tkgd,nkd->tkgn", query, keys, preferred_element_type=jnp.float32) * scale
    live = mask[:, None, None, :]
    scores = jnp.where(live, scores, NEG)
    top = jnp.max(scores, axis=-1)
    weights = jnp.where(live, jnp.exp(scores - top[..., None]), 0.0)
    total = jnp.sum(weights, axis=-1)
    acc = jnp.einsum(
        "tkgn,nkd->tkgd", weights.astype(jnp.bfloat16), values, preferred_element_type=jnp.float32
    )
    return acc / total[..., None]


def general(
    text,
    input_gain,
    q_weight,
    kv_weight,
    o_weight,
    q_gain,
    k_gain,
    attn_gate,
    vision,
    segment_ids,
    seg_images,
    image_slot,
):
    tokens_here = text.shape[0]
    head_dim = q_gain.shape[0]
    ctx_count = lax.axis_size("ctx")
    img_count = lax.axis_size("img")
    heads_here = q_weight.shape[1] // head_dim
    kv_heads = max(1, KVH // img_count)
    group = heads_here // kv_heads
    slots_here, vt_dev = vision.shape[:2]
    rows_here = slots_here * vt_dev

    o_full = lax.all_gather(o_weight, "ctx", axis=1, tiled=True)
    vision_cols = lax.all_to_all(
        vision.reshape(rows_here, -1), "ctx", split_axis=1, concat_axis=0, tiled=True
    )
    hidden = head_norm(text.astype(jnp.float32), input_gain).astype(jnp.bfloat16)
    hidden_cols = lax.all_to_all(hidden, "ctx", split_axis=1, concat_axis=0, tiled=True)

    kv_share = jnp.dot(vision_cols, kv_weight, preferred_element_type=jnp.float32)
    kv_shares = lax.all_to_all(
        kv_share.reshape(ctx_count, rows_here, -1), "ctx", split_axis=0, concat_axis=0, tiled=True
    )
    projected = jnp.sum(kv_shares, axis=0).reshape(rows_here, KVH, 2, head_dim)
    keys = head_norm(projected[:, :, 0], k_gain).astype(jnp.bfloat16)
    values = projected[:, :, 1].astype(jnp.bfloat16)
    kv_rows = jnp.stack((keys, values), axis=2)
    owners = jnp.arange(img_count)[:, None] * KVH // img_count + jnp.arange(kv_heads)[None, :]
    kv_out = jnp.take(kv_rows, owners, axis=1).transpose(1, 0, 2, 3, 4)
    kv_in = lax.all_to_all(kv_out, "img", split_axis=0, concat_axis=0, tiled=True)
    kv_all = lax.all_gather(kv_in, "ctx", axis=0, tiled=False)

    q_share = jnp.dot(hidden_cols, q_weight, preferred_element_type=jnp.float32)
    q_shares = lax.all_to_all(
        q_share.astype(jnp.bfloat16).reshape(ctx_count, tokens_here, -1),
        "ctx",
        split_axis=0,
        concat_axis=0,
        tiled=True,
    )
    query = jnp.sum(q_shares.astype(jnp.float32), axis=0)
    query = head_norm(query.reshape(tokens_here, kv_heads, group, head_dim), q_gain).astype(
        jnp.bfloat16
    )

    slots = img_count * slots_here
    own_slots = jnp.take(image_slot, jnp.take(seg_images, segment_ids, axis=0), axis=0)
    slot_ids = jnp.arange(slots, dtype=jnp.int32)
    sees = jnp.any(own_slots[:, :, None] == slot_ids[None, None, :], axis=1)
    flat = kv_all.reshape(ctx_count * slots * vt_dev, kv_heads, 2, head_dim)
    mask = jnp.broadcast_to(
        sees[:, None, :, None], (tokens_here, ctx_count, slots, vt_dev)
    ).reshape(tokens_here, -1)
    context = attend(query, flat[:, :, 0], flat[:, :, 1], mask)
    context = context.astype(jnp.bfloat16).reshape(tokens_here, heads_here * head_dim)
    partial_terms = jnp.dot(context, o_full, preferred_element_type=jnp.float32)
    width = partial_terms.shape[1] // img_count
    shares = lax.all_to_all(
        partial_terms.astype(jnp.bfloat16).reshape(tokens_here, img_count, width),
        "img",
        split_axis=1,
        concat_axis=1,
        tiled=True,
    )
    update = jnp.sum(shares.astype(jnp.float32), axis=1)
    own_text = lax.dynamic_slice_in_dim(text, lax.axis_index("img") * width, width, 1)
    return (own_text.astype(jnp.float32) + jnp.tanh(attn_gate[0]) * update).astype(jnp.bfloat16)


BF16, F32 = jnp.bfloat16, jnp.float32
SMEM = pl.BlockSpec(memory_space=pltpu.SMEM)
VMEM = pl.BlockSpec(memory_space=pltpu.VMEM)
CHIPS = 4


def call(kernel, args, specs, outs, out_specs=None, scratch=(), flops=0, size=0, name=None, grid=(), limit=24):
    return pl.pallas_call(
        kernel,
        out_shape=outs,
        in_specs=specs,
        out_specs=[VMEM] * len(outs) if out_specs is None else out_specs,
        scratch_shapes=scratch,
        grid=grid,
        compiler_params=pltpu.CompilerParams(vmem_limit_bytes=limit * 2**20),
        cost_estimate=pl.CostEstimate(flops=flops, bytes_accessed=size, transcendentals=0),
        name=name,
    )(*args)


def block(index, size):
    return pl.ds(pl.multiple_of(index * size, size), size)


def start_kernel(where, text_hbm, gain, vis_hbm, q_hbm, *refs):
    pieces, refs = refs[:CHIPS], refs[CHIPS:]
    near, far, text_keep, text_give, q_keep, q_give, text, vis, scale, sems = refs
    chip, core, plane = where[0], where[1], where[2]
    tokens, width = text.shape
    part = width // 2
    half = text_keep.shape[1]
    step = 16
    first = pltpu.make_async_copy(vis_hbm, vis, sems.at[0])
    first.start()
    copies = []
    for k, r in enumerate(range(0, tokens, 2 * step)):
        rows = pl.ds(r, 2 * step)
        copies.append(pltpu.make_async_copy(text_hbm.at[rows, :], text.at[rows, :], sems.at[3 + k]))
        copies[-1].start()
    cuts = [
        pltpu.make_async_copy(q_hbm.at[:, block(core, half)], q_keep, sems.at[1]),
        pltpu.make_async_copy(q_hbm.at[:, block(1 - core, half)], q_give, sems.at[2]),
    ]
    for copy in cuts:
        copy.start()
    first.wait()
    for s in range(CHIPS):
        pieces[s][...] = vis[:, block(chip ^ s, pieces[s].shape[1])]
    for r in range(0, tokens, step):
        if r % (2 * step) == 0:
            copies[r // (2 * step)].wait()
        x = text[r : r + step, :].astype(F32)
        mean_sq = jnp.mean(x * x, axis=-1, keepdims=True)
        scale[r : r + step, :] = jnp.broadcast_to(lax.rsqrt(mean_sq + EPS), (step, 128))
    line = chip // 2
    for out, index in ((far, 1 - line), (near, line)):
        cols = block(index, part)
        row_gain = gain[:, cols]
        for r in range(0, tokens, step):
            x = text[r : r + step, cols].astype(F32)
            out[r : r + step, :] = (x * scale[r : r + step, 0:1] * row_gain).astype(BF16)
    text_keep[...] = text[:, block(2 * plane + core, half)]
    text_give[...] = text[:, block(2 * plane + 1 - core, half)]
    for copy in cuts:
        copy.wait()


def kv_kernel(where, vis, vis_other, kv_own, kv_other, *refs):
    shares, (other, near_total, sems) = refs[:CHIPS], refs[CHIPS:]
    core = where[1]
    rows = kv_own.shape[0]
    head = kv_own.shape[1] // (2 * CHIPS)
    copies = []
    for j in range(CHIPS):
        copies.append(
            pltpu.make_async_copy(
                kv_other.at[:, block(2 * j + core, head)],
                other.at[:, pl.ds(j * head, head)],
                sems.at[j],
            )
        )
        copies[-1].start()
    near, far = block(core, rows), block(1 - core, rows)
    x_near = jnp.concatenate((vis[:, near], vis_other[:, near]), axis=0)
    x_far = jnp.concatenate((vis[:, far], vis_other[:, far]), axis=0)
    total = vis.shape[0]
    count = total // CHIPS
    for j in range(CHIPS):
        near_total[:, j * head : (j + 1) * head] = jnp.dot(
            x_near, kv_own[:, block(2 * j + core, head)], preferred_element_type=F32
        )
    for j in range(CHIPS):
        copies[j].wait()
        cols = slice(j * head, (j + 1) * head)
        out = near_total[:, cols] + jnp.dot(x_far, other[:, cols], preferred_element_type=F32)
        for s in range(CHIPS):
            shares[s][:count, cols] = out[s * count : (s + 1) * count]
            shares[s][count:, cols] = out[total + s * count : total + (s + 1) * count]


def kv_norm_kernel(where, k_gain, *refs):
    shares, (here, there, give) = refs[:CHIPS], refs[CHIPS:]
    plane = where[2]
    lines, head = here.shape
    dim = head // 2
    for t, (out, row) in enumerate(((here, 0), (give, 0), (there, 0), (give, lines))):
        cols = block(plane ^ t, head)
        total = (shares[0][:, cols] + shares[1][:, cols]) + (shares[2][:, cols] + shares[3][:, cols])
        keys = head_norm(total[:, :dim], k_gain[...])
        out[row : row + lines, :dim] = keys.astype(BF16)
        out[row : row + lines, dim:] = total[:, dim:].astype(BF16)


def kv_turn_kernel(there, landed, out):
    lines = there.shape[0]
    out[:lines, :] = there[...]
    out[lines:, :] = landed[lines:, :]


def kv_join_kernel(here, landed, last, out):
    lines = here.shape[0]
    out[:lines, :] = here[...]
    out[lines : 2 * lines, :] = landed[:lines, :]
    out[2 * lines :, :] = last[...]


def query_share(index, own, other, first, second, flip):
    rows = first.shape[0]
    total = None
    for weight, k in ((first, index), (second, index ^ flip)):
        cols = block(k, rows)
        x = jnp.concatenate((own[:, cols], other[:, cols]), axis=0)
        share = jnp.dot(x, weight[...], preferred_element_type=F32)
        total = share if total is None else total + share
    return total


def early_kernel(where, own, other, q_keep, q_other, out):
    index = 2 * lax.rem(where[0], 2) + where[1]
    out[...] = query_share(index, own, other, q_keep, q_other, 1)


def late_kernel(where, own, other, q_side, q_corner, early, out):
    index = (2 * lax.rem(where[0], 2) + where[1]) ^ 2
    share = early[...] + query_share(index, own, other, q_side, q_corner, 1)
    out[...] = share.astype(out.dtype)


def attend_kernel(q_gain, first, landed, *refs):
    kv, (bias, context) = refs[:CHIPS], refs[CHIPS:]
    dim = q_gain.shape[1]
    rows, half = context.shape
    keys = jnp.concatenate([x[:, :dim] for x in kv], axis=0)
    values = jnp.concatenate([x[:, dim:] for x in kv], axis=0)
    step = 128
    for r in range(0, rows, step):
        for g in range(half // dim):
            cols = slice(g * dim, (g + 1) * dim)
            query = first[r : r + step, cols] + landed[r : r + step, cols].astype(F32)
            query = head_norm(query, q_gain[...]).astype(BF16)
            scores = lax.dot_general(
                query, keys, (((1,), (1,)), ((), ())), preferred_element_type=F32
            )
            scores = scores * dim ** (-0.5) + bias[r : r + step, :]
            weights = jnp.exp(scores - jnp.max(scores, axis=-1, keepdims=True))
            total = jnp.sum(weights, axis=-1, keepdims=True)
            acc = jnp.dot(weights.astype(BF16), values, preferred_element_type=F32)
            context[r : r + step, cols] = (acc / total).astype(BF16)


def out_kernel(where, near, far, o_own, o_early, o_late, own, other):
    core = where[1]
    tokens, width = own.shape
    half = near.shape[1]
    turned = jnp.concatenate((far[tokens:, :], far[:tokens, :]), axis=0)
    share = jnp.dot(near[...], o_own[block(core, half), :], preferred_element_type=F32)
    share += jnp.dot(turned, o_own[block(1 - core, half), :], preferred_element_type=F32)
    own[:, : width // 2] = share[:tokens].astype(BF16)
    other[:, : width // 2] = share[tokens:].astype(BF16)
    top = jnp.where(core == 0, near[...], turned)
    low = jnp.where(core == 0, turned, near[...])
    share = jnp.dot(top, o_early[...], preferred_element_type=F32)
    share += jnp.dot(low, o_late[...], preferred_element_type=F32)
    own[:, width // 2 :] = share[:tokens].astype(BF16)
    other[:, width // 2 :] = share[tokens:].astype(BF16)


def pick_kernel(where, own, landed, *outs):
    first = where[0] ^ where[2]
    half = outs[0].shape[1]
    for t in range(CHIPS):
        for s in range(CHIPS):

            @pl.when((first ^ t) == s)
            def _():
                outs[t][...] = (own, landed)[s % 2][:, (s // 2) * half : (s // 2 + 1) * half]


def mixed_rows(gate, text, shares):
    x = [share[...].astype(F32) for share in shares]
    update = (x[0] + x[1]) + (x[2] + x[3])
    return (text[...].astype(F32) + gate[0] * update).astype(BF16)


def give_kernel(gate, text, *refs):
    refs[CHIPS][...] = mixed_rows(gate, text, refs[:CHIPS])


def last_kernel(where, gate, text, back, *refs):
    shares, out = refs[:CHIPS], refs[CHIPS]
    core = where[1]
    half = text.shape[1]
    out[:, block(core, half)] = mixed_rows(gate, text, shares)
    out[:, block(1 - core, half)] = back[...]


def paired(
    text,
    input_gain,
    q_weight,
    kv_weight,
    o_weight,
    q_gain,
    k_gain,
    attn_gate,
    vision,
    segment_ids,
    seg_images,
    image_slot,
):
    ctx_count = lax.axis_size("ctx")
    place, plane = lax.axis_index("ctx"), lax.axis_index("img")
    chip, core = place // 2, place % 2
    where = jnp.stack((chip, core, plane)).astype(jnp.int32)
    tokens, width = text.shape
    head_dim = q_gain.shape[0]
    rows_dev, cols_plane = q_weight.shape
    half = cols_plane // 2
    part = 2 * rows_dev
    slots_here, vt_dev = vision.shape[:2]
    vis_here = slots_here * vt_dev
    kv_cols = kv_weight.shape[1] // 2

    def shape(rows, cols, kind=BF16):
        return jax.ShapeDtypeStruct((rows, cols), kind)

    def swap(x):
        return lax.ppermute(x, "ctx", [(k, k ^ 1) for k in range(ctx_count)])

    def peer(x, s):
        return lax.ppermute(x, "ctx", [(k, k ^ (2 * s)) for k in range(ctx_count)])

    def along_x(x):
        return peer(x, 1)

    def along_y(x):
        return peer(x, 2)

    def across(x, t):
        return lax.ppermute(x, "img", [(k, k ^ t) for k in range(CHIPS)])

    steps = range(1, CHIPS)
    vis = vision.reshape(vis_here, width)
    kv_other = swap(kv_weight)

    anywhere = pl.BlockSpec(memory_space=pl.ANY)
    *vis_pieces, near, far, text_keep, text_give, q_keep, q_give = call(
        start_kernel,
        (where, text, input_gain[None], vis, q_weight),
        [SMEM, anywhere, VMEM, anywhere, anywhere],
        [shape(vis_here, part)] * CHIPS
        + [shape(tokens, width // 2)] * 2
        + [shape(tokens, half)] * 2
        + [shape(rows_dev, half)] * 2,
        scratch=[
            pltpu.VMEM((tokens, width), BF16),
            pltpu.VMEM((vis_here, width), BF16),
            pltpu.VMEM((tokens, 128), F32),
            pltpu.SemaphoreType.DMA((3 + tokens // 32,)),
        ],
        flops=8 * tokens * width,
        size=4 * 2**20,
        name="start",
        limit=60,
    )
    vis_own = jnp.concatenate([vis_pieces[0]] + [peer(vis_pieces[s], s) for s in steps])
    vis_other = swap(vis_own)
    q_side, q_other = along_x(q_keep), swap(q_give)
    far = along_y(far)

    shares = call(
        kv_kernel,
        (where, vis_own, vis_other, kv_weight, kv_other),
        [SMEM] + [VMEM] * 3 + [pl.BlockSpec(memory_space=pl.ANY)],
        [shape(2 * vis_here, kv_cols, F32)] * CHIPS,
        scratch=[
            pltpu.VMEM((rows_dev, kv_cols), BF16),
            pltpu.VMEM((8 * vis_here, kv_cols), F32),
            pltpu.SemaphoreType.DMA((CHIPS,)),
        ],
        flops=4 * vis_here * ctx_count * part * kv_cols,
        size=4 * 2**20,
        name="kv_shares",
    )
    shares = [shares[0]] + [peer(shares[s], s) for s in steps]
    shares, q_side, far = lax.optimization_barrier((shares, q_side, far))
    here, there, give = call(
        kv_norm_kernel,
        (where, k_gain[None], *shares),
        [SMEM] + [VMEM] * (1 + CHIPS),
        [shape(2 * vis_here, 2 * head_dim)] * 2 + [shape(4 * vis_here, 2 * head_dim)],
        name="kv_norm",
    )
    blocks = ((far, swap(far)), (near, swap(near)))
    early = [
        call(
            early_kernel,
            (where, *pair, q_keep, q_other),
            [SMEM] + [VMEM] * 4,
            [shape(2 * tokens, half, F32)],
            flops=4 * tokens * part * half,
            size=2 * 2**20,
            name="q_early",
        )[0]
        for pair in blocks
    ]
    kv_z, early[0] = lax.optimization_barrier((across(give, 1), early[0]))
    turn = call(
        kv_turn_kernel,
        (there, kv_z),
        [VMEM] * 2,
        [shape(4 * vis_here, 2 * head_dim)],
        name="kv_turn",
    )[0]
    kv_first = call(
        kv_join_kernel,
        (here, kv_z, across(turn, 2)),
        [VMEM] * 3,
        [shape(8 * vis_here, 2 * head_dim)],
        name="kv_join",
    )[0]
    kv_all = [kv_first] + [peer(kv_first, s) for s in steps]
    q_behind, _ = lax.optimization_barrier((q_other, shares[0]))
    q_corner = along_x(q_behind)
    q_corner, kv_all[1] = lax.optimization_barrier((q_corner, kv_all[1]))

    o_early, _ = lax.optimization_barrier((o_weight[:half], here))
    early[1], o_early = lax.optimization_barrier((early[1], along_y(o_early)))
    q_far, q_first = [
        call(
            late_kernel,
            (where, *blocks[k], q_side, q_corner, early[k]),
            [SMEM] + [VMEM] * 5,
            [shape(2 * tokens, half, kind)],
            flops=4 * tokens * part * half,
            size=2 * 2**20,
            name="q_late",
        )[0]
        for k, kind in ((0, BF16), (1, F32))
    ]
    landed = along_y(q_far)
    o_late, _ = lax.optimization_barrier((o_weight[half:], q_far))
    o_late = along_y(o_late)

    ids = jnp.concatenate((segment_ids, swap(segment_ids)))
    images = jnp.arange(image_slot.shape[0])
    slot_of = jnp.sum(
        jnp.where(seg_images[:, :, None] == images, image_slot[None, None, :], 0), axis=2
    )
    numbers = jnp.arange(seg_images.shape[0])
    own_slots = jnp.sum(
        jnp.where((ids[:, None] == numbers)[:, :, None], slot_of[None], 0), axis=1
    )
    key_rows = jnp.arange(CHIPS * CHIPS * 2 * vis_here)
    key_plane = plane ^ (key_rows // (2 * vis_here) % CHIPS)
    key_slot = key_plane * slots_here + key_rows // vt_dev % slots_here
    sees = jnp.any(own_slots[:, :, None] == key_slot, axis=1)
    bias = jnp.where(sees, 0.0, NEG).astype(F32)

    context = call(
        attend_kernel,
        (q_gain[None], q_first, landed, *kv_all, bias),
        [VMEM] * (4 + CHIPS),
        [shape(2 * tokens, half)],
        flops=8 * tokens * half * bias.shape[1],
        size=2 * 2**20,
        name="attend",
    )[0]

    context_x = along_x(context)
    shares = [
        call(
            out_kernel,
            (where, x, swap(x), o_weight, o_early, o_late),
            [SMEM] + [VMEM] * 5,
            [shape(tokens, 2 * half)] * 2,
            flops=8 * tokens * cols_plane * half,
            size=2 * 2**20,
            name="o_share",
        )
        for x in (context_x, context)
    ]
    summands = []
    for rows in (1, 0):
        picked = call(
            pick_kernel,
            (where, shares[1][rows], along_x(shares[0][rows])),
            [SMEM] + [VMEM] * 2,
            [shape(tokens, half)] * CHIPS,
            flops=2**20,
            size=2**20,
            name="pick",
        )
        summands.append([picked[0]] + [across(picked[t], t) for t in steps])
    gate = jnp.tanh(attn_gate)
    give = call(
        give_kernel,
        (gate, swap(text_give), *summands[0]),
        [SMEM] + [VMEM] * (1 + CHIPS),
        [shape(tokens, half)],
        flops=2**20,
        size=2**20,
        name="mix_give",
    )[0]
    return call(
        last_kernel,
        (where, gate, text_keep, swap(give), *summands[1]),
        [SMEM, SMEM] + [VMEM] * (2 + CHIPS),
        [shape(tokens, 2 * half)],
        flops=2**20,
        size=2**20,
        name="mix_keep",
    )[0]


def solution(mesh):
    fits = mesh.shape["img"] == 4 and mesh.shape["ctx"] == 8
    return jax.shard_map(
        paired if fits else general,
        mesh=mesh,
        in_specs=(
            P("ctx", None),
            P(),
            P("ctx", "img"),
            P("ctx", None),
            P("img", "ctx"),
            P(),
            P(),
            P(),
            P("img", "ctx", None),
            P("ctx"),
            P(),
            P(),
        ),
        out_specs=P("ctx", "img"),
        check_vma=False,
    )
```

profile of v0, /device:TPU:0, one launch (start us, length us, event | category | flops | bytes accessed | tf_op | source)
XLA Modules:
  0.0 105.5 jit_solution(2905438773727664194)
XLA Ops:
  1.1 4.1 %start.1 = (bf16[16,1024]{1,0:T(8,128)(2,1)}, bf16[16,1024]{1,0:T(8,128)(2,1)}, bf16[16,1024]{1,0:T(8,128)(2,1)}, bf16[16,1024]{1,0:T(8,128)(2,1)}, bf16[128,204...) custom-call(s32[3]{0:T(128)} %pad_add_fusion.1.where, ...), custom_call_target="tpu_custom_call" | custom-call | flops 4194304 | bytes 4194304 | tf_op jit(solution)/shard_map/start/pallas_call | solution.py:122
  5.2 2.6 %collective-permute-start.2 = (bf16[16,1024]{1,0:T(8,128)(2,1)}, bf16[16,1024]{1,0:T(8,128)(2,1)S(1)}, u32[]{:S(2)}, u32[]{:S(2)}) collective-permute-start(bf16[16,1024]{1,0:T(8,128)(2,1)} %get-tuple-element.53), channel_id=1, source_target_pairs={{0,8},{4,12},{8,0},{12,4},{16,24},{20,28},{24,16},{28,20},{1,9},{5... | collective-permute-start | bytes 98312 | tf_op jit(solution)/shard_map/ppermute | solution.py:365
  7.7 1.5 %collective-permute-start.3 = (bf16[16,1024]{1,0:T(8,128)(2,1)}, bf16[16,1024]{1,0:T(8,128)(2,1)S(1)}, u32[]{:S(2)}, u32[]{:S(2)}) collective-permute-start(bf16[16,1024]{1,0:T(8,128)(2,1)} %get-tuple-element.54), channel_id=1, source_target_pairs={{0,16},{4,20},{8,24},{12,28},{16,0},{20,4},{24,8},{28,12},{1,17},{... | collective-permute-start | bytes 98312 | tf_op jit(solution)/shard_map/ppermute | solution.py:365
  9.3 1.9 %collective-permute-start.10 = (bf16[512,512]{1,0:T(8,128)(2,1)}, bf16[512,512]{1,0:T(8,128)(2,1)S(1)}, u32[]{:S(2)}, u32[]{:S(2)}) collective-permute-start(bf16[512,512]{1,0:T(8,128)(2,1)} %get-tuple-element.60.q_keep), channel_id=1, source_target_pairs={{0,8},{4,12},{8,0},{12,4},{16,24},{20,28},{24,16},{28,20},{1,9},{5... | collective-permute-start | bytes 1572872 | tf_op jit(solution)/shard_map/ppermute | solution.py:365
  12.0 1.5 %collective-permute-start.11 = (bf16[128,2048]{1,0:T(8,128)(2,1)}, bf16[128,2048]{1,0:T(8,128)(2,1)S(1)}, u32[]{:S(2)}, u32[]{:S(2)}) collective-permute-start(bf16[128,2048]{1,0:T(8,128)(2,1)} %get-tuple-element.61), channel_id=1, source_target_pairs={{0,16},{4,20},{8,24},{12,28},{16,0},{20,4},{24,8},{28,12},{1,17},{... | collective-permute-start | bytes 1572872 | tf_op jit(solution)/shard_map/ppermute | solution.py:365
  13.5 1.1 %collective-permute-done.4 = bf16[16,1024]{1,0:T(8,128)(2,1)S(1)} collective-permute-done((bf16[16,1024]{1,0:T(8,128)(2,1)}, bf16[16,1024]{1,0:T(8,128)(2,1)S(1)}, u32[]{:S(2)}, u32[]{:S(2)}) %collective-permute-start.4) | collective-permute-done | bytes 32800 | tf_op jit(solution)/shard_map/ppermute | solution.py:365
  16.0 2.6 %kv_shares.1 = (f32[32,1024]{1,0:T(8,128)S(1)}, f32[32,1024]{1,0:T(8,128)S(1)}, f32[32,1024]{1,0:T(8,128)S(1)}, f32[32,1024]{1,0:T(8,128)S(1)}) custom-call(s32[3]{0:T(128)S(1)} %copy-done.5, bf16[64,1024]{1,0:T(8,128)(2,1)S(1)} %constant_dynamic-update-slice_fusion.vis, bf16[64,1024]{1,0:T(8,128)(2,1)S(1)} %collective-permute-done.5.vis_other, ...), custom_call_target="tpu_custom_call" | custom-call | flops 536870912 | bytes 4194304 | tf_op jit(solution)/shard_map/kv_shares/pallas_call | solution.py:122
  19.3 5.6 %collective-permute-done.10.q_side = bf16[512,512]{1,0:T(8,128)(2,1)S(1)} collective-permute-done((bf16[512,512]{1,0:T(8,128)(2,1)}, bf16[512,512]{1,0:T(8,128)(2,1)S(1)}, u32[]{:S(2)}, u32[]{:S(2)}) %collective-permute-start.10) | collective-permute-done | bytes 524320 | tf_op jit(solution)/shard_map/ppermute | solution.py:365
  24.9 2.3 %collective-permute-start.9 = (f32[32,1024]{1,0:T(8,128)S(1)}, f32[32,1024]{1,0:T(8,128)S(1)}, u32[]{:S(2)}, u32[]{:S(2)}) collective-permute-start(f32[32,1024]{1,0:T(8,128)S(1)} %get-tuple-element.59), channel_id=1, source_target_pairs={{0,24},{4,28},{8,16},{12,20},{16,8},{20,12},{24,0},{28,4},{1,25},{... | collective-permute-start | bytes 393224 | tf_op jit(solution)/shard_map/ppermute | solution.py:365
  28.0 3.3 %collective-permute-done.8.refs_2_ = f32[32,1024]{1,0:T(8,128)S(1)} collective-permute-done((f32[32,1024]{1,0:T(8,128)S(1)}, f32[32,1024]{1,0:T(8,128)S(1)}, u32[]{:S(2)}, u32[]{:S(2)}) %collective-permute-start.8) | collective-permute-done | bytes 131104 | tf_op jit(solution)/shard_map/ppermute | solution.py:365
  33.0 1.6 %collective-permute-start.14 = (bf16[64,256]{1,0:T(8,128)(2,1)S(1)}, bf16[64,256]{1,0:T(8,128)(2,1)S(1)}, u32[]{:S(2)}, u32[]{:S(2)}) collective-permute-start(bf16[64,256]{1,0:T(8,128)(2,1)S(1)} %get-tuple-element.70), channel_id=1, source_target_pairs={{0,1},{1,0},{2,3},{3,2},{4,5},{5,4},{6,7},{7,6},{8,9},{9,8},{10,11... | collective-permute-start | bytes 98312 | tf_op jit(solution)/shard_map/ppermute | solution.py:374
  34.7 1.6 %collective-permute-start.18 = (bf16[512,512]{1,0:T(8,128)(2,1)S(1)}, bf16[512,512]{1,0:T(8,128)(2,1)S(1)}, u32[]{:S(2)}, u32[]{:S(2)}) collective-permute-start(bf16[512,512]{1,0:T(8,128)(2,1)S(1)} %get-tuple-element.75), channel_id=1, source_target_pairs={{0,16},{4,20},{8,24},{12,28},{16,0},{20,4},{24,8},{28,12},{1,17},{... | collective-permute-start | bytes 1572872 | tf_op jit(solution)/shard_map/ppermute | solution.py:365
  37.3 2.7 %collective-permute-start.16 = (bf16[64,256]{1,0:T(8,128)(2,1)S(1)}, bf16[64,256]{1,0:T(8,128)(2,1)S(1)}, u32[]{:S(2)}, u32[]{:S(2)}) collective-permute-start(bf16[64,256]{1,0:T(8,128)(2,1)S(1)} %kv_turn.1), channel_id=1, source_target_pairs={{0,2},{1,3},{2,0},{3,1},{4,6},{5,7},{6,4},{7,5},{8,10},{9,11},{10,... | collective-permute-start | bytes 98312 | tf_op jit(solution)/shard_map/ppermute | solution.py:374
  40.0 2.1 %collective-permute-done.16.last = bf16[64,256]{1,0:T(8,128)(2,1)S(1)} collective-permute-done((bf16[64,256]{1,0:T(8,128)(2,1)S(1)}, bf16[64,256]{1,0:T(8,128)(2,1)S(1)}, u32[]{:S(2)}, u32[]{:S(2)}) %collective-permute-start.16) | collective-permute-done | bytes 32800 | tf_op jit(solution)/shard_map/ppermute | solution.py:374
  43.2 1.3 %collective-permute-start.20 = (bf16[128,256]{1,0:T(8,128)(2,1)S(1)}, bf16[128,256]{1,0:T(8,128)(2,1)S(1)}, u32[]{:S(2)}, u32[]{:S(2)}) collective-permute-start(bf16[128,256]{1,0:T(8,128)(2,1)S(1)} %kv_join.1.refs_0_), channel_id=1, source_target_pairs={{0,16},{4,20},{8,24},{12,28},{16,0},{20,4},{24,8},{28,12},{1,17},{... | collective-permute-start | bytes 196616 | tf_op jit(solution)/shard_map/ppermute | solution.py:365
  44.5 1.7 %collective-permute-done.13.q_corner = bf16[512,512]{1,0:T(8,128)(2,1)S(1)} collective-permute-done((bf16[512,512]{1,0:T(8,128)(2,1)S(1)}, bf16[512,512]{1,0:T(8,128)(2,1)S(1)}, u32[]{:S(2)}, u32[]{:S(2)}) %collective-permute-start.13) | collective-permute-done | bytes 524320 | tf_op jit(solution)/shard_map/ppermute | solution.py:365
  46.2 1.8 %collective-permute-start.21 = (bf16[128,256]{1,0:T(8,128)(2,1)S(1)}, bf16[128,256]{1,0:T(8,128)(2,1)S(1)}, u32[]{:S(2)}, u32[]{:S(2)}) collective-permute-start(bf16[128,256]{1,0:T(8,128)(2,1)S(1)} %kv_join.1.refs_0_), channel_id=1, source_target_pairs={{0,24},{4,28},{8,16},{12,20},{16,8},{20,12},{24,0},{28,4},{1,25},{... | collective-permute-start | bytes 196616 | tf_op jit(solution)/shard_map/ppermute | solution.py:365
  50.6 1.6 %collective-permute-start.24 = (bf16[512,512]{1,0:T(8,128)(2,1)S(1)}, bf16[512,512]{1,0:T(8,128)(2,1)S(1)}, u32[]{:S(2)}, u32[]{:S(2)}) collective-permute-start(bf16[512,512]{1,0:T(8,128)(2,1)S(1)} %get-tuple-element.80), channel_id=1, source_target_pairs={{0,16},{4,20},{8,24},{12,28},{16,0},{20,4},{24,8},{28,12},{1,17},{... | collective-permute-start | bytes 1572872 | tf_op jit(solution)/shard_map/ppermute | solution.py:365
  53.2 5.1 %collective-permute-done.19.landed = bf16[256,512]{1,0:T(8,128)(2,1)S(1)} collective-permute-done((bf16[256,512]{1,0:T(8,128)(2,1)S(1)}, bf16[256,512]{1,0:T(8,128)(2,1)S(1)}, u32[]{:S(2)}, u32[]{:S(2)}) %collective-permute-start.19) | collective-permute-done | bytes 262176 | tf_op jit(solution)/shard_map/ppermute | solution.py:365
  58.3 2.3 %attend.1.near = bf16[256,512]{1,0:T(8,128)(2,1)S(1)} custom-call(f32[1,128]{1,0:T(1,128)S(1)} %bitcast.8, f32[256,512]{1,0:T(8,128)S(1)} %q_late.2.first, bf16[256,512]{1,0:T(8,128)(2,1)S(1)} %collective-permute-done.19.landed, bf16[128,256]{1,0:T(8,128)(2,1)S(1)} %kv_join.1.refs_0_, bf16[128,256]{1,0:T(8,128)(2,1)S(1)} %collective-permute-done.17.refs_1_, ...), custom_call_target="tpu_custom_call" | custom-call | flops 268435456 | bytes 2097152 | tf_op jit(solution)/shard_map/attend/pallas_call | solution.py:122
  60.6 1.0 collective-permute-start.25
  61.6 5.4 %collective-permute-done.25.near = bf16[256,512]{1,0:T(8,128)(2,1)S(1)} collective-permute-done((bf16[256,512]{1,0:T(8,128)(2,1)S(1)}, bf16[256,512]{1,0:T(8,128)(2,1)S(1)}, u32[]{:S(2)}, u32[]{:S(2)}) %collective-permute-start.25) | collective-permute-done | bytes 262176 | tf_op jit(solution)/shard_map/ppermute | solution.py:365
  68.6 1.2 %o_share.3 = (bf16[128,1024]{1,0:T(8,128)(2,1)S(1)}, bf16[128,1024]{1,0:T(8,128)(2,1)S(1)}) custom-call(s32[3]{0:T(128)S(1)} %copy-done.5, bf16[256,512]{1,0:T(8,128)(2,1)S(1)} %collective-permute-done.25.near, bf16[256,512]{1,0:T(8,128)(2,1)S(1)} %collective-permute-done.26.far, bf16[1024,512]{1,0:T(8,128)(2,1)S(1)} %copy-done, ...), custom_call_target="tpu_custom_call" | custom-call | flops 536870912 | bytes 2097152 | tf_op jit(solution)/shard_map/o_share/pallas_call | solution.py:122
  70.9 1.1 %collective-permute-start.32 = (bf16[128,1024]{1,0:T(8,128)(2,1)S(1)}, bf16[128,1024]{1,0:T(8,128)(2,1)S(1)}, u32[]{:S(2)}, u32[]{:S(2)}) collective-permute-start(bf16[128,1024]{1,0:T(8,128)(2,1)S(1)} %get-tuple-element.88), channel_id=1, source_target_pairs={{0,8},{4,12},{8,0},{12,4},{16,24},{20,28},{24,16},{28,20},{1,9},{5... | collective-permute-start | bytes 786440 | tf_op jit(solution)/shard_map/ppermute | solution.py:365
  72.0 1.3 %o_share.2 = (bf16[128,1024]{1,0:T(8,128)(2,1)S(1)}, bf16[128,1024]{1,0:T(8,128)(2,1)S(1)}) custom-call(s32[3]{0:T(128)S(1)} %copy-done.5, bf16[256,512]{1,0:T(8,128)(2,1)S(1)} %attend.1.near, bf16[256,512]{1,0:T(8,128)(2,1)S(1)} %collective-permute-done.23.far, bf16[1024,512]{1,0:T(8,128)(2,1)S(1)} %copy-done, ...), custom_call_target="tpu_custom_call" | custom-call | flops 536870912 | bytes 2097152 | tf_op jit(solution)/shard_map/o_share/pallas_call | solution.py:122
  73.2 5.9 %collective-permute-done.27.landed = bf16[128,1024]{1,0:T(8,128)(2,1)S(1)} collective-permute-done((bf16[128,1024]{1,0:T(8,128)(2,1)S(1)}, bf16[128,1024]{1,0:T(8,128)(2,1)S(1)}, u32[]{:S(2)}, u32[]{:S(2)}) %collective-permute-start.27) | collective-permute-done | bytes 262176 | tf_op jit(solution)/shard_map/ppermute | solution.py:365
  79.7 1.6 %collective-permute-start.28 = (bf16[128,512]{1,0:T(8,128)(2,1)S(1)}, bf16[128,512]{1,0:T(8,128)(2,1)S(1)}, u32[]{:S(2)}, u32[]{:S(2)}) collective-permute-start(bf16[128,512]{1,0:T(8,128)(2,1)S(1)} %get-tuple-element.84), channel_id=1, source_target_pairs={{0,1},{1,0},{2,3},{3,2},{4,5},{5,4},{6,7},{7,6},{8,9},{9,8},{10,11... | collective-permute-start | bytes 393224 | tf_op jit(solution)/shard_map/ppermute | solution.py:374
  81.4 2.6 %collective-permute-start.29 = (bf16[128,512]{1,0:T(8,128)(2,1)S(1)}, bf16[128,512]{1,0:T(8,128)(2,1)S(1)}, u32[]{:S(2)}, u32[]{:S(2)}) collective-permute-start(bf16[128,512]{1,0:T(8,128)(2,1)S(1)} %get-tuple-element.85), channel_id=1, source_target_pairs={{0,2},{1,3},{2,0},{3,1},{4,6},{5,7},{6,4},{7,5},{8,10},{9,11},{10,... | collective-permute-start | bytes 393224 | tf_op jit(solution)/shard_map/ppermute | solution.py:374
  86.3 3.5 %collective-permute-start.34 = (bf16[128,512]{1,0:T(8,128)(2,1)S(1)}, bf16[128,512]{1,0:T(8,128)(2,1)S(1)}, u32[]{:S(2)}, u32[]{:S(2)}) collective-permute-start(bf16[128,512]{1,0:T(8,128)(2,1)S(1)} %get-tuple-element.91), channel_id=1, source_target_pairs={{0,2},{1,3},{2,0},{3,1},{4,6},{5,7},{6,4},{7,5},{8,10},{9,11},{10,... | collective-permute-start | bytes 393224 | tf_op jit(solution)/shard_map/ppermute | solution.py:374
  90.0 4.2 %collective-permute-done.29.refs_2_ = bf16[128,512]{1,0:T(8,128)(2,1)S(1)} collective-permute-done((bf16[128,512]{1,0:T(8,128)(2,1)S(1)}, bf16[128,512]{1,0:T(8,128)(2,1)S(1)}, u32[]{:S(2)}, u32[]{:S(2)}) %collective-permute-start.29) | collective-permute-done | bytes 131104 | tf_op jit(solution)/shard_map/ppermute | solution.py:374
  94.4 9.8 %collective-permute-done.34.refs_2_ = bf16[128,512]{1,0:T(8,128)(2,1)S(1)} collective-permute-done((bf16[128,512]{1,0:T(8,128)(2,1)S(1)}, bf16[128,512]{1,0:T(8,128)(2,1)S(1)}, u32[]{:S(2)}, u32[]{:S(2)}) %collective-permute-start.34) | collective-permute-done | bytes 131104 | tf_op jit(solution)/shard_map/ppermute | solution.py:374
  104.1 1.3 %mix_keep.1 = bf16[128,1024]{1,0:T(8,128)(2,1)} custom-call(s32[3]{0:T(128)S(1)} %copy-done.5, f32[1]{0:T(128)S(6)} %tanh.3.gate, bf16[128,512]{1,0:T(8,128)(2,1)S(1)} %copy-done.4, bf16[128,512]{1,0:T(8,128)(2,1)S(1)} %collective-permute-done.31.back, bf16[128,512]{1,0:T(8,128)(2,1)S(1)} %get-tuple-element.89.refs_0_, ...), custom_call_target="tpu_custom_call" | custom-call | flops 1048576 | bytes 1048576 | tf_op jit(solution)/shard_map/mix_keep/pallas_call | solution.py:122
  (93 shorter events, 17.3 us)
Async XLA Ops:
  0.0 16.0 %collective-permute-start.6 = (bf16[512,2048]{1,0:T(8,128)(2,1)}, bf16[512,2048]{1,0:T(8,128)(2,1)}, u32[]{:S(2)}, u32[]{:S(2)}) collective-permute-start(bf16[512,2048]{1,0:T(8,128)(2,1)} %kv_own.1), channel_id=1, source_target_pairs={{0,4},{4,0},{8,12},{12,8},{16,20},{20,16},{24,28},{28,24},{1,5},{5... | collective-permute-start | bytes 6291464 | tf_op jit(solution)/shard_map/ppermute | solution.py:362
  5.2 6.8 %collective-permute-start.2 = (bf16[16,1024]{1,0:T(8,128)(2,1)}, bf16[16,1024]{1,0:T(8,128)(2,1)S(1)}, u32[]{:S(2)}, u32[]{:S(2)}) collective-permute-start(bf16[16,1024]{1,0:T(8,128)(2,1)} %get-tuple-element.53), channel_id=1, source_target_pairs={{0,8},{4,12},{8,0},{12,4},{16,24},{20,28},{24,16},{28,20},{1,9},{5... | collective-permute-start | bytes 98312 | tf_op jit(solution)/shard_map/ppermute | solution.py:365
  7.7 5.8 %collective-permute-start.3 = (bf16[16,1024]{1,0:T(8,128)(2,1)}, bf16[16,1024]{1,0:T(8,128)(2,1)S(1)}, u32[]{:S(2)}, u32[]{:S(2)}) collective-permute-start(bf16[16,1024]{1,0:T(8,128)(2,1)} %get-tuple-element.54), channel_id=1, source_target_pairs={{0,16},{4,20},{8,24},{12,28},{16,0},{20,4},{24,8},{28,12},{1,17},{... | collective-permute-start | bytes 98312 | tf_op jit(solution)/shard_map/ppermute | solution.py:365
  9.3 5.4 %collective-permute-start.4 = (bf16[16,1024]{1,0:T(8,128)(2,1)}, bf16[16,1024]{1,0:T(8,128)(2,1)S(1)}, u32[]{:S(2)}, u32[]{:S(2)}) collective-permute-start(bf16[16,1024]{1,0:T(8,128)(2,1)} %get-tuple-element.55), channel_id=1, source_target_pairs={{0,24},{4,28},{8,16},{12,20},{16,8},{20,12},{24,0},{28,4},{1,25},{... | collective-permute-start | bytes 98312 | tf_op jit(solution)/shard_map/ppermute | solution.py:365
  9.3 15.6 %collective-permute-start.10 = (bf16[512,512]{1,0:T(8,128)(2,1)}, bf16[512,512]{1,0:T(8,128)(2,1)S(1)}, u32[]{:S(2)}, u32[]{:S(2)}) collective-permute-start(bf16[512,512]{1,0:T(8,128)(2,1)} %get-tuple-element.60.q_keep), channel_id=1, source_target_pairs={{0,8},{4,12},{8,0},{12,4},{16,24},{20,28},{24,16},{28,20},{1,9},{5... | collective-permute-start | bytes 1572872 | tf_op jit(solution)/shard_map/ppermute | solution.py:365
  12.0 15.5 %collective-permute-start.11 = (bf16[128,2048]{1,0:T(8,128)(2,1)}, bf16[128,2048]{1,0:T(8,128)(2,1)S(1)}, u32[]{:S(2)}, u32[]{:S(2)}) collective-permute-start(bf16[128,2048]{1,0:T(8,128)(2,1)} %get-tuple-element.61), channel_id=1, source_target_pairs={{0,16},{4,20},{8,24},{12,28},{16,0},{20,4},{24,8},{28,12},{1,17},{... | collective-permute-start | bytes 1572872 | tf_op jit(solution)/shard_map/ppermute | solution.py:365
  14.6 16.7 %collective-permute-start.12 = (bf16[512,512]{1,0:T(8,128)(2,1)}, bf16[512,512]{1,0:T(8,128)(2,1)S(1)}, u32[]{:S(2)}, u32[]{:S(2)}) collective-permute-start(bf16[512,512]{1,0:T(8,128)(2,1)} %get-tuple-element.63), channel_id=1, source_target_pairs={{0,4},{4,0},{8,12},{12,8},{16,20},{20,16},{24,28},{28,24},{1,5},{5... | collective-permute-start | bytes 1572872 | tf_op jit(solution)/shard_map/ppermute | solution.py:362
  18.6 8.8 %collective-permute-start.7 = (f32[32,1024]{1,0:T(8,128)S(1)}, f32[32,1024]{1,0:T(8,128)S(1)}, u32[]{:S(2)}, u32[]{:S(2)}) collective-permute-start(f32[32,1024]{1,0:T(8,128)S(1)} %get-tuple-element.57), channel_id=1, source_target_pairs={{0,8},{4,12},{8,0},{12,4},{16,24},{20,28},{24,16},{28,20},{1,9},{5... | collective-permute-start | bytes 393224 | tf_op jit(solution)/shard_map/ppermute | solution.py:365
  19.0 12.2 %collective-permute-start.8 = (f32[32,1024]{1,0:T(8,128)S(1)}, f32[32,1024]{1,0:T(8,128)S(1)}, u32[]{:S(2)}, u32[]{:S(2)}) collective-permute-start(f32[32,1024]{1,0:T(8,128)S(1)} %get-tuple-element.58), channel_id=1, source_target_pairs={{0,16},{4,20},{8,24},{12,28},{16,0},{20,4},{24,8},{28,12},{1,17},{... | collective-permute-start | bytes 393224 | tf_op jit(solution)/shard_map/ppermute | solution.py:365
  24.9 6.4 %collective-permute-start.9 = (f32[32,1024]{1,0:T(8,128)S(1)}, f32[32,1024]{1,0:T(8,128)S(1)}, u32[]{:S(2)}, u32[]{:S(2)}) collective-permute-start(f32[32,1024]{1,0:T(8,128)S(1)} %get-tuple-element.59), channel_id=1, source_target_pairs={{0,24},{4,28},{8,16},{12,20},{16,8},{20,12},{24,0},{28,4},{1,25},{... | collective-permute-start | bytes 393224 | tf_op jit(solution)/shard_map/ppermute | solution.py:365
  27.5 22.2 %collective-permute-start.1 = (bf16[128,2048]{1,0:T(8,128)(2,1)S(1)}, bf16[128,2048]{1,0:T(8,128)(2,1)S(1)}, u32[]{:S(2)}, u32[]{:S(2)}) collective-permute-start(bf16[128,2048]{1,0:T(8,128)(2,1)S(1)} %copy-done.2), channel_id=1, source_target_pairs={{0,4},{4,0},{8,12},{12,8},{16,20},{20,16},{24,28},{28,24},{1,5},{5... | collective-permute-start | bytes 1572872 | tf_op jit(solution)/shard_map/ppermute | solution.py:362
  31.3 5.0 %collective-permute-start.15 = (bf16[128,2048]{1,0:T(8,128)(2,1)S(1)}, bf16[128,2048]{1,0:T(8,128)(2,1)S(1)}, u32[]{:S(2)}, u32[]{:S(2)}) collective-permute-start(bf16[128,2048]{1,0:T(8,128)(2,1)S(1)} %collective-permute-done.11.own), channel_id=1, source_target_pairs={{0,4},{4,0},{8,12},{12,8},{16,20},{20,16},{24,28},{28,24},{1,5},{5... | collective-permute-start | bytes 1572872 | tf_op jit(solution)/shard_map/ppermute | solution.py:362
  31.4 14.8 %collective-permute-start.13 = (bf16[512,512]{1,0:T(8,128)(2,1)S(1)}, bf16[512,512]{1,0:T(8,128)(2,1)S(1)}, u32[]{:S(2)}, u32[]{:S(2)}) collective-permute-start(bf16[512,512]{1,0:T(8,128)(2,1)S(1)} %collective-permute-done.12.q_other), channel_id=1, source_target_pairs={{0,8},{4,12},{8,0},{12,4},{16,24},{20,28},{24,16},{28,20},{1,9},{5... | collective-permute-start | bytes 1572872 | tf_op jit(solution)/shard_map/ppermute | solution.py:365
  34.7 15.9 %collective-permute-start.18 = (bf16[512,512]{1,0:T(8,128)(2,1)S(1)}, bf16[512,512]{1,0:T(8,128)(2,1)S(1)}, u32[]{:S(2)}, u32[]{:S(2)}) collective-permute-start(bf16[512,512]{1,0:T(8,128)(2,1)S(1)} %get-tuple-element.75), channel_id=1, source_target_pairs={{0,16},{4,20},{8,24},{12,28},{16,0},{20,4},{24,8},{28,12},{1,17},{... | collective-permute-start | bytes 1572872 | tf_op jit(solution)/shard_map/ppermute | solution.py:365
  37.3 4.9 %collective-permute-start.16 = (bf16[64,256]{1,0:T(8,128)(2,1)S(1)}, bf16[64,256]{1,0:T(8,128)(2,1)S(1)}, u32[]{:S(2)}, u32[]{:S(2)}) collective-permute-start(bf16[64,256]{1,0:T(8,128)(2,1)S(1)} %kv_turn.1), channel_id=1, source_target_pairs={{0,2},{1,3},{2,0},{3,1},{4,6},{5,7},{6,4},{7,5},{8,10},{9,11},{10,... | collective-permute-start | bytes 98312 | tf_op jit(solution)/shard_map/ppermute | solution.py:374
  42.1 5.8 %collective-permute-start.17 = (bf16[128,256]{1,0:T(8,128)(2,1)S(1)}, bf16[128,256]{1,0:T(8,128)(2,1)S(1)}, u32[]{:S(2)}, u32[]{:S(2)}) collective-permute-start(bf16[128,256]{1,0:T(8,128)(2,1)S(1)} %kv_join.1.refs_0_), channel_id=1, source_target_pairs={{0,8},{4,12},{8,0},{12,4},{16,24},{20,28},{24,16},{28,20},{1,9},{5... | collective-permute-start | bytes 196616 | tf_op jit(solution)/shard_map/ppermute | solution.py:365
  43.2 9.9 %collective-permute-start.20 = (bf16[128,256]{1,0:T(8,128)(2,1)S(1)}, bf16[128,256]{1,0:T(8,128)(2,1)S(1)}, u32[]{:S(2)}, u32[]{:S(2)}) collective-permute-start(bf16[128,256]{1,0:T(8,128)(2,1)S(1)} %kv_join.1.refs_0_), channel_id=1, source_target_pairs={{0,16},{4,20},{8,24},{12,28},{16,0},{20,4},{24,8},{28,12},{1,17},{... | collective-permute-start | bytes 196616 | tf_op jit(solution)/shard_map/ppermute | solution.py:365
  46.2 7.0 %collective-permute-start.21 = (bf16[128,256]{1,0:T(8,128)(2,1)S(1)}, bf16[128,256]{1,0:T(8,128)(2,1)S(1)}, u32[]{:S(2)}, u32[]{:S(2)}) collective-permute-start(bf16[128,256]{1,0:T(8,128)(2,1)S(1)} %kv_join.1.refs_0_), channel_id=1, source_target_pairs={{0,24},{4,28},{8,16},{12,20},{16,8},{20,12},{24,0},{28,4},{1,25},{... | collective-permute-start | bytes 196616 | tf_op jit(solution)/shard_map/ppermute | solution.py:365
  49.0 9.3 %collective-permute-start.19 = (bf16[256,512]{1,0:T(8,128)(2,1)S(1)}, bf16[256,512]{1,0:T(8,128)(2,1)S(1)}, u32[]{:S(2)}, u32[]{:S(2)}) collective-permute-start(bf16[256,512]{1,0:T(8,128)(2,1)S(1)} %q_late.3), channel_id=1, source_target_pairs={{0,16},{4,20},{8,24},{12,28},{16,0},{20,4},{24,8},{28,12},{1,17},{... | collective-permute-start | bytes 786440 | tf_op jit(solution)/shard_map/ppermute | solution.py:365
  50.6 17.6 %collective-permute-start.24 = (bf16[512,512]{1,0:T(8,128)(2,1)S(1)}, bf16[512,512]{1,0:T(8,128)(2,1)S(1)}, u32[]{:S(2)}, u32[]{:S(2)}) collective-permute-start(bf16[512,512]{1,0:T(8,128)(2,1)S(1)} %get-tuple-element.80), channel_id=1, source_target_pairs={{0,16},{4,20},{8,24},{12,28},{16,0},{20,4},{24,8},{28,12},{1,17},{... | collective-permute-start | bytes 1572872 | tf_op jit(solution)/shard_map/ppermute | solution.py:365
  60.6 6.4 %collective-permute-start.25 = (bf16[256,512]{1,0:T(8,128)(2,1)S(1)}, bf16[256,512]{1,0:T(8,128)(2,1)S(1)}, u32[]{:S(2)}, u32[]{:S(2)}) collective-permute-start(bf16[256,512]{1,0:T(8,128)(2,1)S(1)} %attend.1.near), channel_id=1, source_target_pairs={{0,8},{4,12},{8,0},{12,4},{16,24},{20,28},{24,16},{28,20},{1,9},{5... | collective-permute-start | bytes 786440 | tf_op jit(solution)/shard_map/ppermute | solution.py:365
  67.1 4.9 %collective-permute-start.23 = (bf16[256,512]{1,0:T(8,128)(2,1)S(1)}, bf16[256,512]{1,0:T(8,128)(2,1)S(1)}, u32[]{:S(2)}, u32[]{:S(2)}) collective-permute-start(bf16[256,512]{1,0:T(8,128)(2,1)S(1)} %attend.1.near), channel_id=1, source_target_pairs={{0,4},{4,0},{8,12},{12,8},{16,20},{20,16},{24,28},{28,24},{1,5},{5... | collective-permute-start | bytes 786440 | tf_op jit(solution)/shard_map/ppermute | solution.py:362
  69.8 9.2 %collective-permute-start.27 = (bf16[128,1024]{1,0:T(8,128)(2,1)S(1)}, bf16[128,1024]{1,0:T(8,128)(2,1)S(1)}, u32[]{:S(2)}, u32[]{:S(2)}) collective-permute-start(bf16[128,1024]{1,0:T(8,128)(2,1)S(1)} %get-tuple-element.82), channel_id=1, source_target_pairs={{0,8},{4,12},{8,0},{12,4},{16,24},{20,28},{24,16},{28,20},{1,9},{5... | collective-permute-start | bytes 786440 | tf_op jit(solution)/shard_map/ppermute | solution.py:365
  70.9 14.0 %collective-permute-start.32 = (bf16[128,1024]{1,0:T(8,128)(2,1)S(1)}, bf16[128,1024]{1,0:T(8,128)(2,1)S(1)}, u32[]{:S(2)}, u32[]{:S(2)}) collective-permute-start(bf16[128,1024]{1,0:T(8,128)(2,1)S(1)} %get-tuple-element.88), channel_id=1, source_target_pairs={{0,8},{4,12},{8,0},{12,4},{16,24},{20,28},{24,16},{28,20},{1,9},{5... | collective-permute-start | bytes 786440 | tf_op jit(solution)/shard_map/ppermute | solution.py:365
  71.9 14.3 %collective-permute-start = (bf16[128,512]{1,0:T(8,128)(2,1)S(1)}, bf16[128,512]{1,0:T(8,128)(2,1)S(1)}, u32[]{:S(2)}, u32[]{:S(2)}) collective-permute-start(bf16[128,512]{1,0:T(8,128)(2,1)S(1)} %copy-done.11), channel_id=1, source_target_pairs={{0,4},{4,0},{8,12},{12,8},{16,20},{20,16},{24,28},{28,24},{1,5},{5... | collective-permute-start | bytes 393224 | tf_op jit(solution)/shard_map/ppermute | solution.py:362
  79.7 10.0 %collective-permute-start.28 = (bf16[128,512]{1,0:T(8,128)(2,1)S(1)}, bf16[128,512]{1,0:T(8,128)(2,1)S(1)}, u32[]{:S(2)}, u32[]{:S(2)}) collective-permute-start(bf16[128,512]{1,0:T(8,128)(2,1)S(1)} %get-tuple-element.84), channel_id=1, source_target_pairs={{0,1},{1,0},{2,3},{3,2},{4,5},{5,4},{6,7},{7,6},{8,9},{9,8},{10,11... | collective-permute-start | bytes 393224 | tf_op jit(solution)/shard_map/ppermute | solution.py:374
  81.4 12.8 %collective-permute-start.29 = (bf16[128,512]{1,0:T(8,128)(2,1)S(1)}, bf16[128,512]{1,0:T(8,128)(2,1)S(1)}, u32[]{:S(2)}, u32[]{:S(2)}) collective-permute-start(bf16[128,512]{1,0:T(8,128)(2,1)S(1)} %get-tuple-element.85), channel_id=1, source_target_pairs={{0,2},{1,3},{2,0},{3,1},{4,6},{5,7},{6,4},{7,5},{8,10},{9,11},{10,... | collective-permute-start | bytes 393224 | tf_op jit(solution)/shard_map/ppermute | solution.py:374
  83.9 10.2 %collective-permute-start.30 = (bf16[128,512]{1,0:T(8,128)(2,1)S(1)}, bf16[128,512]{1,0:T(8,128)(2,1)S(1)}, u32[]{:S(2)}, u32[]{:S(2)}) collective-permute-start(bf16[128,512]{1,0:T(8,128)(2,1)S(1)} %get-tuple-element.86), channel_id=1, source_target_pairs={{0,3},{1,2},{2,1},{3,0},{4,7},{5,6},{6,5},{7,4},{8,11},{9,10},{10,... | collective-permute-start | bytes 393224 | tf_op jit(solution)/shard_map/ppermute | solution.py:374
  85.5 8.8 %collective-permute-start.33 = (bf16[128,512]{1,0:T(8,128)(2,1)S(1)}, bf16[128,512]{1,0:T(8,128)(2,1)S(1)}, u32[]{:S(2)}, u32[]{:S(2)}) collective-permute-start(bf16[128,512]{1,0:T(8,128)(2,1)S(1)} %get-tuple-element.90), channel_id=1, source_target_pairs={{0,1},{1,0},{2,3},{3,2},{4,5},{5,4},{6,7},{7,6},{8,9},{9,8},{10,11... | collective-permute-start | bytes 393224 | tf_op jit(solution)/shard_map/ppermute | solution.py:374
  86.3 17.9 %collective-permute-start.34 = (bf16[128,512]{1,0:T(8,128)(2,1)S(1)}, bf16[128,512]{1,0:T(8,128)(2,1)S(1)}, u32[]{:S(2)}, u32[]{:S(2)}) collective-permute-start(bf16[128,512]{1,0:T(8,128)(2,1)S(1)} %get-tuple-element.91), channel_id=1, source_target_pairs={{0,2},{1,3},{2,0},{3,1},{4,6},{5,7},{6,4},{7,5},{8,10},{9,11},{10,... | collective-permute-start | bytes 393224 | tf_op jit(solution)/shard_map/ppermute | solution.py:374
  89.8 14.4 %collective-permute-start.35 = (bf16[128,512]{1,0:T(8,128)(2,1)S(1)}, bf16[128,512]{1,0:T(8,128)(2,1)S(1)}, u32[]{:S(2)}, u32[]{:S(2)}) collective-permute-start(bf16[128,512]{1,0:T(8,128)(2,1)S(1)} %get-tuple-element.92), channel_id=1, source_target_pairs={{0,3},{1,2},{2,1},{3,0},{4,7},{5,6},{6,5},{7,4},{8,11},{9,10},{10,... | collective-permute-start | bytes 393224 | tf_op jit(solution)/shard_map/ppermute | solution.py:374
  94.3 9.9 %collective-permute-start.31 = (bf16[128,512]{1,0:T(8,128)(2,1)S(1)}, bf16[128,512]{1,0:T(8,128)(2,1)S(1)}, u32[]{:S(2)}, u32[]{:S(2)}) collective-permute-start(bf16[128,512]{1,0:T(8,128)(2,1)S(1)} %mix_give.1), channel_id=1, source_target_pairs={{0,4},{4,0},{8,12},{12,8},{16,20},{20,16},{24,28},{28,24},{1,5},{5... | collective-permute-start | bytes 393224 | tf_op jit(solution)/shard_map/ppermute | solution.py:362
  (16 other events, 183.5 us)
where the time goes:
time: 106 us; the launch traced here: 105 us
  waiting for transfers between devices  46.2 us (44%)
  starting transfers between devices  37.6 us (35%)
  Pallas kernels  18.7 us (18%)
  other arithmetic  1.07 us (1%)
    ppermute x18, waiting for transfers between devices, peer(): return lax.ppermute(x, 'ctx', [(k, k ^ 2 * s) for k in range(ctx_count)])  28.8 us
    ppermute x18, starting transfers between devices, peer(): return lax.ppermute(x, 'ctx', [(k, k ^ 2 * s) for k in range(ctx_count)])  22.3 us
    pallas_call x16, Pallas kernels, call(): pl.pallas_call(kernel, out_shape=outs, in_specs=specs, out_specs=[VMEM] *...  18.7 us
    ppermute x8, waiting for transfers between devices, across(): return lax.ppermute(x, 'img', [(k, k ^ t) for k in range(CHIPS)])  16.1 us
    ppermute x8, starting transfers between devices, across(): return lax.ppermute(x, 'img', [(k, k ^ t) for k in range(CHIPS)])  13.2 us
  transfers between devices with their start and end apart: 36, of which 14 were waited for; matrix products, arithmetic and copies ran while one was open for 2% of the time, Pallas kernels for 16%

commit v1 on v0

--- a/solution.py
+++ b/solution.py
@@ -417,6 +417,7 @@
         name="kv_shares",
     )
     shares = [shares[0]] + [peer(shares[s], s) for s in steps]
+    own_share = shares[0]
     shares, q_side, far = lax.optimization_barrier((shares, q_side, far))
     here, there, give = call(
         kv_norm_kernel,
@@ -454,12 +455,12 @@
         name="kv_join",
     )[0]
     kv_all = [kv_first] + [peer(kv_first, s) for s in steps]
-    q_behind, _ = lax.optimization_barrier((q_other, shares[0]))
+    q_behind, _ = lax.optimization_barrier((q_other, own_share))
     q_corner = along_x(q_behind)
     q_corner, kv_all[1] = lax.optimization_barrier((q_corner, kv_all[1]))
 
     o_early, _ = lax.optimization_barrier((o_weight[:half], here))
-    early[1], o_early = lax.optimization_barrier((early[1], along_y(o_early)))
+    q_corner, o_early = lax.optimization_barrier((q_corner, along_y(o_early)))
     q_far, q_first = [
         call(
             late_kernel,

time: 106 us -> 106 us (level)
    ppermute x8, waiting for transfers between devices: 16.1 us -> 17.4 us  [across(): return lax.ppermute(x, 'img', [(k, k ^ t) for k in range(CHIPS)])]
  transfers between devices with their start and end apart: 36 -> 36, of which waited for: 14 -> 15; matrix products, arithmetic and copies ran while one was open for 2% -> 2% of each run, Pallas kernels for 16% -> 16%
where the time goes in v1:
time: 106 us
  waiting for transfers between devices  46.7 us (44%)
  starting transfers between devices  37 us (35%)
  Pallas kernels  18.7 us (18%)
  other arithmetic  1.07 us (1%)
    ppermute x18, waiting for transfers between devices, peer(): return lax.ppermute(x, 'ctx', [(k, k ^ 2 * s) for k in range(ctx_count)])  28 us
    ppermute x18, starting transfers between devices, peer(): return lax.ppermute(x, 'ctx', [(k, k ^ 2 * s) for k in range(ctx_count)])  21.9 us
    pallas_call x16, Pallas kernels, call(): pl.pallas_call(kernel, out_shape=outs, in_specs=specs, out_specs=[VMEM] *...  18.7 us
    ppermute x8, waiting for transfers between devices, across(): return lax.ppermute(x, 'img', [(k, k ^ t) for k in range(CHIPS)])  17.4 us
    ppermute x8, starting transfers between devices, across(): return lax.ppermute(x, 'img', [(k, k ^ t) for k in range(CHIPS)])  13.1 us
  transfers between devices with their start and end apart: 36, of which 15 were waited for; matrix products, arithmetic and copies ran while one was open for 2% of the time, Pallas kernels for 16%

profile of v1, /device:TPU:0, one launch (start us, length us, event | category | flops | bytes accessed | tf_op | source)
XLA Modules:
  0.0 105.5 jit_solution(9677193788358200386)
XLA Ops:
  1.1 4.1 %start.1 = (bf16[16,1024]{1,0:T(8,128)(2,1)}, bf16[16,1024]{1,0:T(8,128)(2,1)}, bf16[16,1024]{1,0:T(8,128)(2,1)}, bf16[16,1024]{1,0:T(8,128)(2,1)}, bf16[128,204...) custom-call(s32[3]{0:T(128)} %pad_add_fusion.1.where, ...), custom_call_target="tpu_custom_call" | custom-call | flops 4194304 | bytes 4194304 | tf_op jit(solution)/shard_map/start/pallas_call | solution.py:122
  5.2 2.6 %collective-permute-start.2 = (bf16[16,1024]{1,0:T(8,128)(2,1)}, bf16[16,1024]{1,0:T(8,128)(2,1)S(1)}, u32[]{:S(2)}, u32[]{:S(2)}) collective-permute-start(bf16[16,1024]{1,0:T(8,128)(2,1)} %get-tuple-element.53), channel_id=1, source_target_pairs={{0,8},{4,12},{8,0},{12,4},{16,24},{20,28},{24,16},{28,20},{1,9},{5... | collective-permute-start | bytes 98312 | tf_op jit(solution)/shard_map/ppermute | solution.py:365
  7.7 1.5 %collective-permute-start.3 = (bf16[16,1024]{1,0:T(8,128)(2,1)}, bf16[16,1024]{1,0:T(8,128)(2,1)S(1)}, u32[]{:S(2)}, u32[]{:S(2)}) collective-permute-start(bf16[16,1024]{1,0:T(8,128)(2,1)} %get-tuple-element.54), channel_id=1, source_target_pairs={{0,16},{4,20},{8,24},{12,28},{16,0},{20,4},{24,8},{28,12},{1,17},{... | collective-permute-start | bytes 98312 | tf_op jit(solution)/shard_map/ppermute | solution.py:365
  9.3 1.9 %collective-permute-start.10 = (bf16[512,512]{1,0:T(8,128)(2,1)}, bf16[512,512]{1,0:T(8,128)(2,1)S(1)}, u32[]{:S(2)}, u32[]{:S(2)}) collective-permute-start(bf16[512,512]{1,0:T(8,128)(2,1)} %get-tuple-element.60.q_keep), channel_id=1, source_target_pairs={{0,8},{4,12},{8,0},{12,4},{16,24},{20,28},{24,16},{28,20},{1,9},{5... | collective-permute-start | bytes 1572872 | tf_op jit(solution)/shard_map/ppermute | solution.py:365
  12.0 1.5 %collective-permute-start.11 = (bf16[128,2048]{1,0:T(8,128)(2,1)}, bf16[128,2048]{1,0:T(8,128)(2,1)S(1)}, u32[]{:S(2)}, u32[]{:S(2)}) collective-permute-start(bf16[128,2048]{1,0:T(8,128)(2,1)} %get-tuple-element.61), channel_id=1, source_target_pairs={{0,16},{4,20},{8,24},{12,28},{16,0},{20,4},{24,8},{28,12},{1,17},{... | collective-permute-start | bytes 1572872 | tf_op jit(solution)/shard_map/ppermute | solution.py:365
  13.5 1.1 %collective-permute-done.4 = bf16[16,1024]{1,0:T(8,128)(2,1)S(1)} collective-permute-done((bf16[16,1024]{1,0:T(8,128)(2,1)}, bf16[16,1024]{1,0:T(8,128)(2,1)S(1)}, u32[]{:S(2)}, u32[]{:S(2)}) %collective-permute-start.4) | collective-permute-done | bytes 32800 | tf_op jit(solution)/shard_map/ppermute | solution.py:365
  16.0 2.6 %kv_shares.1 = (f32[32,1024]{1,0:T(8,128)S(1)}, f32[32,1024]{1,0:T(8,128)S(1)}, f32[32,1024]{1,0:T(8,128)S(1)}, f32[32,1024]{1,0:T(8,128)S(1)}) custom-call(s32[3]{0:T(128)S(1)} %copy-done.5, bf16[64,1024]{1,0:T(8,128)(2,1)S(1)} %constant_dynamic-update-slice_fusion.vis, bf16[64,1024]{1,0:T(8,128)(2,1)S(1)} %collective-permute-done.5.vis_other, ...), custom_call_target="tpu_custom_call" | custom-call | flops 536870912 | bytes 4194304 | tf_op jit(solution)/shard_map/kv_shares/pallas_call | solution.py:122
  19.3 5.6 %collective-permute-done.10.q_side = bf16[512,512]{1,0:T(8,128)(2,1)S(1)} collective-permute-done((bf16[512,512]{1,0:T(8,128)(2,1)}, bf16[512,512]{1,0:T(8,128)(2,1)S(1)}, u32[]{:S(2)}, u32[]{:S(2)}) %collective-permute-start.10) | collective-permute-done | bytes 524320 | tf_op jit(solution)/shard_map/ppermute | solution.py:365
  24.9 2.3 %collective-permute-start.9 = (f32[32,1024]{1,0:T(8,128)S(1)}, f32[32,1024]{1,0:T(8,128)S(1)}, u32[]{:S(2)}, u32[]{:S(2)}) collective-permute-start(f32[32,1024]{1,0:T(8,128)S(1)} %get-tuple-element.59), channel_id=1, source_target_pairs={{0,24},{4,28},{8,16},{12,20},{16,8},{20,12},{24,0},{28,4},{1,25},{... | collective-permute-start | bytes 393224 | tf_op jit(solution)/shard_map/ppermute | solution.py:365
  28.0 3.3 %collective-permute-done.8.refs_2_ = f32[32,1024]{1,0:T(8,128)S(1)} collective-permute-done((f32[32,1024]{1,0:T(8,128)S(1)}, f32[32,1024]{1,0:T(8,128)S(1)}, u32[]{:S(2)}, u32[]{:S(2)}) %collective-permute-start.8) | collective-permute-done | bytes 131104 | tf_op jit(solution)/shard_map/ppermute | solution.py:365
  33.0 1.6 %collective-permute-start.18 = (bf16[512,512]{1,0:T(8,128)(2,1)S(1)}, bf16[512,512]{1,0:T(8,128)(2,1)S(1)}, u32[]{:S(2)}, u32[]{:S(2)}) collective-permute-start(bf16[512,512]{1,0:T(8,128)(2,1)S(1)} %get-tuple-element.75), channel_id=1, source_target_pairs={{0,16},{4,20},{8,24},{12,28},{16,0},{20,4},{24,8},{28,12},{1,17},{... | collective-permute-start | bytes 1572872 | tf_op jit(solution)/shard_map/ppermute | solution.py:365
  34.6 1.6 %collective-permute-start.14 = (bf16[64,256]{1,0:T(8,128)(2,1)S(1)}, bf16[64,256]{1,0:T(8,128)(2,1)S(1)}, u32[]{:S(2)}, u32[]{:S(2)}) collective-permute-start(bf16[64,256]{1,0:T(8,128)(2,1)S(1)} %get-tuple-element.70), channel_id=1, source_target_pairs={{0,1},{1,0},{2,3},{3,2},{4,5},{5,4},{6,7},{7,6},{8,9},{9,8},{10,11... | collective-permute-start | bytes 98312 | tf_op jit(solution)/shard_map/ppermute | solution.py:374
  37.2 1.3 %collective-permute-done.14.landed = bf16[64,256]{1,0:T(8,128)(2,1)S(1)} collective-permute-done((bf16[64,256]{1,0:T(8,128)(2,1)S(1)}, bf16[64,256]{1,0:T(8,128)(2,1)S(1)}, u32[]{:S(2)}, u32[]{:S(2)}) %collective-permute-start.14) | collective-permute-done | bytes 32800 | tf_op jit(solution)/shard_map/ppermute | solution.py:374
  38.6 2.6 %collective-permute-start.16 = (bf16[64,256]{1,0:T(8,128)(2,1)S(1)}, bf16[64,256]{1,0:T(8,128)(2,1)S(1)}, u32[]{:S(2)}, u32[]{:S(2)}) collective-permute-start(bf16[64,256]{1,0:T(8,128)(2,1)S(1)} %kv_turn.1), channel_id=1, source_target_pairs={{0,2},{1,3},{2,0},{3,1},{4,6},{5,7},{6,4},{7,5},{8,10},{9,11},{10,... | collective-permute-start | bytes 98312 | tf_op jit(solution)/shard_map/ppermute | solution.py:374
  41.3 2.1 %collective-permute-done.16.last = bf16[64,256]{1,0:T(8,128)(2,1)S(1)} collective-permute-done((bf16[64,256]{1,0:T(8,128)(2,1)S(1)}, bf16[64,256]{1,0:T(8,128)(2,1)S(1)}, u32[]{:S(2)}, u32[]{:S(2)}) %collective-permute-start.16) | collective-permute-done | bytes 32800 | tf_op jit(solution)/shard_map/ppermute | solution.py:374
  46.2 1.8 %collective-permute-start.21 = (bf16[128,256]{1,0:T(8,128)(2,1)S(1)}, bf16[128,256]{1,0:T(8,128)(2,1)S(1)}, u32[]{:S(2)}, u32[]{:S(2)}) collective-permute-start(bf16[128,256]{1,0:T(8,128)(2,1)S(1)} %kv_join.1.refs_0_), channel_id=1, source_target_pairs={{0,24},{4,28},{8,16},{12,20},{16,8},{20,12},{24,0},{28,4},{1,25},{... | collective-permute-start | bytes 196616 | tf_op jit(solution)/shard_map/ppermute | solution.py:365
  49.0 1.4 %collective-permute-start.19 = (bf16[256,512]{1,0:T(8,128)(2,1)S(1)}, bf16[256,512]{1,0:T(8,128)(2,1)S(1)}, u32[]{:S(2)}, u32[]{:S(2)}) collective-permute-start(bf16[256,512]{1,0:T(8,128)(2,1)S(1)} %q_late.3), channel_id=1, source_target_pairs={{0,16},{4,20},{8,24},{12,28},{16,0},{20,4},{24,8},{28,12},{1,17},{... | collective-permute-start | bytes 786440 | tf_op jit(solution)/shard_map/ppermute | solution.py:365
  53.2 5.1 %collective-permute-done.19.landed = bf16[256,512]{1,0:T(8,128)(2,1)S(1)} collective-permute-done((bf16[256,512]{1,0:T(8,128)(2,1)S(1)}, bf16[256,512]{1,0:T(8,128)(2,1)S(1)}, u32[]{:S(2)}, u32[]{:S(2)}) %collective-permute-start.19) | collective-permute-done | bytes 262176 | tf_op jit(solution)/shard_map/ppermute | solution.py:365
  58.3 2.3 %attend.1.near = bf16[256,512]{1,0:T(8,128)(2,1)S(1)} custom-call(f32[1,128]{1,0:T(1,128)S(1)} %bitcast.8, f32[256,512]{1,0:T(8,128)S(1)} %q_late.2.first, bf16[256,512]{1,0:T(8,128)(2,1)S(1)} %collective-permute-done.19.landed, bf16[128,256]{1,0:T(8,128)(2,1)S(1)} %kv_join.1.refs_0_, bf16[128,256]{1,0:T(8,128)(2,1)S(1)} %collective-permute-done.17.refs_1_, ...), custom_call_target="tpu_custom_call" | custom-call | flops 268435456 | bytes 2097152 | tf_op jit(solution)/shard_map/attend/pallas_call | solution.py:122
  60.6 1.0 collective-permute-start.25
  61.7 5.4 %collective-permute-done.25.near = bf16[256,512]{1,0:T(8,128)(2,1)S(1)} collective-permute-done((bf16[256,512]{1,0:T(8,128)(2,1)S(1)}, bf16[256,512]{1,0:T(8,128)(2,1)S(1)}, u32[]{:S(2)}, u32[]{:S(2)}) %collective-permute-start.25) | collective-permute-done | bytes 262176 | tf_op jit(solution)/shard_map/ppermute | solution.py:365
  68.6 1.2 %o_share.3 = (bf16[128,1024]{1,0:T(8,128)(2,1)S(1)}, bf16[128,1024]{1,0:T(8,128)(2,1)S(1)}) custom-call(s32[3]{0:T(128)S(1)} %copy-done.5, bf16[256,512]{1,0:T(8,128)(2,1)S(1)} %collective-permute-done.25.near, bf16[256,512]{1,0:T(8,128)(2,1)S(1)} %collective-permute-done.26.far, bf16[1024,512]{1,0:T(8,128)(2,1)S(1)} %copy-done, ...), custom_call_target="tpu_custom_call" | custom-call | flops 536870912 | bytes 2097152 | tf_op jit(solution)/shard_map/o_share/pallas_call | solution.py:122
  69.9 1.0 collective-permute-start.27
  70.9 1.1 %collective-permute-start.32 = (bf16[128,1024]{1,0:T(8,128)(2,1)S(1)}, bf16[128,1024]{1,0:T(8,128)(2,1)S(1)}, u32[]{:S(2)}, u32[]{:S(2)}) collective-permute-start(bf16[128,1024]{1,0:T(8,128)(2,1)S(1)} %get-tuple-element.88), channel_id=1, source_target_pairs={{0,8},{4,12},{8,0},{12,4},{16,24},{20,28},{24,16},{28,20},{1,9},{5... | collective-permute-start | bytes 786440 | tf_op jit(solution)/shard_map/ppermute | solution.py:365
  72.0 1.3 %o_share.2 = (bf16[128,1024]{1,0:T(8,128)(2,1)S(1)}, bf16[128,1024]{1,0:T(8,128)(2,1)S(1)}) custom-call(s32[3]{0:T(128)S(1)} %copy-done.5, bf16[256,512]{1,0:T(8,128)(2,1)S(1)} %attend.1.near, bf16[256,512]{1,0:T(8,128)(2,1)S(1)} %collective-permute-done.23.far, bf16[1024,512]{1,0:T(8,128)(2,1)S(1)} %copy-done, ...), custom_call_target="tpu_custom_call" | custom-call | flops 536870912 | bytes 2097152 | tf_op jit(solution)/shard_map/o_share/pallas_call | solution.py:122
  73.2 5.9 %collective-permute-done.27.landed = bf16[128,1024]{1,0:T(8,128)(2,1)S(1)} collective-permute-done((bf16[128,1024]{1,0:T(8,128)(2,1)S(1)}, bf16[128,1024]{1,0:T(8,128)(2,1)S(1)}, u32[]{:S(2)}, u32[]{:S(2)}) %collective-permute-start.27) | collective-permute-done | bytes 262176 | tf_op jit(solution)/shard_map/ppermute | solution.py:365
  79.7 1.6 %collective-permute-start.28 = (bf16[128,512]{1,0:T(8,128)(2,1)S(1)}, bf16[128,512]{1,0:T(8,128)(2,1)S(1)}, u32[]{:S(2)}, u32[]{:S(2)}) collective-permute-start(bf16[128,512]{1,0:T(8,128)(2,1)S(1)} %get-tuple-element.84), channel_id=1, source_target_pairs={{0,1},{1,0},{2,3},{3,2},{4,5},{5,4},{6,7},{7,6},{8,9},{9,8},{10,11... | collective-permute-start | bytes 393224 | tf_op jit(solution)/shard_map/ppermute | solution.py:374
  81.4 2.6 %collective-permute-start.29 = (bf16[128,512]{1,0:T(8,128)(2,1)S(1)}, bf16[128,512]{1,0:T(8,128)(2,1)S(1)}, u32[]{:S(2)}, u32[]{:S(2)}) collective-permute-start(bf16[128,512]{1,0:T(8,128)(2,1)S(1)} %get-tuple-element.85), channel_id=1, source_target_pairs={{0,2},{1,3},{2,0},{3,1},{4,6},{5,7},{6,4},{7,5},{8,10},{9,11},{10,... | collective-permute-start | bytes 393224 | tf_op jit(solution)/shard_map/ppermute | solution.py:374
  86.3 3.5 %collective-permute-start.34 = (bf16[128,512]{1,0:T(8,128)(2,1)S(1)}, bf16[128,512]{1,0:T(8,128)(2,1)S(1)}, u32[]{:S(2)}, u32[]{:S(2)}) collective-permute-start(bf16[128,512]{1,0:T(8,128)(2,1)S(1)} %get-tuple-element.91), channel_id=1, source_target_pairs={{0,2},{1,3},{2,0},{3,1},{4,6},{5,7},{6,4},{7,5},{8,10},{9,11},{10,... | collective-permute-start | bytes 393224 | tf_op jit(solution)/shard_map/ppermute | solution.py:374
  90.0 4.2 %collective-permute-done.29.refs_2_ = bf16[128,512]{1,0:T(8,128)(2,1)S(1)} collective-permute-done((bf16[128,512]{1,0:T(8,128)(2,1)S(1)}, bf16[128,512]{1,0:T(8,128)(2,1)S(1)}, u32[]{:S(2)}, u32[]{:S(2)}) %collective-permute-start.29) | collective-permute-done | bytes 131104 | tf_op jit(solution)/shard_map/ppermute | solution.py:374
  94.4 9.8 %collective-permute-done.34.refs_2_ = bf16[128,512]{1,0:T(8,128)(2,1)S(1)} collective-permute-done((bf16[128,512]{1,0:T(8,128)(2,1)S(1)}, bf16[128,512]{1,0:T(8,128)(2,1)S(1)}, u32[]{:S(2)}, u32[]{:S(2)}) %collective-permute-start.34) | collective-permute-done | bytes 131104 | tf_op jit(solution)/shard_map/ppermute | solution.py:374
  104.2 1.3 %mix_keep.1 = bf16[128,1024]{1,0:T(8,128)(2,1)} custom-call(s32[3]{0:T(128)S(1)} %copy-done.5, f32[1]{0:T(128)S(6)} %tanh.3.gate, bf16[128,512]{1,0:T(8,128)(2,1)S(1)} %copy-done.4, bf16[128,512]{1,0:T(8,128)(2,1)S(1)} %collective-permute-done.31.back, bf16[128,512]{1,0:T(8,128)(2,1)S(1)} %get-tuple-element.89.refs_0_, ...), custom_call_target="tpu_custom_call" | custom-call | flops 1048576 | bytes 1048576 | tf_op jit(solution)/shard_map/mix_keep/pallas_call | solution.py:122
  (93 shorter events, 18.2 us)
Async XLA Ops:
  0.0 16.0 %collective-permute-start.6 = (bf16[512,2048]{1,0:T(8,128)(2,1)}, bf16[512,2048]{1,0:T(8,128)(2,1)}, u32[]{:S(2)}, u32[]{:S(2)}) collective-permute-start(bf16[512,2048]{1,0:T(8,128)(2,1)} %kv_own.1), channel_id=1, source_target_pairs={{0,4},{4,0},{8,12},{12,8},{16,20},{20,16},{24,28},{28,24},{1,5},{5... | collective-permute-start | bytes 6291464 | tf_op jit(solution)/shard_map/ppermute | solution.py:362
  5.2 6.8 %collective-permute-start.2 = (bf16[16,1024]{1,0:T(8,128)(2,1)}, bf16[16,1024]{1,0:T(8,128)(2,1)S(1)}, u32[]{:S(2)}, u32[]{:S(2)}) collective-permute-start(bf16[16,1024]{1,0:T(8,128)(2,1)} %get-tuple-element.53), channel_id=1, source_target_pairs={{0,8},{4,12},{8,0},{12,4},{16,24},{20,28},{24,16},{28,20},{1,9},{5... | collective-permute-start | bytes 98312 | tf_op jit(solution)/shard_map/ppermute | solution.py:365
  7.7 5.8 %collective-permute-start.3 = (bf16[16,1024]{1,0:T(8,128)(2,1)}, bf16[16,1024]{1,0:T(8,128)(2,1)S(1)}, u32[]{:S(2)}, u32[]{:S(2)}) collective-permute-start(bf16[16,1024]{1,0:T(8,128)(2,1)} %get-tuple-element.54), channel_id=1, source_target_pairs={{0,16},{4,20},{8,24},{12,28},{16,0},{20,4},{24,8},{28,12},{1,17},{... | collective-permute-start | bytes 98312 | tf_op jit(solution)/shard_map/ppermute | solution.py:365
  9.3 5.4 %collective-permute-start.4 = (bf16[16,1024]{1,0:T(8,128)(2,1)}, bf16[16,1024]{1,0:T(8,128)(2,1)S(1)}, u32[]{:S(2)}, u32[]{:S(2)}) collective-permute-start(bf16[16,1024]{1,0:T(8,128)(2,1)} %get-tuple-element.55), channel_id=1, source_target_pairs={{0,24},{4,28},{8,16},{12,20},{16,8},{20,12},{24,0},{28,4},{1,25},{... | collective-permute-start | bytes 98312 | tf_op jit(solution)/shard_map/ppermute | solution.py:365
  9.3 15.6 %collective-permute-start.10 = (bf16[512,512]{1,0:T(8,128)(2,1)}, bf16[512,512]{1,0:T(8,128)(2,1)S(1)}, u32[]{:S(2)}, u32[]{:S(2)}) collective-permute-start(bf16[512,512]{1,0:T(8,128)(2,1)} %get-tuple-element.60.q_keep), channel_id=1, source_target_pairs={{0,8},{4,12},{8,0},{12,4},{16,24},{20,28},{24,16},{28,20},{1,9},{5... | collective-permute-start | bytes 1572872 | tf_op jit(solution)/shard_map/ppermute | solution.py:365
  12.0 15.5 %collective-permute-start.11 = (bf16[128,2048]{1,0:T(8,128)(2,1)}, bf16[128,2048]{1,0:T(8,128)(2,1)S(1)}, u32[]{:S(2)}, u32[]{:S(2)}) collective-permute-start(bf16[128,2048]{1,0:T(8,128)(2,1)} %get-tuple-element.61), channel_id=1, source_target_pairs={{0,16},{4,20},{8,24},{12,28},{16,0},{20,4},{24,8},{28,12},{1,17},{... | collective-permute-start | bytes 1572872 | tf_op jit(solution)/shard_map/ppermute | solution.py:365
  14.6 16.7 %collective-permute-start.12 = (bf16[512,512]{1,0:T(8,128)(2,1)}, bf16[512,512]{1,0:T(8,128)(2,1)S(1)}, u32[]{:S(2)}, u32[]{:S(2)}) collective-permute-start(bf16[512,512]{1,0:T(8,128)(2,1)} %get-tuple-element.63), channel_id=1, source_target_pairs={{0,4},{4,0},{8,12},{12,8},{16,20},{20,16},{24,28},{28,24},{1,5},{5... | collective-permute-start | bytes 1572872 | tf_op jit(solution)/shard_map/ppermute | solution.py:362
  18.6 8.8 %collective-permute-start.7 = (f32[32,1024]{1,0:T(8,128)S(1)}, f32[32,1024]{1,0:T(8,128)S(1)}, u32[]{:S(2)}, u32[]{:S(2)}) collective-permute-start(f32[32,1024]{1,0:T(8,128)S(1)} %get-tuple-element.57), channel_id=1, source_target_pairs={{0,8},{4,12},{8,0},{12,4},{16,24},{20,28},{24,16},{28,20},{1,9},{5... | collective-permute-start | bytes 393224 | tf_op jit(solution)/shard_map/ppermute | solution.py:365
  19.0 12.2 %collective-permute-start.8 = (f32[32,1024]{1,0:T(8,128)S(1)}, f32[32,1024]{1,0:T(8,128)S(1)}, u32[]{:S(2)}, u32[]{:S(2)}) collective-permute-start(f32[32,1024]{1,0:T(8,128)S(1)} %get-tuple-element.58), channel_id=1, source_target_pairs={{0,16},{4,20},{8,24},{12,28},{16,0},{20,4},{24,8},{28,12},{1,17},{... | collective-permute-start | bytes 393224 | tf_op jit(solution)/shard_map/ppermute | solution.py:365
  24.9 6.4 %collective-permute-start.9 = (f32[32,1024]{1,0:T(8,128)S(1)}, f32[32,1024]{1,0:T(8,128)S(1)}, u32[]{:S(2)}, u32[]{:S(2)}) collective-permute-start(f32[32,1024]{1,0:T(8,128)S(1)} %get-tuple-element.59), channel_id=1, source_target_pairs={{0,24},{4,28},{8,16},{12,20},{16,8},{20,12},{24,0},{28,4},{1,25},{... | collective-permute-start | bytes 393224 | tf_op jit(solution)/shard_map/ppermute | solution.py:365
  27.5 23.0 %collective-permute-start.1 = (bf16[128,2048]{1,0:T(8,128)(2,1)S(1)}, bf16[128,2048]{1,0:T(8,128)(2,1)S(1)}, u32[]{:S(2)}, u32[]{:S(2)}) collective-permute-start(bf16[128,2048]{1,0:T(8,128)(2,1)S(1)} %copy-done.2), channel_id=1, source_target_pairs={{0,4},{4,0},{8,12},{12,8},{16,20},{20,16},{24,28},{28,24},{1,5},{5... | collective-permute-start | bytes 1572872 | tf_op jit(solution)/shard_map/ppermute | solution.py:362
  27.5 7.1 %collective-permute-start.22 = (s32[128]{0:T(128)S(1)}, s32[128]{0:T(128)S(1)}, u32[]{:S(2)}, u32[]{:S(2)}) collective-permute-start(s32[128]{0:T(128)S(1)} %copy-done.10), channel_id=1, source_target_pairs={{0,4},{4,0},{8,12},{12,8},{16,20},{20,16},{24,28},{28,24},{1,5},{5... | collective-permute-start | bytes 1544 | tf_op jit(solution)/shard_map/ppermute | solution.py:362
  31.3 5.0 %collective-permute-start.15 = (bf16[128,2048]{1,0:T(8,128)(2,1)S(1)}, bf16[128,2048]{1,0:T(8,128)(2,1)S(1)}, u32[]{:S(2)}, u32[]{:S(2)}) collective-permute-start(bf16[128,2048]{1,0:T(8,128)(2,1)S(1)} %collective-permute-done.11.own), channel_id=1, source_target_pairs={{0,4},{4,0},{8,12},{12,8},{16,20},{20,16},{24,28},{28,24},{1,5},{5... | collective-permute-start | bytes 1572872 | tf_op jit(solution)/shard_map/ppermute | solution.py:362
  31.4 14.8 %collective-permute-start.13 = (bf16[512,512]{1,0:T(8,128)(2,1)S(1)}, bf16[512,512]{1,0:T(8,128)(2,1)S(1)}, u32[]{:S(2)}, u32[]{:S(2)}) collective-permute-start(bf16[512,512]{1,0:T(8,128)(2,1)S(1)} %collective-permute-done.12.q_other), channel_id=1, source_target_pairs={{0,8},{4,12},{8,0},{12,4},{16,24},{20,28},{24,16},{28,20},{1,9},{5... | collective-permute-start | bytes 1572872 | tf_op jit(solution)/shard_map/ppermute | solution.py:365
  33.0 15.0 %collective-permute-start.18 = (bf16[512,512]{1,0:T(8,128)(2,1)S(1)}, bf16[512,512]{1,0:T(8,128)(2,1)S(1)}, u32[]{:S(2)}, u32[]{:S(2)}) collective-permute-start(bf16[512,512]{1,0:T(8,128)(2,1)S(1)} %get-tuple-element.75), channel_id=1, source_target_pairs={{0,16},{4,20},{8,24},{12,28},{16,0},{20,4},{24,8},{28,12},{1,17},{... | collective-permute-start | bytes 1572872 | tf_op jit(solution)/shard_map/ppermute | solution.py:365
  38.6 4.8 %collective-permute-start.16 = (bf16[64,256]{1,0:T(8,128)(2,1)S(1)}, bf16[64,256]{1,0:T(8,128)(2,1)S(1)}, u32[]{:S(2)}, u32[]{:S(2)}) collective-permute-start(bf16[64,256]{1,0:T(8,128)(2,1)S(1)} %kv_turn.1), channel_id=1, source_target_pairs={{0,2},{1,3},{2,0},{3,1},{4,6},{5,7},{6,4},{7,5},{8,10},{9,11},{10,... | collective-permute-start | bytes 98312 | tf_op jit(solution)/shard_map/ppermute | solution.py:374
  44.5 8.7 %collective-permute-start.20 = (bf16[128,256]{1,0:T(8,128)(2,1)S(1)}, bf16[128,256]{1,0:T(8,128)(2,1)S(1)}, u32[]{:S(2)}, u32[]{:S(2)}) collective-permute-start(bf16[128,256]{1,0:T(8,128)(2,1)S(1)} %kv_join.1.refs_0_), channel_id=1, source_target_pairs={{0,16},{4,20},{8,24},{12,28},{16,0},{20,4},{24,8},{28,12},{1,17},{... | collective-permute-start | bytes 196616 | tf_op jit(solution)/shard_map/ppermute | solution.py:365
  46.2 7.0 %collective-permute-start.21 = (bf16[128,256]{1,0:T(8,128)(2,1)S(1)}, bf16[128,256]{1,0:T(8,128)(2,1)S(1)}, u32[]{:S(2)}, u32[]{:S(2)}) collective-permute-start(bf16[128,256]{1,0:T(8,128)(2,1)S(1)} %kv_join.1.refs_0_), channel_id=1, source_target_pairs={{0,24},{4,28},{8,16},{12,20},{16,8},{20,12},{24,0},{28,4},{1,25},{... | collective-permute-start | bytes 196616 | tf_op jit(solution)/shard_map/ppermute | solution.py:365
  49.0 9.3 %collective-permute-start.19 = (bf16[256,512]{1,0:T(8,128)(2,1)S(1)}, bf16[256,512]{1,0:T(8,128)(2,1)S(1)}, u32[]{:S(2)}, u32[]{:S(2)}) collective-permute-start(bf16[256,512]{1,0:T(8,128)(2,1)S(1)} %q_late.3), channel_id=1, source_target_pairs={{0,16},{4,20},{8,24},{12,28},{16,0},{20,4},{24,8},{28,12},{1,17},{... | collective-permute-start | bytes 786440 | tf_op jit(solution)/shard_map/ppermute | solution.py:365
  51.4 16.7 %collective-permute-start.24 = (bf16[512,512]{1,0:T(8,128)(2,1)S(1)}, bf16[512,512]{1,0:T(8,128)(2,1)S(1)}, u32[]{:S(2)}, u32[]{:S(2)}) collective-permute-start(bf16[512,512]{1,0:T(8,128)(2,1)S(1)} %get-tuple-element.80), channel_id=1, source_target_pairs={{0,16},{4,20},{8,24},{12,28},{16,0},{20,4},{24,8},{28,12},{1,17},{... | collective-permute-start | bytes 1572872 | tf_op jit(solution)/shard_map/ppermute | solution.py:365
  60.6 6.4 %collective-permute-start.25 = (bf16[256,512]{1,0:T(8,128)(2,1)S(1)}, bf16[256,512]{1,0:T(8,128)(2,1)S(1)}, u32[]{:S(2)}, u32[]{:S(2)}) collective-permute-start(bf16[256,512]{1,0:T(8,128)(2,1)S(1)} %attend.1.near), channel_id=1, source_target_pairs={{0,8},{4,12},{8,0},{12,4},{16,24},{20,28},{24,16},{28,20},{1,9},{5... | collective-permute-start | bytes 786440 | tf_op jit(solution)/shard_map/ppermute | solution.py:365
  67.1 4.9 %collective-permute-start.23 = (bf16[256,512]{1,0:T(8,128)(2,1)S(1)}, bf16[256,512]{1,0:T(8,128)(2,1)S(1)}, u32[]{:S(2)}, u32[]{:S(2)}) collective-permute-start(bf16[256,512]{1,0:T(8,128)(2,1)S(1)} %attend.1.near), channel_id=1, source_target_pairs={{0,4},{4,0},{8,12},{12,8},{16,20},{20,16},{24,28},{28,24},{1,5},{5... | collective-permute-start | bytes 786440 | tf_op jit(solution)/shard_map/ppermute | solution.py:362
  69.9 9.2 %collective-permute-start.27 = (bf16[128,1024]{1,0:T(8,128)(2,1)S(1)}, bf16[128,1024]{1,0:T(8,128)(2,1)S(1)}, u32[]{:S(2)}, u32[]{:S(2)}) collective-permute-start(bf16[128,1024]{1,0:T(8,128)(2,1)S(1)} %get-tuple-element.82), channel_id=1, source_target_pairs={{0,8},{4,12},{8,0},{12,4},{16,24},{20,28},{24,16},{28,20},{1,9},{5... | collective-permute-start | bytes 786440 | tf_op jit(solution)/shard_map/ppermute | solution.py:365
  70.9 14.0 %collective-permute-start.32 = (bf16[128,1024]{1,0:T(8,128)(2,1)S(1)}, bf16[128,1024]{1,0:T(8,128)(2,1)S(1)}, u32[]{:S(2)}, u32[]{:S(2)}) collective-permute-start(bf16[128,1024]{1,0:T(8,128)(2,1)S(1)} %get-tuple-element.88), channel_id=1, source_target_pairs={{0,8},{4,12},{8,0},{12,4},{16,24},{20,28},{24,16},{28,20},{1,9},{5... | collective-permute-start | bytes 786440 | tf_op jit(solution)/shard_map/ppermute | solution.py:365
  72.0 14.3 %collective-permute-start = (bf16[128,512]{1,0:T(8,128)(2,1)S(1)}, bf16[128,512]{1,0:T(8,128)(2,1)S(1)}, u32[]{:S(2)}, u32[]{:S(2)}) collective-permute-start(bf16[128,512]{1,0:T(8,128)(2,1)S(1)} %copy-done.11), channel_id=1, source_target_pairs={{0,4},{4,0},{8,12},{12,8},{16,20},{20,16},{24,28},{28,24},{1,5},{5... | collective-permute-start | bytes 393224 | tf_op jit(solution)/shard_map/ppermute | solution.py:362
  79.7 10.0 %collective-permute-start.28 = (bf16[128,512]{1,0:T(8,128)(2,1)S(1)}, bf16[128,512]{1,0:T(8,128)(2,1)S(1)}, u32[]{:S(2)}, u32[]{:S(2)}) collective-permute-start(bf16[128,512]{1,0:T(8,128)(2,1)S(1)} %get-tuple-element.84), channel_id=1, source_target_pairs={{0,1},{1,0},{2,3},{3,2},{4,5},{5,4},{6,7},{7,6},{8,9},{9,8},{10,11... | collective-permute-start | bytes 393224 | tf_op jit(solution)/shard_map/ppermute | solution.py:374
  81.4 12.8 %collective-permute-start.29 = (bf16[128,512]{1,0:T(8,128)(2,1)S(1)}, bf16[128,512]{1,0:T(8,128)(2,1)S(1)}, u32[]{:S(2)}, u32[]{:S(2)}) collective-permute-start(bf16[128,512]{1,0:T(8,128)(2,1)S(1)} %get-tuple-element.85), channel_id=1, source_target_pairs={{0,2},{1,3},{2,0},{3,1},{4,6},{5,7},{6,4},{7,5},{8,10},{9,11},{10,... | collective-permute-start | bytes 393224 | tf_op jit(solution)/shard_map/ppermute | solution.py:374
  84.0 10.2 %collective-permute-start.30 = (bf16[128,512]{1,0:T(8,128)(2,1)S(1)}, bf16[128,512]{1,0:T(8,128)(2,1)S(1)}, u32[]{:S(2)}, u32[]{:S(2)}) collective-permute-start(bf16[128,512]{1,0:T(8,128)(2,1)S(1)} %get-tuple-element.86), channel_id=1, source_target_pairs={{0,3},{1,2},{2,1},{3,0},{4,7},{5,6},{6,5},{7,4},{8,11},{9,10},{10,... | collective-permute-start | bytes 393224 | tf_op jit(solution)/shard_map/ppermute | solution.py:374
  85.5 8.8 %collective-permute-start.33 = (bf16[128,512]{1,0:T(8,128)(2,1)S(1)}, bf16[128,512]{1,0:T(8,128)(2,1)S(1)}, u32[]{:S(2)}, u32[]{:S(2)}) collective-permute-start(bf16[128,512]{1,0:T(8,128)(2,1)S(1)} %get-tuple-element.90), channel_id=1, source_target_pairs={{0,1},{1,0},{2,3},{3,2},{4,5},{5,4},{6,7},{7,6},{8,9},{9,8},{10,11... | collective-permute-start | bytes 393224 | tf_op jit(solution)/shard_map/ppermute | solution.py:374
  86.3 17.9 %collective-permute-start.34 = (bf16[128,512]{1,0:T(8,128)(2,1)S(1)}, bf16[128,512]{1,0:T(8,128)(2,1)S(1)}, u32[]{:S(2)}, u32[]{:S(2)}) collective-permute-start(bf16[128,512]{1,0:T(8,128)(2,1)S(1)} %get-tuple-element.91), channel_id=1, source_target_pairs={{0,2},{1,3},{2,0},{3,1},{4,6},{5,7},{6,4},{7,5},{8,10},{9,11},{10,... | collective-permute-start | bytes 393224 | tf_op jit(solution)/shard_map/ppermute | solution.py:374
  89.8 14.4 %collective-permute-start.35 = (bf16[128,512]{1,0:T(8,128)(2,1)S(1)}, bf16[128,512]{1,0:T(8,128)(2,1)S(1)}, u32[]{:S(2)}, u32[]{:S(2)}) collective-permute-start(bf16[128,512]{1,0:T(8,128)(2,1)S(1)} %get-tuple-element.92), channel_id=1, source_target_pairs={{0,3},{1,2},{2,1},{3,0},{4,7},{5,6},{6,5},{7,4},{8,11},{9,10},{10,... | collective-permute-start | bytes 393224 | tf_op jit(solution)/shard_map/ppermute | solution.py:374
  94.3 9.9 %collective-permute-start.31 = (bf16[128,512]{1,0:T(8,128)(2,1)S(1)}, bf16[128,512]{1,0:T(8,128)(2,1)S(1)}, u32[]{:S(2)}, u32[]{:S(2)}) collective-permute-start(bf16[128,512]{1,0:T(8,128)(2,1)S(1)} %mix_give.1), channel_id=1, source_target_pairs={{0,4},{4,0},{8,12},{12,8},{16,20},{20,16},{24,28},{28,24},{1,5},{5... | collective-permute-start | bytes 393224 | tf_op jit(solution)/shard_map/ppermute | solution.py:362
  (16 other events, 182.2 us)

commit v2 on v1

--- a/solution.py
+++ b/solution.py
@@ -418,6 +418,8 @@
     )
     shares = [shares[0]] + [peer(shares[s], s) for s in steps]
     own_share = shares[0]
+    q_behind, _ = lax.optimization_barrier((q_other, (own_share, q_side)))
+    q_corner = along_x(q_behind)
     shares, q_side, far = lax.optimization_barrier((shares, q_side, far))
     here, there, give = call(
         kv_norm_kernel,
@@ -439,28 +441,9 @@
         )[0]
         for pair in blocks
     ]
-    kv_z, early[0] = lax.optimization_barrier((across(give, 1), early[0]))
-    turn = call(
-        kv_turn_kernel,
-        (there, kv_z),
-        [VMEM] * 2,
-        [shape(4 * vis_here, 2 * head_dim)],
-        name="kv_turn",
-    )[0]
-    kv_first = call(
-        kv_join_kernel,
-        (here, kv_z, across(turn, 2)),
-        [VMEM] * 3,
-        [shape(8 * vis_here, 2 * head_dim)],
-        name="kv_join",
-    )[0]
-    kv_all = [kv_first] + [peer(kv_first, s) for s in steps]
-    q_behind, _ = lax.optimization_barrier((q_other, own_share))
-    q_corner = along_x(q_behind)
-    q_corner, kv_all[1] = lax.optimization_barrier((q_corner, kv_all[1]))
-
+    kv_z, q_corner = lax.optimization_barrier((across(give, 1), q_corner))
     o_early, _ = lax.optimization_barrier((o_weight[:half], here))
-    q_corner, o_early = lax.optimization_barrier((q_corner, along_y(o_early)))
+    o_early = along_y(o_early)
     q_far, q_first = [
         call(
             late_kernel,
@@ -473,6 +456,24 @@
         )[0]
         for k, kind in ((0, BF16), (1, F32))
     ]
+    turn = call(
+        kv_turn_kernel,
+        (there, kv_z),
+        [VMEM] * 2,
+        [shape(4 * vis_here, 2 * head_dim)],
+        name="kv_turn",
+    )[0]
+    kv_last, o_early, q_far = lax.optimization_barrier((across(turn, 2), o_early, q_far))
+    kv_first = call(
+        kv_join_kernel,
+        (here, kv_z, kv_last),
+        [VMEM] * 3,
+        [shape(8 * vis_here, 2 * head_dim)],
+        name="kv_join",
+    )[0]
+    kv_first, _ = lax.optimization_barrier((kv_first, q_first))
+    kv_all = [kv_first] + [peer(kv_first, s) for s in steps]
+
     landed = along_y(q_far)
     o_late, _ = lax.optimization_barrier((o_weight[half:], q_far))
     o_late = along_y(o_late)

time: 106 us -> 107 us (level)
  waiting for transfers between devices: 46.7 us -> 48.1 us
    ppermute x18, waiting for transfers between devices: 28 us -> 30.8 us  [peer(): return lax.ppermute(x, 'ctx', [(k, k ^ 2 * s) for k in range(ctx_count)])]
    ppermute x8, waiting for transfers between devices: 17.4 us -> 15.4 us  [across(): return lax.ppermute(x, 'img', [(k, k ^ t) for k in range(CHIPS)])]
where the time goes in v2:
time: 107 us; the launch traced here: 106 us
  waiting for transfers between devices  48.1 us (45%)
  starting transfers between devices  36.4 us (34%)
  Pallas kernels  18.9 us (18%)
  other arithmetic  1.07 us (1%)
    ppermute x18, waiting for transfers between devices, peer(): return lax.ppermute(x, 'ctx', [(k, k ^ 2 * s) for k in range(ctx_count)])  30.8 us
    ppermute x18, starting transfers between devices, peer(): return lax.ppermute(x, 'ctx', [(k, k ^ 2 * s) for k in range(ctx_count)])  21.7 us
    pallas_call x16, Pallas kernels, call(): pl.pallas_call(kernel, out_shape=outs, in_specs=specs, out_specs=[VMEM] *...  18.9 us
    ppermute x8, waiting for transfers between devices, across(): return lax.ppermute(x, 'img', [(k, k ^ t) for k in range(CHIPS)])  15.4 us
    ppermute x8, starting transfers between devices, across(): return lax.ppermute(x, 'img', [(k, k ^ t) for k in range(CHIPS)])  13.1 us
  transfers between devices with their start and end apart: 36, of which 15 were waited for; matrix products, arithmetic and copies ran while one was open for 2% of the time, Pallas kernels for 16%

profile of v2, /device:TPU:0, one launch (start us, length us, event | category | flops | bytes accessed | tf_op | source)
XLA Modules:
  0.0 106.4 jit_solution(18258049677933413110)
XLA Ops:
  1.1 4.2 %start.1 = (bf16[16,1024]{1,0:T(8,128)(2,1)}, bf16[16,1024]{1,0:T(8,128)(2,1)}, bf16[16,1024]{1,0:T(8,128)(2,1)}, bf16[16,1024]{1,0:T(8,128)(2,1)}, bf16[128,204...) custom-call(s32[3]{0:T(128)} %pad_add_fusion.1.where, ...), custom_call_target="tpu_custom_call" | custom-call | flops 4194304 | bytes 4194304 | tf_op jit(solution)/shard_map/start/pallas_call | solution.py:122
  5.3 2.6 %collective-permute-start.2 = (bf16[16,1024]{1,0:T(8,128)(2,1)}, bf16[16,1024]{1,0:T(8,128)(2,1)S(1)}, u32[]{:S(2)}, u32[]{:S(2)}) collective-permute-start(bf16[16,1024]{1,0:T(8,128)(2,1)} %get-tuple-element.53), channel_id=1, source_target_pairs={{0,8},{4,12},{8,0},{12,4},{16,24},{20,28},{24,16},{28,20},{1,9},{5... | collective-permute-start | bytes 98312 | tf_op jit(solution)/shard_map/ppermute | solution.py:365
  7.9 1.5 %collective-permute-start.3 = (bf16[16,1024]{1,0:T(8,128)(2,1)}, bf16[16,1024]{1,0:T(8,128)(2,1)S(1)}, u32[]{:S(2)}, u32[]{:S(2)}) collective-permute-start(bf16[16,1024]{1,0:T(8,128)(2,1)} %get-tuple-element.54), channel_id=1, source_target_pairs={{0,16},{4,20},{8,24},{12,28},{16,0},{20,4},{24,8},{28,12},{1,17},{... | collective-permute-start | bytes 98312 | tf_op jit(solution)/shard_map/ppermute | solution.py:365
  9.4 1.9 %collective-permute-start.10 = (bf16[512,512]{1,0:T(8,128)(2,1)}, bf16[512,512]{1,0:T(8,128)(2,1)S(1)}, u32[]{:S(2)}, u32[]{:S(2)}) collective-permute-start(bf16[512,512]{1,0:T(8,128)(2,1)} %get-tuple-element.60.q_keep), channel_id=1, source_target_pairs={{0,8},{4,12},{8,0},{12,4},{16,24},{20,28},{24,16},{28,20},{1,9},{5... | collective-permute-start | bytes 1572872 | tf_op jit(solution)/shard_map/ppermute | solution.py:365
  12.1 1.5 %collective-permute-start.11 = (bf16[128,2048]{1,0:T(8,128)(2,1)}, bf16[128,2048]{1,0:T(8,128)(2,1)S(1)}, u32[]{:S(2)}, u32[]{:S(2)}) collective-permute-start(bf16[128,2048]{1,0:T(8,128)(2,1)} %get-tuple-element.61), channel_id=1, source_target_pairs={{0,16},{4,20},{8,24},{12,28},{16,0},{20,4},{24,8},{28,12},{1,17},{... | collective-permute-start | bytes 1572872 | tf_op jit(solution)/shard_map/ppermute | solution.py:365
  14.9 1.2 %collective-permute-done.5.vis_other = bf16[64,1024]{1,0:T(8,128)(2,1)S(1)} collective-permute-done((bf16[64,1024]{1,0:T(8,128)(2,1)S(1)}, bf16[64,1024]{1,0:T(8,128)(2,1)S(1)}, u32[]{:S(2)}, u32[]{:S(2)}) %collective-permute-start.5) | collective-permute-done | bytes 131104 | tf_op jit(solution)/shard_map/ppermute | solution.py:362
  16.1 2.6 %kv_shares.1 = (f32[32,1024]{1,0:T(8,128)S(1)}, f32[32,1024]{1,0:T(8,128)S(1)}, f32[32,1024]{1,0:T(8,128)S(1)}, f32[32,1024]{1,0:T(8,128)S(1)}) custom-call(s32[3]{0:T(128)S(1)} %copy-done.5, bf16[64,1024]{1,0:T(8,128)(2,1)S(1)} %constant_dynamic-update-slice_fusion.vis, bf16[64,1024]{1,0:T(8,128)(2,1)S(1)} %collective-permute-done.5.vis_other, ...), custom_call_target="tpu_custom_call" | custom-call | flops 536870912 | bytes 4194304 | tf_op jit(solution)/shard_map/kv_shares/pallas_call | solution.py:122
  19.3 5.7 %collective-permute-done.10.q_side = bf16[512,512]{1,0:T(8,128)(2,1)S(1)} collective-permute-done((bf16[512,512]{1,0:T(8,128)(2,1)}, bf16[512,512]{1,0:T(8,128)(2,1)S(1)}, u32[]{:S(2)}, u32[]{:S(2)}) %collective-permute-start.10) | collective-permute-done | bytes 524320 | tf_op jit(solution)/shard_map/ppermute | solution.py:365
  25.1 2.3 %collective-permute-start.9 = (f32[32,1024]{1,0:T(8,128)S(1)}, f32[32,1024]{1,0:T(8,128)S(1)}, u32[]{:S(2)}, u32[]{:S(2)}) collective-permute-start(f32[32,1024]{1,0:T(8,128)S(1)} %get-tuple-element.59), channel_id=1, source_target_pairs={{0,24},{4,28},{8,16},{12,20},{16,8},{20,12},{24,0},{28,4},{1,25},{... | collective-permute-start | bytes 393224 | tf_op jit(solution)/shard_map/ppermute | solution.py:365
  28.7 2.7 %collective-permute-done.8.refs_2_ = f32[32,1024]{1,0:T(8,128)S(1)} collective-permute-done((f32[32,1024]{1,0:T(8,128)S(1)}, f32[32,1024]{1,0:T(8,128)S(1)}, u32[]{:S(2)}, u32[]{:S(2)}) %collective-permute-start.8) | collective-permute-done | bytes 131104 | tf_op jit(solution)/shard_map/ppermute | solution.py:365
  32.1 1.4 %collective-permute-start.16 = (bf16[512,512]{1,0:T(8,128)(2,1)S(1)}, bf16[512,512]{1,0:T(8,128)(2,1)S(1)}, u32[]{:S(2)}, u32[]{:S(2)}) collective-permute-start(bf16[512,512]{1,0:T(8,128)(2,1)S(1)} %get-tuple-element.74), channel_id=1, source_target_pairs={{0,16},{4,20},{8,24},{12,28},{16,0},{20,4},{24,8},{28,12},{1,17},{... | collective-permute-start | bytes 1572872 | tf_op jit(solution)/shard_map/ppermute | solution.py:365
  33.6 1.6 %collective-permute-start.12 = (bf16[64,256]{1,0:T(8,128)(2,1)S(1)}, bf16[64,256]{1,0:T(8,128)(2,1)S(1)}, u32[]{:S(2)}, u32[]{:S(2)}) collective-permute-start(bf16[64,256]{1,0:T(8,128)(2,1)S(1)} %get-tuple-element.67), channel_id=1, source_target_pairs={{0,1},{1,0},{2,3},{3,2},{4,5},{5,4},{6,7},{7,6},{8,9},{9,8},{10,11... | collective-permute-start | bytes 98312 | tf_op jit(solution)/shard_map/ppermute | solution.py:374
  36.4 1.2 %collective-permute-done.12.landed = bf16[64,256]{1,0:T(8,128)(2,1)S(1)} collective-permute-done((bf16[64,256]{1,0:T(8,128)(2,1)S(1)}, bf16[64,256]{1,0:T(8,128)(2,1)S(1)}, u32[]{:S(2)}, u32[]{:S(2)}) %collective-permute-start.12) | collective-permute-done | bytes 32800 | tf_op jit(solution)/shard_map/ppermute | solution.py:374
  37.6 4.7 %collective-permute-done.14.q_corner = bf16[512,512]{1,0:T(8,128)(2,1)S(1)} collective-permute-done((bf16[512,512]{1,0:T(8,128)(2,1)S(1)}, bf16[512,512]{1,0:T(8,128)(2,1)S(1)}, u32[]{:S(2)}, u32[]{:S(2)}) %collective-permute-start.14) | collective-permute-done | bytes 524320 | tf_op jit(solution)/shard_map/ppermute | solution.py:365
  42.3 2.6 %collective-permute-start.15 = (bf16[64,256]{1,0:T(8,128)(2,1)S(1)}, bf16[64,256]{1,0:T(8,128)(2,1)S(1)}, u32[]{:S(2)}, u32[]{:S(2)}) collective-permute-start(bf16[64,256]{1,0:T(8,128)(2,1)S(1)} %kv_turn.1), channel_id=1, source_target_pairs={{0,2},{1,3},{2,0},{3,1},{4,6},{5,7},{6,4},{7,5},{8,10},{9,11},{10,... | collective-permute-start | bytes 98312 | tf_op jit(solution)/shard_map/ppermute | solution.py:374
  47.1 2.0 %collective-permute-start.18 = (bf16[256,512]{1,0:T(8,128)(2,1)S(1)}, bf16[256,512]{1,0:T(8,128)(2,1)S(1)}, u32[]{:S(2)}, u32[]{:S(2)}) collective-permute-start(bf16[256,512]{1,0:T(8,128)(2,1)S(1)} %q_late.3), channel_id=1, source_target_pairs={{0,16},{4,20},{8,24},{12,28},{16,0},{20,4},{24,8},{28,12},{1,17},{... | collective-permute-start | bytes 786440 | tf_op jit(solution)/shard_map/ppermute | solution.py:365
  51.5 2.2 %collective-permute-start.21 = (bf16[128,256]{1,0:T(8,128)(2,1)S(1)}, bf16[128,256]{1,0:T(8,128)(2,1)S(1)}, u32[]{:S(2)}, u32[]{:S(2)}) collective-permute-start(bf16[128,256]{1,0:T(8,128)(2,1)S(1)} %kv_join.1.refs_0_), channel_id=1, source_target_pairs={{0,24},{4,28},{8,16},{12,20},{16,8},{20,12},{24,0},{28,4},{1,25},{... | collective-permute-start | bytes 196616 | tf_op jit(solution)/shard_map/ppermute | solution.py:365
  53.8 1.1 %collective-permute-done.19.refs_1_ = bf16[128,256]{1,0:T(8,128)(2,1)S(1)} collective-permute-done((bf16[128,256]{1,0:T(8,128)(2,1)S(1)}, bf16[128,256]{1,0:T(8,128)(2,1)S(1)}, u32[]{:S(2)}, u32[]{:S(2)}) %collective-permute-start.19) | collective-permute-done | bytes 65568 | tf_op jit(solution)/shard_map/ppermute | solution.py:365
  54.9 4.2 %collective-permute-done.20.refs_2_ = bf16[128,256]{1,0:T(8,128)(2,1)S(1)} collective-permute-done((bf16[128,256]{1,0:T(8,128)(2,1)S(1)}, bf16[128,256]{1,0:T(8,128)(2,1)S(1)}, u32[]{:S(2)}, u32[]{:S(2)}) %collective-permute-start.20) | collective-permute-done | bytes 65568 | tf_op jit(solution)/shard_map/ppermute | solution.py:365
  59.2 2.3 %attend.1.near = bf16[256,512]{1,0:T(8,128)(2,1)S(1)} custom-call(f32[1,128]{1,0:T(1,128)S(1)} %bitcast.8, f32[256,512]{1,0:T(8,128)S(1)} %q_late.2.first, bf16[256,512]{1,0:T(8,128)(2,1)S(1)} %collective-permute-done.18.landed, bf16[128,256]{1,0:T(8,128)(2,1)S(1)} %kv_join.1.refs_0_, bf16[128,256]{1,0:T(8,128)(2,1)S(1)} %collective-permute-done.19.refs_1_, ...), custom_call_target="tpu_custom_call" | custom-call | flops 268435456 | bytes 2097152 | tf_op jit(solution)/shard_map/attend/pallas_call | solution.py:122
  61.5 1.4 %collective-permute-start.25 = (bf16[256,512]{1,0:T(8,128)(2,1)S(1)}, bf16[256,512]{1,0:T(8,128)(2,1)S(1)}, u32[]{:S(2)}, u32[]{:S(2)}) collective-permute-start(bf16[256,512]{1,0:T(8,128)(2,1)S(1)} %attend.1.near), channel_id=1, source_target_pairs={{0,8},{4,12},{8,0},{12,4},{16,24},{20,28},{24,16},{28,20},{1,9},{5... | collective-permute-start | bytes 786440 | tf_op jit(solution)/shard_map/ppermute | solution.py:365
  62.8 5.1 %collective-permute-done.25.near = bf16[256,512]{1,0:T(8,128)(2,1)S(1)} collective-permute-done((bf16[256,512]{1,0:T(8,128)(2,1)S(1)}, bf16[256,512]{1,0:T(8,128)(2,1)S(1)}, u32[]{:S(2)}, u32[]{:S(2)}) %collective-permute-start.25) | collective-permute-done | bytes 262176 | tf_op jit(solution)/shard_map/ppermute | solution.py:365
  69.5 1.2 %o_share.3 = (bf16[128,1024]{1,0:T(8,128)(2,1)S(1)}, bf16[128,1024]{1,0:T(8,128)(2,1)S(1)}) custom-call(s32[3]{0:T(128)S(1)} %copy-done.5, bf16[256,512]{1,0:T(8,128)(2,1)S(1)} %collective-permute-done.25.near, bf16[256,512]{1,0:T(8,128)(2,1)S(1)} %collective-permute-done.26.far, bf16[1024,512]{1,0:T(8,128)(2,1)S(1)} %copy-done, ...), custom_call_target="tpu_custom_call" | custom-call | flops 536870912 | bytes 2097152 | tf_op jit(solution)/shard_map/o_share/pallas_call | solution.py:122
  70.7 1.4 %collective-permute-start.27 = (bf16[128,1024]{1,0:T(8,128)(2,1)S(1)}, bf16[128,1024]{1,0:T(8,128)(2,1)S(1)}, u32[]{:S(2)}, u32[]{:S(2)}) collective-permute-start(bf16[128,1024]{1,0:T(8,128)(2,1)S(1)} %get-tuple-element.82), channel_id=1, source_target_pairs={{0,8},{4,12},{8,0},{12,4},{16,24},{20,28},{24,16},{28,20},{1,9},{5... | collective-permute-start | bytes 786440 | tf_op jit(solution)/shard_map/ppermute | solution.py:365
  72.8 1.3 %o_share.2 = (bf16[128,1024]{1,0:T(8,128)(2,1)S(1)}, bf16[128,1024]{1,0:T(8,128)(2,1)S(1)}) custom-call(s32[3]{0:T(128)S(1)} %copy-done.5, bf16[256,512]{1,0:T(8,128)(2,1)S(1)} %attend.1.near, bf16[256,512]{1,0:T(8,128)(2,1)S(1)} %collective-permute-done.23.far, bf16[1024,512]{1,0:T(8,128)(2,1)S(1)} %copy-done, ...), custom_call_target="tpu_custom_call" | custom-call | flops 536870912 | bytes 2097152 | tf_op jit(solution)/shard_map/o_share/pallas_call | solution.py:122
  74.1 5.8 %collective-permute-done.27.landed = bf16[128,1024]{1,0:T(8,128)(2,1)S(1)} collective-permute-done((bf16[128,1024]{1,0:T(8,128)(2,1)S(1)}, bf16[128,1024]{1,0:T(8,128)(2,1)S(1)}, u32[]{:S(2)}, u32[]{:S(2)}) %collective-permute-start.27) | collective-permute-done | bytes 262176 | tf_op jit(solution)/shard_map/ppermute | solution.py:365
  80.6 1.7 %collective-permute-start.28 = (bf16[128,512]{1,0:T(8,128)(2,1)S(1)}, bf16[128,512]{1,0:T(8,128)(2,1)S(1)}, u32[]{:S(2)}, u32[]{:S(2)}) collective-permute-start(bf16[128,512]{1,0:T(8,128)(2,1)S(1)} %get-tuple-element.84), channel_id=1, source_target_pairs={{0,1},{1,0},{2,3},{3,2},{4,5},{5,4},{6,7},{7,6},{8,9},{9,8},{10,11... | collective-permute-start | bytes 393224 | tf_op jit(solution)/shard_map/ppermute | solution.py:374
  82.2 2.4 %collective-permute-start.29 = (bf16[128,512]{1,0:T(8,128)(2,1)S(1)}, bf16[128,512]{1,0:T(8,128)(2,1)S(1)}, u32[]{:S(2)}, u32[]{:S(2)}) collective-permute-start(bf16[128,512]{1,0:T(8,128)(2,1)S(1)} %get-tuple-element.85), channel_id=1, source_target_pairs={{0,2},{1,3},{2,0},{3,1},{4,6},{5,7},{6,4},{7,5},{8,10},{9,11},{10,... | collective-permute-start | bytes 393224 | tf_op jit(solution)/shard_map/ppermute | solution.py:374
  87.1 3.3 %collective-permute-start.34 = (bf16[128,512]{1,0:T(8,128)(2,1)S(1)}, bf16[128,512]{1,0:T(8,128)(2,1)S(1)}, u32[]{:S(2)}, u32[]{:S(2)}) collective-permute-start(bf16[128,512]{1,0:T(8,128)(2,1)S(1)} %get-tuple-element.91), channel_id=1, source_target_pairs={{0,2},{1,3},{2,0},{3,1},{4,6},{5,7},{6,4},{7,5},{8,10},{9,11},{10,... | collective-permute-start | bytes 393224 | tf_op jit(solution)/shard_map/ppermute | solution.py:374
  90.8 4.2 %collective-permute-done.29.refs_2_ = bf16[128,512]{1,0:T(8,128)(2,1)S(1)} collective-permute-done((bf16[128,512]{1,0:T(8,128)(2,1)S(1)}, bf16[128,512]{1,0:T(8,128)(2,1)S(1)}, u32[]{:S(2)}, u32[]{:S(2)}) %collective-permute-start.29) | collective-permute-done | bytes 131104 | tf_op jit(solution)/shard_map/ppermute | solution.py:374
  95.2 9.8 %collective-permute-done.34.refs_2_ = bf16[128,512]{1,0:T(8,128)(2,1)S(1)} collective-permute-done((bf16[128,512]{1,0:T(8,128)(2,1)S(1)}, bf16[128,512]{1,0:T(8,128)(2,1)S(1)}, u32[]{:S(2)}, u32[]{:S(2)}) %collective-permute-start.34) | collective-permute-done | bytes 131104 | tf_op jit(solution)/shard_map/ppermute | solution.py:374
  105.0 1.4 %mix_keep.1 = bf16[128,1024]{1,0:T(8,128)(2,1)} custom-call(s32[3]{0:T(128)S(1)} %copy-done.5, f32[1]{0:T(128)S(6)} %tanh.3.gate, bf16[128,512]{1,0:T(8,128)(2,1)S(1)} %copy-done.4, bf16[128,512]{1,0:T(8,128)(2,1)S(1)} %collective-permute-done.31.back, bf16[128,512]{1,0:T(8,128)(2,1)S(1)} %get-tuple-element.89.refs_0_, ...), custom_call_target="tpu_custom_call" | custom-call | flops 1048576 | bytes 1048576 | tf_op jit(solution)/shard_map/mix_keep/pallas_call | solution.py:122
  (93 shorter events, 17.1 us)
Async XLA Ops:
  0.0 16.1 %collective-permute-start.6 = (bf16[512,2048]{1,0:T(8,128)(2,1)}, bf16[512,2048]{1,0:T(8,128)(2,1)}, u32[]{:S(2)}, u32[]{:S(2)}) collective-permute-start(bf16[512,2048]{1,0:T(8,128)(2,1)} %kv_own.1), channel_id=1, source_target_pairs={{0,4},{4,0},{8,12},{12,8},{16,20},{20,16},{24,28},{28,24},{1,5},{5... | collective-permute-start | bytes 6291464 | tf_op jit(solution)/shard_map/ppermute | solution.py:362
  5.3 6.8 %collective-permute-start.2 = (bf16[16,1024]{1,0:T(8,128)(2,1)}, bf16[16,1024]{1,0:T(8,128)(2,1)S(1)}, u32[]{:S(2)}, u32[]{:S(2)}) collective-permute-start(bf16[16,1024]{1,0:T(8,128)(2,1)} %get-tuple-element.53), channel_id=1, source_target_pairs={{0,8},{4,12},{8,0},{12,4},{16,24},{20,28},{24,16},{28,20},{1,9},{5... | collective-permute-start | bytes 98312 | tf_op jit(solution)/shard_map/ppermute | solution.py:365
  7.9 5.8 %collective-permute-start.3 = (bf16[16,1024]{1,0:T(8,128)(2,1)}, bf16[16,1024]{1,0:T(8,128)(2,1)S(1)}, u32[]{:S(2)}, u32[]{:S(2)}) collective-permute-start(bf16[16,1024]{1,0:T(8,128)(2,1)} %get-tuple-element.54), channel_id=1, source_target_pairs={{0,16},{4,20},{8,24},{12,28},{16,0},{20,4},{24,8},{28,12},{1,17},{... | collective-permute-start | bytes 98312 | tf_op jit(solution)/shard_map/ppermute | solution.py:365
  9.4 5.4 %collective-permute-start.4 = (bf16[16,1024]{1,0:T(8,128)(2,1)}, bf16[16,1024]{1,0:T(8,128)(2,1)S(1)}, u32[]{:S(2)}, u32[]{:S(2)}) collective-permute-start(bf16[16,1024]{1,0:T(8,128)(2,1)} %get-tuple-element.55), channel_id=1, source_target_pairs={{0,24},{4,28},{8,16},{12,20},{16,8},{20,12},{24,0},{28,4},{1,25},{... | collective-permute-start | bytes 98312 | tf_op jit(solution)/shard_map/ppermute | solution.py:365
  9.4 15.6 %collective-permute-start.10 = (bf16[512,512]{1,0:T(8,128)(2,1)}, bf16[512,512]{1,0:T(8,128)(2,1)S(1)}, u32[]{:S(2)}, u32[]{:S(2)}) collective-permute-start(bf16[512,512]{1,0:T(8,128)(2,1)} %get-tuple-element.60.q_keep), channel_id=1, source_target_pairs={{0,8},{4,12},{8,0},{12,4},{16,24},{20,28},{24,16},{28,20},{1,9},{5... | collective-permute-start | bytes 1572872 | tf_op jit(solution)/shard_map/ppermute | solution.py:365
  12.1 15.5 %collective-permute-start.11 = (bf16[128,2048]{1,0:T(8,128)(2,1)}, bf16[128,2048]{1,0:T(8,128)(2,1)S(1)}, u32[]{:S(2)}, u32[]{:S(2)}) collective-permute-start(bf16[128,2048]{1,0:T(8,128)(2,1)} %get-tuple-element.61), channel_id=1, source_target_pairs={{0,16},{4,20},{8,24},{12,28},{16,0},{20,4},{24,8},{28,12},{1,17},{... | collective-permute-start | bytes 1572872 | tf_op jit(solution)/shard_map/ppermute | solution.py:365
  13.7 13.8 %collective-permute-start.13 = (bf16[512,512]{1,0:T(8,128)(2,1)}, bf16[512,512]{1,0:T(8,128)(2,1)S(1)}, u32[]{:S(2)}, u32[]{:S(2)}) collective-permute-start(bf16[512,512]{1,0:T(8,128)(2,1)} %get-tuple-element.68), channel_id=1, source_target_pairs={{0,4},{4,0},{8,12},{12,8},{16,20},{20,16},{24,28},{28,24},{1,5},{5... | collective-permute-start | bytes 1572872 | tf_op jit(solution)/shard_map/ppermute | solution.py:362
  18.7 9.4 %collective-permute-start.7 = (f32[32,1024]{1,0:T(8,128)S(1)}, f32[32,1024]{1,0:T(8,128)S(1)}, u32[]{:S(2)}, u32[]{:S(2)}) collective-permute-start(f32[32,1024]{1,0:T(8,128)S(1)} %get-tuple-element.57), channel_id=1, source_target_pairs={{0,8},{4,12},{8,0},{12,4},{16,24},{20,28},{24,16},{28,20},{1,9},{5... | collective-permute-start | bytes 393224 | tf_op jit(solution)/shard_map/ppermute | solution.py:365
  19.1 12.3 %collective-permute-start.8 = (f32[32,1024]{1,0:T(8,128)S(1)}, f32[32,1024]{1,0:T(8,128)S(1)}, u32[]{:S(2)}, u32[]{:S(2)}) collective-permute-start(f32[32,1024]{1,0:T(8,128)S(1)} %get-tuple-element.58), channel_id=1, source_target_pairs={{0,16},{4,20},{8,24},{12,28},{16,0},{20,4},{24,8},{28,12},{1,17},{... | collective-permute-start | bytes 393224 | tf_op jit(solution)/shard_map/ppermute | solution.py:365
  25.1 6.4 %collective-permute-start.9 = (f32[32,1024]{1,0:T(8,128)S(1)}, f32[32,1024]{1,0:T(8,128)S(1)}, u32[]{:S(2)}, u32[]{:S(2)}) collective-permute-start(f32[32,1024]{1,0:T(8,128)S(1)} %get-tuple-element.59), channel_id=1, source_target_pairs={{0,24},{4,28},{8,16},{12,20},{16,8},{20,12},{24,0},{28,4},{1,25},{... | collective-permute-start | bytes 393224 | tf_op jit(solution)/shard_map/ppermute | solution.py:365
  27.6 7.8 %collective-permute-start.1 = (bf16[128,2048]{1,0:T(8,128)(2,1)S(1)}, bf16[128,2048]{1,0:T(8,128)(2,1)S(1)}, u32[]{:S(2)}, u32[]{:S(2)}) collective-permute-start(bf16[128,2048]{1,0:T(8,128)(2,1)S(1)} %copy-done.2), channel_id=1, source_target_pairs={{0,4},{4,0},{8,12},{12,8},{16,20},{20,16},{24,28},{28,24},{1,5},{5... | collective-permute-start | bytes 1572872 | tf_op jit(solution)/shard_map/ppermute | solution.py:362
  28.1 14.2 %collective-permute-start.14 = (bf16[512,512]{1,0:T(8,128)(2,1)S(1)}, bf16[512,512]{1,0:T(8,128)(2,1)S(1)}, u32[]{:S(2)}, u32[]{:S(2)}) collective-permute-start(bf16[512,512]{1,0:T(8,128)(2,1)S(1)} %collective-permute-done.13.q_other), channel_id=1, source_target_pairs={{0,8},{4,12},{8,0},{12,4},{16,24},{20,28},{24,16},{28,20},{1,9},{5... | collective-permute-start | bytes 1572872 | tf_op jit(solution)/shard_map/ppermute | solution.py:365
  31.4 13.4 %collective-permute-start.17 = (bf16[128,2048]{1,0:T(8,128)(2,1)S(1)}, bf16[128,2048]{1,0:T(8,128)(2,1)S(1)}, u32[]{:S(2)}, u32[]{:S(2)}) collective-permute-start(bf16[128,2048]{1,0:T(8,128)(2,1)S(1)} %collective-permute-done.11.own), channel_id=1, source_target_pairs={{0,4},{4,0},{8,12},{12,8},{16,20},{20,16},{24,28},{28,24},{1,5},{5... | collective-permute-start | bytes 1572872 | tf_op jit(solution)/shard_map/ppermute | solution.py:362
  32.1 15.0 %collective-permute-start.16 = (bf16[512,512]{1,0:T(8,128)(2,1)S(1)}, bf16[512,512]{1,0:T(8,128)(2,1)S(1)}, u32[]{:S(2)}, u32[]{:S(2)}) collective-permute-start(bf16[512,512]{1,0:T(8,128)(2,1)S(1)} %get-tuple-element.74), channel_id=1, source_target_pairs={{0,16},{4,20},{8,24},{12,28},{16,0},{20,4},{24,8},{28,12},{1,17},{... | collective-permute-start | bytes 1572872 | tf_op jit(solution)/shard_map/ppermute | solution.py:365
  42.3 4.8 %collective-permute-start.15 = (bf16[64,256]{1,0:T(8,128)(2,1)S(1)}, bf16[64,256]{1,0:T(8,128)(2,1)S(1)}, u32[]{:S(2)}, u32[]{:S(2)}) collective-permute-start(bf16[64,256]{1,0:T(8,128)(2,1)S(1)} %kv_turn.1), channel_id=1, source_target_pairs={{0,2},{1,3},{2,0},{3,1},{4,6},{5,7},{6,4},{7,5},{8,10},{9,11},{10,... | collective-permute-start | bytes 98312 | tf_op jit(solution)/shard_map/ppermute | solution.py:374
  47.1 12.1 %collective-permute-start.18 = (bf16[256,512]{1,0:T(8,128)(2,1)S(1)}, bf16[256,512]{1,0:T(8,128)(2,1)S(1)}, u32[]{:S(2)}, u32[]{:S(2)}) collective-permute-start(bf16[256,512]{1,0:T(8,128)(2,1)S(1)} %q_late.3), channel_id=1, source_target_pairs={{0,16},{4,20},{8,24},{12,28},{16,0},{20,4},{24,8},{28,12},{1,17},{... | collective-permute-start | bytes 786440 | tf_op jit(solution)/shard_map/ppermute | solution.py:365
  50.1 4.9 %collective-permute-start.19 = (bf16[128,256]{1,0:T(8,128)(2,1)S(1)}, bf16[128,256]{1,0:T(8,128)(2,1)S(1)}, u32[]{:S(2)}, u32[]{:S(2)}) collective-permute-start(bf16[128,256]{1,0:T(8,128)(2,1)S(1)} %kv_join.1.refs_0_), channel_id=1, source_target_pairs={{0,8},{4,12},{8,0},{12,4},{16,24},{20,28},{24,16},{28,20},{1,9},{5... | collective-permute-start | bytes 196616 | tf_op jit(solution)/shard_map/ppermute | solution.py:365
  51.0 8.2 %collective-permute-start.20 = (bf16[128,256]{1,0:T(8,128)(2,1)S(1)}, bf16[128,256]{1,0:T(8,128)(2,1)S(1)}, u32[]{:S(2)}, u32[]{:S(2)}) collective-permute-start(bf16[128,256]{1,0:T(8,128)(2,1)S(1)} %kv_join.1.refs_0_), channel_id=1, source_target_pairs={{0,16},{4,20},{8,24},{12,28},{16,0},{20,4},{24,8},{28,12},{1,17},{... | collective-permute-start | bytes 196616 | tf_op jit(solution)/shard_map/ppermute | solution.py:365
  51.5 7.7 %collective-permute-start.21 = (bf16[128,256]{1,0:T(8,128)(2,1)S(1)}, bf16[128,256]{1,0:T(8,128)(2,1)S(1)}, u32[]{:S(2)}, u32[]{:S(2)}) collective-permute-start(bf16[128,256]{1,0:T(8,128)(2,1)S(1)} %kv_join.1.refs_0_), channel_id=1, source_target_pairs={{0,24},{4,28},{8,16},{12,20},{16,8},{20,12},{24,0},{28,4},{1,25},{... | collective-permute-start | bytes 196616 | tf_op jit(solution)/shard_map/ppermute | solution.py:365
  53.7 15.1 %collective-permute-start.24 = (bf16[512,512]{1,0:T(8,128)(2,1)S(1)}, bf16[512,512]{1,0:T(8,128)(2,1)S(1)}, u32[]{:S(2)}, u32[]{:S(2)}) collective-permute-start(bf16[512,512]{1,0:T(8,128)(2,1)S(1)} %get-tuple-element.80), channel_id=1, source_target_pairs={{0,16},{4,20},{8,24},{12,28},{16,0},{20,4},{24,8},{28,12},{1,17},{... | collective-permute-start | bytes 1572872 | tf_op jit(solution)/shard_map/ppermute | solution.py:365
  61.5 6.4 %collective-permute-start.25 = (bf16[256,512]{1,0:T(8,128)(2,1)S(1)}, bf16[256,512]{1,0:T(8,128)(2,1)S(1)}, u32[]{:S(2)}, u32[]{:S(2)}) collective-permute-start(bf16[256,512]{1,0:T(8,128)(2,1)S(1)} %attend.1.near), channel_id=1, source_target_pairs={{0,8},{4,12},{8,0},{12,4},{16,24},{20,28},{24,16},{28,20},{1,9},{5... | collective-permute-start | bytes 786440 | tf_op jit(solution)/shard_map/ppermute | solution.py:365
  67.9 4.9 %collective-permute-start.23 = (bf16[256,512]{1,0:T(8,128)(2,1)S(1)}, bf16[256,512]{1,0:T(8,128)(2,1)S(1)}, u32[]{:S(2)}, u32[]{:S(2)}) collective-permute-start(bf16[256,512]{1,0:T(8,128)(2,1)S(1)} %attend.1.near), channel_id=1, source_target_pairs={{0,4},{4,0},{8,12},{12,8},{16,20},{20,16},{24,28},{28,24},{1,5},{5... | collective-permute-start | bytes 786440 | tf_op jit(solution)/shard_map/ppermute | solution.py:362
  70.7 9.2 %collective-permute-start.27 = (bf16[128,1024]{1,0:T(8,128)(2,1)S(1)}, bf16[128,1024]{1,0:T(8,128)(2,1)S(1)}, u32[]{:S(2)}, u32[]{:S(2)}) collective-permute-start(bf16[128,1024]{1,0:T(8,128)(2,1)S(1)} %get-tuple-element.82), channel_id=1, source_target_pairs={{0,8},{4,12},{8,0},{12,4},{16,24},{20,28},{24,16},{28,20},{1,9},{5... | collective-permute-start | bytes 786440 | tf_op jit(solution)/shard_map/ppermute | solution.py:365
  72.1 13.7 %collective-permute-start.32 = (bf16[128,1024]{1,0:T(8,128)(2,1)S(1)}, bf16[128,1024]{1,0:T(8,128)(2,1)S(1)}, u32[]{:S(2)}, u32[]{:S(2)}) collective-permute-start(bf16[128,1024]{1,0:T(8,128)(2,1)S(1)} %get-tuple-element.88), channel_id=1, source_target_pairs={{0,8},{4,12},{8,0},{12,4},{16,24},{20,28},{24,16},{28,20},{1,9},{5... | collective-permute-start | bytes 786440 | tf_op jit(solution)/shard_map/ppermute | solution.py:365
  72.8 14.3 %collective-permute-start = (bf16[128,512]{1,0:T(8,128)(2,1)S(1)}, bf16[128,512]{1,0:T(8,128)(2,1)S(1)}, u32[]{:S(2)}, u32[]{:S(2)}) collective-permute-start(bf16[128,512]{1,0:T(8,128)(2,1)S(1)} %copy-done.11), channel_id=1, source_target_pairs={{0,4},{4,0},{8,12},{12,8},{16,20},{20,16},{24,28},{28,24},{1,5},{5... | collective-permute-start | bytes 393224 | tf_op jit(solution)/shard_map/ppermute | solution.py:362
  80.6 9.8 %collective-permute-start.28 = (bf16[128,512]{1,0:T(8,128)(2,1)S(1)}, bf16[128,512]{1,0:T(8,128)(2,1)S(1)}, u32[]{:S(2)}, u32[]{:S(2)}) collective-permute-start(bf16[128,512]{1,0:T(8,128)(2,1)S(1)} %get-tuple-element.84), channel_id=1, source_target_pairs={{0,1},{1,0},{2,3},{3,2},{4,5},{5,4},{6,7},{7,6},{8,9},{9,8},{10,11... | collective-permute-start | bytes 393224 | tf_op jit(solution)/shard_map/ppermute | solution.py:374
  82.2 12.8 %collective-permute-start.29 = (bf16[128,512]{1,0:T(8,128)(2,1)S(1)}, bf16[128,512]{1,0:T(8,128)(2,1)S(1)}, u32[]{:S(2)}, u32[]{:S(2)}) collective-permute-start(bf16[128,512]{1,0:T(8,128)(2,1)S(1)} %get-tuple-element.85), channel_id=1, source_target_pairs={{0,2},{1,3},{2,0},{3,1},{4,6},{5,7},{6,4},{7,5},{8,10},{9,11},{10,... | collective-permute-start | bytes 393224 | tf_op jit(solution)/shard_map/ppermute | solution.py:374
  84.6 10.4 %collective-permute-start.30 = (bf16[128,512]{1,0:T(8,128)(2,1)S(1)}, bf16[128,512]{1,0:T(8,128)(2,1)S(1)}, u32[]{:S(2)}, u32[]{:S(2)}) collective-permute-start(bf16[128,512]{1,0:T(8,128)(2,1)S(1)} %get-tuple-element.86), channel_id=1, source_target_pairs={{0,3},{1,2},{2,1},{3,0},{4,7},{5,6},{6,5},{7,4},{8,11},{9,10},{10,... | collective-permute-start | bytes 393224 | tf_op jit(solution)/shard_map/ppermute | solution.py:374
  86.4 8.8 %collective-permute-start.33 = (bf16[128,512]{1,0:T(8,128)(2,1)S(1)}, bf16[128,512]{1,0:T(8,128)(2,1)S(1)}, u32[]{:S(2)}, u32[]{:S(2)}) collective-permute-start(bf16[128,512]{1,0:T(8,128)(2,1)S(1)} %get-tuple-element.90), channel_id=1, source_target_pairs={{0,1},{1,0},{2,3},{3,2},{4,5},{5,4},{6,7},{7,6},{8,9},{9,8},{10,11... | collective-permute-start | bytes 393224 | tf_op jit(solution)/shard_map/ppermute | solution.py:374
  87.1 17.9 %collective-permute-start.34 = (bf16[128,512]{1,0:T(8,128)(2,1)S(1)}, bf16[128,512]{1,0:T(8,128)(2,1)S(1)}, u32[]{:S(2)}, u32[]{:S(2)}) collective-permute-start(bf16[128,512]{1,0:T(8,128)(2,1)S(1)} %get-tuple-element.91), channel_id=1, source_target_pairs={{0,2},{1,3},{2,0},{3,1},{4,6},{5,7},{6,4},{7,5},{8,10},{9,11},{10,... | collective-permute-start | bytes 393224 | tf_op jit(solution)/shard_map/ppermute | solution.py:374
  90.4 14.6 %collective-permute-start.35 = (bf16[128,512]{1,0:T(8,128)(2,1)S(1)}, bf16[128,512]{1,0:T(8,128)(2,1)S(1)}, u32[]{:S(2)}, u32[]{:S(2)}) collective-permute-start(bf16[128,512]{1,0:T(8,128)(2,1)S(1)} %get-tuple-element.92), channel_id=1, source_target_pairs={{0,3},{1,2},{2,1},{3,0},{4,7},{5,6},{6,5},{7,4},{8,11},{9,10},{10,... | collective-permute-start | bytes 393224 | tf_op jit(solution)/shard_map/ppermute | solution.py:374
  95.1 9.9 %collective-permute-start.31 = (bf16[128,512]{1,0:T(8,128)(2,1)S(1)}, bf16[128,512]{1,0:T(8,128)(2,1)S(1)}, u32[]{:S(2)}, u32[]{:S(2)}) collective-permute-start(bf16[128,512]{1,0:T(8,128)(2,1)S(1)} %mix_give.1), channel_id=1, source_target_pairs={{0,4},{4,0},{8,12},{12,8},{16,20},{20,16},{24,28},{28,24},{1,5},{5... | collective-permute-start | bytes 393224 | tf_op jit(solution)/shard_map/ppermute | solution.py:362
  (16 other events, 201.1 us)

commit v3 on v2

--- a/solution.py
+++ b/solution.py
@@ -441,7 +441,7 @@
         )[0]
         for pair in blocks
     ]
-    kv_z, q_corner = lax.optimization_barrier((across(give, 1), q_corner))
+    kv_z = across(give, 1)
     o_early, _ = lax.optimization_barrier((o_weight[:half], here))
     o_early = along_y(o_early)
     q_far, q_first = [
@@ -450,7 +450,7 @@
             (where, *blocks[k], q_side, q_corner, early[k]),
             [SMEM] + [VMEM] * 5,
             [shape(2 * tokens, half, kind)],
-            flops=4 * tokens * part * half,
+            flops=40 * tokens * part * half,
             size=2 * 2**20,
             name="q_late",
         )[0]

time: 107 us -> 106 us (level)
  transfers between devices with their start and end apart: 36 -> 36, of which waited for: 15 -> 14; matrix products, arithmetic and copies ran while one was open for 2% -> 2% of each run, Pallas kernels for 16% -> 17%
where the time goes in v3:
time: 106 us
  waiting for transfers between devices  47.2 us (45%)
  starting transfers between devices  36.7 us (35%)
  Pallas kernels  18.9 us (18%)
  other arithmetic  1.07 us (1%)
    ppermute x18, waiting for transfers between devices, peer(): return lax.ppermute(x, 'ctx', [(k, k ^ 2 * s) for k in range(ctx_count)])  30.5 us
    ppermute x18, starting transfers between devices, peer(): return lax.ppermute(x, 'ctx', [(k, k ^ 2 * s) for k in range(ctx_count)])  22 us
    pallas_call x16, Pallas kernels, call(): pl.pallas_call(kernel, out_shape=outs, in_specs=specs, out_specs=[VMEM] *...  18.9 us
    ppermute x8, waiting for transfers between devices, across(): return lax.ppermute(x, 'img', [(k, k ^ t) for k in range(CHIPS)])  15.2 us
    ppermute x8, starting transfers between devices, across(): return lax.ppermute(x, 'img', [(k, k ^ t) for k in range(CHIPS)])  13.1 us
  transfers between devices with their start and end apart: 36, of which 14 were waited for; matrix products, arithmetic and copies ran while one was open for 2% of the time, Pallas kernels for 17%

profile of v3, /device:TPU:0, one launch (start us, length us, event | category | flops | bytes accessed | tf_op | source)
XLA Modules:
  0.0 105.8 jit_solution(5697898749203882093)
XLA Ops:
  1.1 4.2 %start.1 = (bf16[16,1024]{1,0:T(8,128)(2,1)}, bf16[16,1024]{1,0:T(8,128)(2,1)}, bf16[16,1024]{1,0:T(8,128)(2,1)}, bf16[16,1024]{1,0:T(8,128)(2,1)}, bf16[128,204...) custom-call(s32[3]{0:T(128)} %pad_add_fusion.1.where, ...), custom_call_target="tpu_custom_call" | custom-call | flops 4194304 | bytes 4194304 | tf_op jit(solution)/shard_map/start/pallas_call | solution.py:122
  5.3 2.6 %collective-permute-start.2 = (bf16[16,1024]{1,0:T(8,128)(2,1)}, bf16[16,1024]{1,0:T(8,128)(2,1)S(1)}, u32[]{:S(2)}, u32[]{:S(2)}) collective-permute-start(bf16[16,1024]{1,0:T(8,128)(2,1)} %get-tuple-element.51), channel_id=1, source_target_pairs={{0,8},{4,12},{8,0},{12,4},{16,24},{20,28},{24,16},{28,20},{1,9},{5... | collective-permute-start | bytes 98312 | tf_op jit(solution)/shard_map/ppermute | solution.py:365
  7.9 1.5 %collective-permute-start.3 = (bf16[16,1024]{1,0:T(8,128)(2,1)}, bf16[16,1024]{1,0:T(8,128)(2,1)S(1)}, u32[]{:S(2)}, u32[]{:S(2)}) collective-permute-start(bf16[16,1024]{1,0:T(8,128)(2,1)} %get-tuple-element.52), channel_id=1, source_target_pairs={{0,16},{4,20},{8,24},{12,28},{16,0},{20,4},{24,8},{28,12},{1,17},{... | collective-permute-start | bytes 98312 | tf_op jit(solution)/shard_map/ppermute | solution.py:365
  9.4 1.9 %collective-permute-start.10 = (bf16[512,512]{1,0:T(8,128)(2,1)}, bf16[512,512]{1,0:T(8,128)(2,1)S(1)}, u32[]{:S(2)}, u32[]{:S(2)}) collective-permute-start(bf16[512,512]{1,0:T(8,128)(2,1)} %get-tuple-element.58.q_keep), channel_id=1, source_target_pairs={{0,8},{4,12},{8,0},{12,4},{16,24},{20,28},{24,16},{28,20},{1,9},{5... | collective-permute-start | bytes 1572872 | tf_op jit(solution)/shard_map/ppermute | solution.py:365
  12.1 1.5 %collective-permute-start.11 = (bf16[128,2048]{1,0:T(8,128)(2,1)}, bf16[128,2048]{1,0:T(8,128)(2,1)S(1)}, u32[]{:S(2)}, u32[]{:S(2)}) collective-permute-start(bf16[128,2048]{1,0:T(8,128)(2,1)} %get-tuple-element.59), channel_id=1, source_target_pairs={{0,16},{4,20},{8,24},{12,28},{16,0},{20,4},{24,8},{28,12},{1,17},{... | collective-permute-start | bytes 1572872 | tf_op jit(solution)/shard_map/ppermute | solution.py:365
  14.9 1.2 %collective-permute-done.5.vis_other = bf16[64,1024]{1,0:T(8,128)(2,1)S(1)} collective-permute-done((bf16[64,1024]{1,0:T(8,128)(2,1)S(1)}, bf16[64,1024]{1,0:T(8,128)(2,1)S(1)}, u32[]{:S(2)}, u32[]{:S(2)}) %collective-permute-start.5) | collective-permute-done | bytes 131104 | tf_op jit(solution)/shard_map/ppermute | solution.py:362
  16.1 2.6 %kv_shares.1 = (f32[32,1024]{1,0:T(8,128)S(1)}, f32[32,1024]{1,0:T(8,128)S(1)}, f32[32,1024]{1,0:T(8,128)S(1)}, f32[32,1024]{1,0:T(8,128)S(1)}) custom-call(s32[3]{0:T(128)S(1)} %copy-done.5, bf16[64,1024]{1,0:T(8,128)(2,1)S(1)} %constant_dynamic-update-slice_fusion.vis, bf16[64,1024]{1,0:T(8,128)(2,1)S(1)} %collective-permute-done.5.vis_other, ...), custom_call_target="tpu_custom_call" | custom-call | flops 536870912 | bytes 4194304 | tf_op jit(solution)/shard_map/kv_shares/pallas_call | solution.py:122
  19.3 5.7 %collective-permute-done.10.q_side = bf16[512,512]{1,0:T(8,128)(2,1)S(1)} collective-permute-done((bf16[512,512]{1,0:T(8,128)(2,1)}, bf16[512,512]{1,0:T(8,128)(2,1)S(1)}, u32[]{:S(2)}, u32[]{:S(2)}) %collective-permute-start.10) | collective-permute-done | bytes 524320 | tf_op jit(solution)/shard_map/ppermute | solution.py:365
  25.1 2.3 %collective-permute-start.9 = (f32[32,1024]{1,0:T(8,128)S(1)}, f32[32,1024]{1,0:T(8,128)S(1)}, u32[]{:S(2)}, u32[]{:S(2)}) collective-permute-start(f32[32,1024]{1,0:T(8,128)S(1)} %get-tuple-element.57), channel_id=1, source_target_pairs={{0,24},{4,28},{8,16},{12,20},{16,8},{20,12},{24,0},{28,4},{1,25},{... | collective-permute-start | bytes 393224 | tf_op jit(solution)/shard_map/ppermute | solution.py:365
  28.7 2.7 %collective-permute-done.8.refs_2_ = f32[32,1024]{1,0:T(8,128)S(1)} collective-permute-done((f32[32,1024]{1,0:T(8,128)S(1)}, f32[32,1024]{1,0:T(8,128)S(1)}, u32[]{:S(2)}, u32[]{:S(2)}) %collective-permute-start.8) | collective-permute-done | bytes 131104 | tf_op jit(solution)/shard_map/ppermute | solution.py:365
  32.1 1.4 %collective-permute-start.16 = (bf16[512,512]{1,0:T(8,128)(2,1)S(1)}, bf16[512,512]{1,0:T(8,128)(2,1)S(1)}, u32[]{:S(2)}, u32[]{:S(2)}) collective-permute-start(bf16[512,512]{1,0:T(8,128)(2,1)S(1)} %get-tuple-element.70), channel_id=1, source_target_pairs={{0,16},{4,20},{8,24},{12,28},{16,0},{20,4},{24,8},{28,12},{1,17},{... | collective-permute-start | bytes 1572872 | tf_op jit(solution)/shard_map/ppermute | solution.py:365
  33.6 1.6 %collective-permute-start.14 = (bf16[64,256]{1,0:T(8,128)(2,1)S(1)}, bf16[64,256]{1,0:T(8,128)(2,1)S(1)}, u32[]{:S(2)}, u32[]{:S(2)}) collective-permute-start(bf16[64,256]{1,0:T(8,128)(2,1)S(1)} %get-tuple-element.68), channel_id=1, source_target_pairs={{0,1},{1,0},{2,3},{3,2},{4,5},{5,4},{6,7},{7,6},{8,9},{9,8},{10,11... | collective-permute-start | bytes 98312 | tf_op jit(solution)/shard_map/ppermute | solution.py:374
  36.4 1.2 %collective-permute-done.14.landed = bf16[64,256]{1,0:T(8,128)(2,1)S(1)} collective-permute-done((bf16[64,256]{1,0:T(8,128)(2,1)S(1)}, bf16[64,256]{1,0:T(8,128)(2,1)S(1)}, u32[]{:S(2)}, u32[]{:S(2)}) %collective-permute-start.14) | collective-permute-done | bytes 32800 | tf_op jit(solution)/shard_map/ppermute | solution.py:374
  37.6 2.6 %collective-permute-start.15 = (bf16[64,256]{1,0:T(8,128)(2,1)S(1)}, bf16[64,256]{1,0:T(8,128)(2,1)S(1)}, u32[]{:S(2)}, u32[]{:S(2)}) collective-permute-start(bf16[64,256]{1,0:T(8,128)(2,1)S(1)} %kv_turn.1), channel_id=1, source_target_pairs={{0,2},{1,3},{2,0},{3,1},{4,6},{5,7},{6,4},{7,5},{8,10},{9,11},{10,... | collective-permute-start | bytes 98312 | tf_op jit(solution)/shard_map/ppermute | solution.py:374
  43.3 3.3 %collective-permute-done.16.o_early = bf16[512,512]{1,0:T(8,128)(2,1)S(1)} collective-permute-done((bf16[512,512]{1,0:T(8,128)(2,1)S(1)}, bf16[512,512]{1,0:T(8,128)(2,1)S(1)}, u32[]{:S(2)}, u32[]{:S(2)}) %collective-permute-start.16) | collective-permute-done | bytes 524320 | tf_op jit(solution)/shard_map/ppermute | solution.py:365
  46.5 1.3 %collective-permute-start.18 = (bf16[256,512]{1,0:T(8,128)(2,1)S(1)}, bf16[256,512]{1,0:T(8,128)(2,1)S(1)}, u32[]{:S(2)}, u32[]{:S(2)}) collective-permute-start(bf16[256,512]{1,0:T(8,128)(2,1)S(1)} %q_late.3), channel_id=1, source_target_pairs={{0,16},{4,20},{8,24},{12,28},{16,0},{20,4},{24,8},{28,12},{1,17},{... | collective-permute-start | bytes 786440 | tf_op jit(solution)/shard_map/ppermute | solution.py:365
  48.8 2.1 %collective-permute-start.19 = (bf16[128,256]{1,0:T(8,128)(2,1)S(1)}, bf16[128,256]{1,0:T(8,128)(2,1)S(1)}, u32[]{:S(2)}, u32[]{:S(2)}) collective-permute-start(bf16[128,256]{1,0:T(8,128)(2,1)S(1)} %kv_join.1.refs_0_), channel_id=1, source_target_pairs={{0,8},{4,12},{8,0},{12,4},{16,24},{20,28},{24,16},{28,20},{1,9},{5... | collective-permute-start | bytes 196616 | tf_op jit(solution)/shard_map/ppermute | solution.py:365
  51.3 1.3 %collective-permute-start.21 = (bf16[128,256]{1,0:T(8,128)(2,1)S(1)}, bf16[128,256]{1,0:T(8,128)(2,1)S(1)}, u32[]{:S(2)}, u32[]{:S(2)}) collective-permute-start(bf16[128,256]{1,0:T(8,128)(2,1)S(1)} %kv_join.1.refs_0_), channel_id=1, source_target_pairs={{0,24},{4,28},{8,16},{12,20},{16,8},{20,12},{24,0},{28,4},{1,25},{... | collective-permute-start | bytes 196616 | tf_op jit(solution)/shard_map/ppermute | solution.py:365
  53.2 5.3 %collective-permute-done.20.refs_2_ = bf16[128,256]{1,0:T(8,128)(2,1)S(1)} collective-permute-done((bf16[128,256]{1,0:T(8,128)(2,1)S(1)}, bf16[128,256]{1,0:T(8,128)(2,1)S(1)}, u32[]{:S(2)}, u32[]{:S(2)}) %collective-permute-start.20) | collective-permute-done | bytes 65568 | tf_op jit(solution)/shard_map/ppermute | solution.py:365
  58.6 2.3 %attend.1.near = bf16[256,512]{1,0:T(8,128)(2,1)S(1)} custom-call(f32[1,128]{1,0:T(1,128)S(1)} %bitcast.8, f32[256,512]{1,0:T(8,128)S(1)} %q_late.2.first, bf16[256,512]{1,0:T(8,128)(2,1)S(1)} %collective-permute-done.18.landed, bf16[128,256]{1,0:T(8,128)(2,1)S(1)} %kv_join.1.refs_0_, bf16[128,256]{1,0:T(8,128)(2,1)S(1)} %collective-permute-done.19.refs_1_, ...), custom_call_target="tpu_custom_call" | custom-call | flops 268435456 | bytes 2097152 | tf_op jit(solution)/shard_map/attend/pallas_call | solution.py:122
  60.9 1.7 %collective-permute-start.25 = (bf16[256,512]{1,0:T(8,128)(2,1)S(1)}, bf16[256,512]{1,0:T(8,128)(2,1)S(1)}, u32[]{:S(2)}, u32[]{:S(2)}) collective-permute-start(bf16[256,512]{1,0:T(8,128)(2,1)S(1)} %attend.1.near), channel_id=1, source_target_pairs={{0,8},{4,12},{8,0},{12,4},{16,24},{20,28},{24,16},{28,20},{1,9},{5... | collective-permute-start | bytes 786440 | tf_op jit(solution)/shard_map/ppermute | solution.py:365
  62.6 4.8 %collective-permute-done.25.near = bf16[256,512]{1,0:T(8,128)(2,1)S(1)} collective-permute-done((bf16[256,512]{1,0:T(8,128)(2,1)S(1)}, bf16[256,512]{1,0:T(8,128)(2,1)S(1)}, u32[]{:S(2)}, u32[]{:S(2)}) %collective-permute-start.25) | collective-permute-done | bytes 262176 | tf_op jit(solution)/shard_map/ppermute | solution.py:365
  68.9 1.3 %o_share.3 = (bf16[128,1024]{1,0:T(8,128)(2,1)S(1)}, bf16[128,1024]{1,0:T(8,128)(2,1)S(1)}) custom-call(s32[3]{0:T(128)S(1)} %copy-done.5, bf16[256,512]{1,0:T(8,128)(2,1)S(1)} %collective-permute-done.25.near, bf16[256,512]{1,0:T(8,128)(2,1)S(1)} %collective-permute-done.26.far, bf16[1024,512]{1,0:T(8,128)(2,1)S(1)} %copy-done, ...), custom_call_target="tpu_custom_call" | custom-call | flops 536870912 | bytes 2097152 | tf_op jit(solution)/shard_map/o_share/pallas_call | solution.py:122
  70.1 1.7 %collective-permute-start.27 = (bf16[128,1024]{1,0:T(8,128)(2,1)S(1)}, bf16[128,1024]{1,0:T(8,128)(2,1)S(1)}, u32[]{:S(2)}, u32[]{:S(2)}) collective-permute-start(bf16[128,1024]{1,0:T(8,128)(2,1)S(1)} %get-tuple-element.78), channel_id=1, source_target_pairs={{0,8},{4,12},{8,0},{12,4},{16,24},{20,28},{24,16},{28,20},{1,9},{5... | collective-permute-start | bytes 786440 | tf_op jit(solution)/shard_map/ppermute | solution.py:365
  72.2 1.3 %o_share.2 = (bf16[128,1024]{1,0:T(8,128)(2,1)S(1)}, bf16[128,1024]{1,0:T(8,128)(2,1)S(1)}) custom-call(s32[3]{0:T(128)S(1)} %copy-done.5, bf16[256,512]{1,0:T(8,128)(2,1)S(1)} %attend.1.near, bf16[256,512]{1,0:T(8,128)(2,1)S(1)} %collective-permute-done.23.far, bf16[1024,512]{1,0:T(8,128)(2,1)S(1)} %copy-done, ...), custom_call_target="tpu_custom_call" | custom-call | flops 536870912 | bytes 2097152 | tf_op jit(solution)/shard_map/o_share/pallas_call | solution.py:122
  73.5 5.8 %collective-permute-done.27.landed = bf16[128,1024]{1,0:T(8,128)(2,1)S(1)} collective-permute-done((bf16[128,1024]{1,0:T(8,128)(2,1)S(1)}, bf16[128,1024]{1,0:T(8,128)(2,1)S(1)}, u32[]{:S(2)}, u32[]{:S(2)}) %collective-permute-start.27) | collective-permute-done | bytes 262176 | tf_op jit(solution)/shard_map/ppermute | solution.py:365
  80.0 1.6 %collective-permute-start.28 = (bf16[128,512]{1,0:T(8,128)(2,1)S(1)}, bf16[128,512]{1,0:T(8,128)(2,1)S(1)}, u32[]{:S(2)}, u32[]{:S(2)}) collective-permute-start(bf16[128,512]{1,0:T(8,128)(2,1)S(1)} %get-tuple-element.80), channel_id=1, source_target_pairs={{0,1},{1,0},{2,3},{3,2},{4,5},{5,4},{6,7},{7,6},{8,9},{9,8},{10,11... | collective-permute-start | bytes 393224 | tf_op jit(solution)/shard_map/ppermute | solution.py:374
  81.6 2.6 %collective-permute-start.29 = (bf16[128,512]{1,0:T(8,128)(2,1)S(1)}, bf16[128,512]{1,0:T(8,128)(2,1)S(1)}, u32[]{:S(2)}, u32[]{:S(2)}) collective-permute-start(bf16[128,512]{1,0:T(8,128)(2,1)S(1)} %get-tuple-element.81), channel_id=1, source_target_pairs={{0,2},{1,3},{2,0},{3,1},{4,6},{5,7},{6,4},{7,5},{8,10},{9,11},{10,... | collective-permute-start | bytes 393224 | tf_op jit(solution)/shard_map/ppermute | solution.py:374
  86.5 3.5 %collective-permute-start.34 = (bf16[128,512]{1,0:T(8,128)(2,1)S(1)}, bf16[128,512]{1,0:T(8,128)(2,1)S(1)}, u32[]{:S(2)}, u32[]{:S(2)}) collective-permute-start(bf16[128,512]{1,0:T(8,128)(2,1)S(1)} %get-tuple-element.87), channel_id=1, source_target_pairs={{0,2},{1,3},{2,0},{3,1},{4,6},{5,7},{6,4},{7,5},{8,10},{9,11},{10,... | collective-permute-start | bytes 393224 | tf_op jit(solution)/shard_map/ppermute | solution.py:374
  90.3 4.2 %collective-permute-done.29.refs_2_ = bf16[128,512]{1,0:T(8,128)(2,1)S(1)} collective-permute-done((bf16[128,512]{1,0:T(8,128)(2,1)S(1)}, bf16[128,512]{1,0:T(8,128)(2,1)S(1)}, u32[]{:S(2)}, u32[]{:S(2)}) %collective-permute-start.29) | collective-permute-done | bytes 131104 | tf_op jit(solution)/shard_map/ppermute | solution.py:374
  94.7 9.8 %collective-permute-done.34.refs_2_ = bf16[128,512]{1,0:T(8,128)(2,1)S(1)} collective-permute-done((bf16[128,512]{1,0:T(8,128)(2,1)S(1)}, bf16[128,512]{1,0:T(8,128)(2,1)S(1)}, u32[]{:S(2)}, u32[]{:S(2)}) %collective-permute-start.34) | collective-permute-done | bytes 131104 | tf_op jit(solution)/shard_map/ppermute | solution.py:374
  104.4 1.4 %mix_keep.1 = bf16[128,1024]{1,0:T(8,128)(2,1)} custom-call(s32[3]{0:T(128)S(1)} %copy-done.5, f32[1]{0:T(128)S(6)} %tanh.3.gate, bf16[128,512]{1,0:T(8,128)(2,1)S(1)} %copy-done.4, bf16[128,512]{1,0:T(8,128)(2,1)S(1)} %collective-permute-done.31.back, bf16[128,512]{1,0:T(8,128)(2,1)S(1)} %get-tuple-element.85.refs_0_, ...), custom_call_target="tpu_custom_call" | custom-call | flops 1048576 | bytes 1048576 | tf_op jit(solution)/shard_map/mix_keep/pallas_call | solution.py:122
  (93 shorter events, 16.7 us)
Async XLA Ops:
  0.0 16.1 %collective-permute-start.6 = (bf16[512,2048]{1,0:T(8,128)(2,1)}, bf16[512,2048]{1,0:T(8,128)(2,1)}, u32[]{:S(2)}, u32[]{:S(2)}) collective-permute-start(bf16[512,2048]{1,0:T(8,128)(2,1)} %kv_own.1), channel_id=1, source_target_pairs={{0,4},{4,0},{8,12},{12,8},{16,20},{20,16},{24,28},{28,24},{1,5},{5... | collective-permute-start | bytes 6291464 | tf_op jit(solution)/shard_map/ppermute | solution.py:362
  5.3 6.8 %collective-permute-start.2 = (bf16[16,1024]{1,0:T(8,128)(2,1)}, bf16[16,1024]{1,0:T(8,128)(2,1)S(1)}, u32[]{:S(2)}, u32[]{:S(2)}) collective-permute-start(bf16[16,1024]{1,0:T(8,128)(2,1)} %get-tuple-element.51), channel_id=1, source_target_pairs={{0,8},{4,12},{8,0},{12,4},{16,24},{20,28},{24,16},{28,20},{1,9},{5... | collective-permute-start | bytes 98312 | tf_op jit(solution)/shard_map/ppermute | solution.py:365
  7.9 5.8 %collective-permute-start.3 = (bf16[16,1024]{1,0:T(8,128)(2,1)}, bf16[16,1024]{1,0:T(8,128)(2,1)S(1)}, u32[]{:S(2)}, u32[]{:S(2)}) collective-permute-start(bf16[16,1024]{1,0:T(8,128)(2,1)} %get-tuple-element.52), channel_id=1, source_target_pairs={{0,16},{4,20},{8,24},{12,28},{16,0},{20,4},{24,8},{28,12},{1,17},{... | collective-permute-start | bytes 98312 | tf_op jit(solution)/shard_map/ppermute | solution.py:365
  9.4 5.4 %collective-permute-start.4 = (bf16[16,1024]{1,0:T(8,128)(2,1)}, bf16[16,1024]{1,0:T(8,128)(2,1)S(1)}, u32[]{:S(2)}, u32[]{:S(2)}) collective-permute-start(bf16[16,1024]{1,0:T(8,128)(2,1)} %get-tuple-element.53), channel_id=1, source_target_pairs={{0,24},{4,28},{8,16},{12,20},{16,8},{20,12},{24,0},{28,4},{1,25},{... | collective-permute-start | bytes 98312 | tf_op jit(solution)/shard_map/ppermute | solution.py:365
  9.4 15.6 %collective-permute-start.10 = (bf16[512,512]{1,0:T(8,128)(2,1)}, bf16[512,512]{1,0:T(8,128)(2,1)S(1)}, u32[]{:S(2)}, u32[]{:S(2)}) collective-permute-start(bf16[512,512]{1,0:T(8,128)(2,1)} %get-tuple-element.58.q_keep), channel_id=1, source_target_pairs={{0,8},{4,12},{8,0},{12,4},{16,24},{20,28},{24,16},{28,20},{1,9},{5... | collective-permute-start | bytes 1572872 | tf_op jit(solution)/shard_map/ppermute | solution.py:365
  12.1 15.5 %collective-permute-start.11 = (bf16[128,2048]{1,0:T(8,128)(2,1)}, bf16[128,2048]{1,0:T(8,128)(2,1)S(1)}, u32[]{:S(2)}, u32[]{:S(2)}) collective-permute-start(bf16[128,2048]{1,0:T(8,128)(2,1)} %get-tuple-element.59), channel_id=1, source_target_pairs={{0,16},{4,20},{8,24},{12,28},{16,0},{20,4},{24,8},{28,12},{1,17},{... | collective-permute-start | bytes 1572872 | tf_op jit(solution)/shard_map/ppermute | solution.py:365
  13.7 13.8 %collective-permute-start.12 = (bf16[512,512]{1,0:T(8,128)(2,1)}, bf16[512,512]{1,0:T(8,128)(2,1)S(1)}, u32[]{:S(2)}, u32[]{:S(2)}) collective-permute-start(bf16[512,512]{1,0:T(8,128)(2,1)} %get-tuple-element.61), channel_id=1, source_target_pairs={{0,4},{4,0},{8,12},{12,8},{16,20},{20,16},{24,28},{28,24},{1,5},{5... | collective-permute-start | bytes 1572872 | tf_op jit(solution)/shard_map/ppermute | solution.py:362
  18.7 9.4 %collective-permute-start.7 = (f32[32,1024]{1,0:T(8,128)S(1)}, f32[32,1024]{1,0:T(8,128)S(1)}, u32[]{:S(2)}, u32[]{:S(2)}) collective-permute-start(f32[32,1024]{1,0:T(8,128)S(1)} %get-tuple-element.55), channel_id=1, source_target_pairs={{0,8},{4,12},{8,0},{12,4},{16,24},{20,28},{24,16},{28,20},{1,9},{5... | collective-permute-start | bytes 393224 | tf_op jit(solution)/shard_map/ppermute | solution.py:365
  19.1 12.3 %collective-permute-start.8 = (f32[32,1024]{1,0:T(8,128)S(1)}, f32[32,1024]{1,0:T(8,128)S(1)}, u32[]{:S(2)}, u32[]{:S(2)}) collective-permute-start(f32[32,1024]{1,0:T(8,128)S(1)} %get-tuple-element.56), channel_id=1, source_target_pairs={{0,16},{4,20},{8,24},{12,28},{16,0},{20,4},{24,8},{28,12},{1,17},{... | collective-permute-start | bytes 393224 | tf_op jit(solution)/shard_map/ppermute | solution.py:365
  25.1 6.4 %collective-permute-start.9 = (f32[32,1024]{1,0:T(8,128)S(1)}, f32[32,1024]{1,0:T(8,128)S(1)}, u32[]{:S(2)}, u32[]{:S(2)}) collective-permute-start(f32[32,1024]{1,0:T(8,128)S(1)} %get-tuple-element.57), channel_id=1, source_target_pairs={{0,24},{4,28},{8,16},{12,20},{16,8},{20,12},{24,0},{28,4},{1,25},{... | collective-permute-start | bytes 393224 | tf_op jit(solution)/shard_map/ppermute | solution.py:365
  27.6 7.8 %collective-permute-start.1 = (bf16[128,2048]{1,0:T(8,128)(2,1)S(1)}, bf16[128,2048]{1,0:T(8,128)(2,1)S(1)}, u32[]{:S(2)}, u32[]{:S(2)}) collective-permute-start(bf16[128,2048]{1,0:T(8,128)(2,1)S(1)} %copy-done.3), channel_id=1, source_target_pairs={{0,4},{4,0},{8,12},{12,8},{16,20},{20,16},{24,28},{28,24},{1,5},{5... | collective-permute-start | bytes 1572872 | tf_op jit(solution)/shard_map/ppermute | solution.py:362
  28.1 14.2 %collective-permute-start.13 = (bf16[512,512]{1,0:T(8,128)(2,1)S(1)}, bf16[512,512]{1,0:T(8,128)(2,1)S(1)}, u32[]{:S(2)}, u32[]{:S(2)}) collective-permute-start(bf16[512,512]{1,0:T(8,128)(2,1)S(1)} %collective-permute-done.12.q_other), channel_id=1, source_target_pairs={{0,8},{4,12},{8,0},{12,4},{16,24},{20,28},{24,16},{28,20},{1,9},{5... | collective-permute-start | bytes 1572872 | tf_op jit(solution)/shard_map/ppermute | solution.py:365
  31.4 8.8 %collective-permute-start.17 = (bf16[128,2048]{1,0:T(8,128)(2,1)S(1)}, bf16[128,2048]{1,0:T(8,128)(2,1)S(1)}, u32[]{:S(2)}, u32[]{:S(2)}) collective-permute-start(bf16[128,2048]{1,0:T(8,128)(2,1)S(1)} %collective-permute-done.11.own), channel_id=1, source_target_pairs={{0,4},{4,0},{8,12},{12,8},{16,20},{20,16},{24,28},{28,24},{1,5},{5... | collective-permute-start | bytes 1572872 | tf_op jit(solution)/shard_map/ppermute | solution.py:362
  32.1 14.4 %collective-permute-start.16 = (bf16[512,512]{1,0:T(8,128)(2,1)S(1)}, bf16[512,512]{1,0:T(8,128)(2,1)S(1)}, u32[]{:S(2)}, u32[]{:S(2)}) collective-permute-start(bf16[512,512]{1,0:T(8,128)(2,1)S(1)} %get-tuple-element.70), channel_id=1, source_target_pairs={{0,16},{4,20},{8,24},{12,28},{16,0},{20,4},{24,8},{28,12},{1,17},{... | collective-permute-start | bytes 1572872 | tf_op jit(solution)/shard_map/ppermute | solution.py:365
  37.6 5.7 %collective-permute-start.15 = (bf16[64,256]{1,0:T(8,128)(2,1)S(1)}, bf16[64,256]{1,0:T(8,128)(2,1)S(1)}, u32[]{:S(2)}, u32[]{:S(2)}) collective-permute-start(bf16[64,256]{1,0:T(8,128)(2,1)S(1)} %kv_turn.1), channel_id=1, source_target_pairs={{0,2},{1,3},{2,0},{3,1},{4,6},{5,7},{6,4},{7,5},{8,10},{9,11},{10,... | collective-permute-start | bytes 98312 | tf_op jit(solution)/shard_map/ppermute | solution.py:374
  46.5 12.0 %collective-permute-start.18 = (bf16[256,512]{1,0:T(8,128)(2,1)S(1)}, bf16[256,512]{1,0:T(8,128)(2,1)S(1)}, u32[]{:S(2)}, u32[]{:S(2)}) collective-permute-start(bf16[256,512]{1,0:T(8,128)(2,1)S(1)} %q_late.3), channel_id=1, source_target_pairs={{0,16},{4,20},{8,24},{12,28},{16,0},{20,4},{24,8},{28,12},{1,17},{... | collective-permute-start | bytes 786440 | tf_op jit(solution)/shard_map/ppermute | solution.py:365
  48.8 4.4 %collective-permute-start.19 = (bf16[128,256]{1,0:T(8,128)(2,1)S(1)}, bf16[128,256]{1,0:T(8,128)(2,1)S(1)}, u32[]{:S(2)}, u32[]{:S(2)}) collective-permute-start(bf16[128,256]{1,0:T(8,128)(2,1)S(1)} %kv_join.1.refs_0_), channel_id=1, source_target_pairs={{0,8},{4,12},{8,0},{12,4},{16,24},{20,28},{24,16},{28,20},{1,9},{5... | collective-permute-start | bytes 196616 | tf_op jit(solution)/shard_map/ppermute | solution.py:365
  51.0 7.6 %collective-permute-start.20 = (bf16[128,256]{1,0:T(8,128)(2,1)S(1)}, bf16[128,256]{1,0:T(8,128)(2,1)S(1)}, u32[]{:S(2)}, u32[]{:S(2)}) collective-permute-start(bf16[128,256]{1,0:T(8,128)(2,1)S(1)} %kv_join.1.refs_0_), channel_id=1, source_target_pairs={{0,16},{4,20},{8,24},{12,28},{16,0},{20,4},{24,8},{28,12},{1,17},{... | collective-permute-start | bytes 196616 | tf_op jit(solution)/shard_map/ppermute | solution.py:365
  51.3 7.3 %collective-permute-start.21 = (bf16[128,256]{1,0:T(8,128)(2,1)S(1)}, bf16[128,256]{1,0:T(8,128)(2,1)S(1)}, u32[]{:S(2)}, u32[]{:S(2)}) collective-permute-start(bf16[128,256]{1,0:T(8,128)(2,1)S(1)} %kv_join.1.refs_0_), channel_id=1, source_target_pairs={{0,24},{4,28},{8,16},{12,20},{16,8},{20,12},{24,0},{28,4},{1,25},{... | collective-permute-start | bytes 196616 | tf_op jit(solution)/shard_map/ppermute | solution.py:365
  52.6 15.9 %collective-permute-start.24 = (bf16[512,512]{1,0:T(8,128)(2,1)S(1)}, bf16[512,512]{1,0:T(8,128)(2,1)S(1)}, u32[]{:S(2)}, u32[]{:S(2)}) collective-permute-start(bf16[512,512]{1,0:T(8,128)(2,1)S(1)} %get-tuple-element.76), channel_id=1, source_target_pairs={{0,16},{4,20},{8,24},{12,28},{16,0},{20,4},{24,8},{28,12},{1,17},{... | collective-permute-start | bytes 1572872 | tf_op jit(solution)/shard_map/ppermute | solution.py:365
  60.9 6.4 %collective-permute-start.25 = (bf16[256,512]{1,0:T(8,128)(2,1)S(1)}, bf16[256,512]{1,0:T(8,128)(2,1)S(1)}, u32[]{:S(2)}, u32[]{:S(2)}) collective-permute-start(bf16[256,512]{1,0:T(8,128)(2,1)S(1)} %attend.1.near), channel_id=1, source_target_pairs={{0,8},{4,12},{8,0},{12,4},{16,24},{20,28},{24,16},{28,20},{1,9},{5... | collective-permute-start | bytes 786440 | tf_op jit(solution)/shard_map/ppermute | solution.py:365
  67.3 4.9 %collective-permute-start.23 = (bf16[256,512]{1,0:T(8,128)(2,1)S(1)}, bf16[256,512]{1,0:T(8,128)(2,1)S(1)}, u32[]{:S(2)}, u32[]{:S(2)}) collective-permute-start(bf16[256,512]{1,0:T(8,128)(2,1)S(1)} %attend.1.near), channel_id=1, source_target_pairs={{0,4},{4,0},{8,12},{12,8},{16,20},{20,16},{24,28},{28,24},{1,5},{5... | collective-permute-start | bytes 786440 | tf_op jit(solution)/shard_map/ppermute | solution.py:362
  70.1 9.2 %collective-permute-start.27 = (bf16[128,1024]{1,0:T(8,128)(2,1)S(1)}, bf16[128,1024]{1,0:T(8,128)(2,1)S(1)}, u32[]{:S(2)}, u32[]{:S(2)}) collective-permute-start(bf16[128,1024]{1,0:T(8,128)(2,1)S(1)} %get-tuple-element.78), channel_id=1, source_target_pairs={{0,8},{4,12},{8,0},{12,4},{16,24},{20,28},{24,16},{28,20},{1,9},{5... | collective-permute-start | bytes 786440 | tf_op jit(solution)/shard_map/ppermute | solution.py:365
  71.8 13.3 %collective-permute-start.32 = (bf16[128,1024]{1,0:T(8,128)(2,1)S(1)}, bf16[128,1024]{1,0:T(8,128)(2,1)S(1)}, u32[]{:S(2)}, u32[]{:S(2)}) collective-permute-start(bf16[128,1024]{1,0:T(8,128)(2,1)S(1)} %get-tuple-element.84), channel_id=1, source_target_pairs={{0,8},{4,12},{8,0},{12,4},{16,24},{20,28},{24,16},{28,20},{1,9},{5... | collective-permute-start | bytes 786440 | tf_op jit(solution)/shard_map/ppermute | solution.py:365
  72.2 14.3 %collective-permute-start = (bf16[128,512]{1,0:T(8,128)(2,1)S(1)}, bf16[128,512]{1,0:T(8,128)(2,1)S(1)}, u32[]{:S(2)}, u32[]{:S(2)}) collective-permute-start(bf16[128,512]{1,0:T(8,128)(2,1)S(1)} %copy-done.11), channel_id=1, source_target_pairs={{0,4},{4,0},{8,12},{12,8},{16,20},{20,16},{24,28},{28,24},{1,5},{5... | collective-permute-start | bytes 393224 | tf_op jit(solution)/shard_map/ppermute | solution.py:362
  80.0 10.0 %collective-permute-start.28 = (bf16[128,512]{1,0:T(8,128)(2,1)S(1)}, bf16[128,512]{1,0:T(8,128)(2,1)S(1)}, u32[]{:S(2)}, u32[]{:S(2)}) collective-permute-start(bf16[128,512]{1,0:T(8,128)(2,1)S(1)} %get-tuple-element.80), channel_id=1, source_target_pairs={{0,1},{1,0},{2,3},{3,2},{4,5},{5,4},{6,7},{7,6},{8,9},{9,8},{10,11... | collective-permute-start | bytes 393224 | tf_op jit(solution)/shard_map/ppermute | solution.py:374
  81.6 12.8 %collective-permute-start.29 = (bf16[128,512]{1,0:T(8,128)(2,1)S(1)}, bf16[128,512]{1,0:T(8,128)(2,1)S(1)}, u32[]{:S(2)}, u32[]{:S(2)}) collective-permute-start(bf16[128,512]{1,0:T(8,128)(2,1)S(1)} %get-tuple-element.81), channel_id=1, source_target_pairs={{0,2},{1,3},{2,0},{3,1},{4,6},{5,7},{6,4},{7,5},{8,10},{9,11},{10,... | collective-permute-start | bytes 393224 | tf_op jit(solution)/shard_map/ppermute | solution.py:374
  84.2 10.2 %collective-permute-start.30 = (bf16[128,512]{1,0:T(8,128)(2,1)S(1)}, bf16[128,512]{1,0:T(8,128)(2,1)S(1)}, u32[]{:S(2)}, u32[]{:S(2)}) collective-permute-start(bf16[128,512]{1,0:T(8,128)(2,1)S(1)} %get-tuple-element.82), channel_id=1, source_target_pairs={{0,3},{1,2},{2,1},{3,0},{4,7},{5,6},{6,5},{7,4},{8,11},{9,10},{10,... | collective-permute-start | bytes 393224 | tf_op jit(solution)/shard_map/ppermute | solution.py:374
  85.8 8.8 %collective-permute-start.33 = (bf16[128,512]{1,0:T(8,128)(2,1)S(1)}, bf16[128,512]{1,0:T(8,128)(2,1)S(1)}, u32[]{:S(2)}, u32[]{:S(2)}) collective-permute-start(bf16[128,512]{1,0:T(8,128)(2,1)S(1)} %get-tuple-element.86), channel_id=1, source_target_pairs={{0,1},{1,0},{2,3},{3,2},{4,5},{5,4},{6,7},{7,6},{8,9},{9,8},{10,11... | collective-permute-start | bytes 393224 | tf_op jit(solution)/shard_map/ppermute | solution.py:374
  86.5 17.9 %collective-permute-start.34 = (bf16[128,512]{1,0:T(8,128)(2,1)S(1)}, bf16[128,512]{1,0:T(8,128)(2,1)S(1)}, u32[]{:S(2)}, u32[]{:S(2)}) collective-permute-start(bf16[128,512]{1,0:T(8,128)(2,1)S(1)} %get-tuple-element.87), channel_id=1, source_target_pairs={{0,2},{1,3},{2,0},{3,1},{4,6},{5,7},{6,4},{7,5},{8,10},{9,11},{10,... | collective-permute-start | bytes 393224 | tf_op jit(solution)/shard_map/ppermute | solution.py:374
  90.0 14.4 %collective-permute-start.35 = (bf16[128,512]{1,0:T(8,128)(2,1)S(1)}, bf16[128,512]{1,0:T(8,128)(2,1)S(1)}, u32[]{:S(2)}, u32[]{:S(2)}) collective-permute-start(bf16[128,512]{1,0:T(8,128)(2,1)S(1)} %get-tuple-element.88), channel_id=1, source_target_pairs={{0,3},{1,2},{2,1},{3,0},{4,7},{5,6},{6,5},{7,4},{8,11},{9,10},{10,... | collective-permute-start | bytes 393224 | tf_op jit(solution)/shard_map/ppermute | solution.py:374
  94.6 9.9 %collective-permute-start.31 = (bf16[128,512]{1,0:T(8,128)(2,1)S(1)}, bf16[128,512]{1,0:T(8,128)(2,1)S(1)}, u32[]{:S(2)}, u32[]{:S(2)}) collective-permute-start(bf16[128,512]{1,0:T(8,128)(2,1)S(1)} %mix_give.1), channel_id=1, source_target_pairs={{0,4},{4,0},{8,12},{12,8},{16,20},{20,16},{24,28},{28,24},{1,5},{5... | collective-permute-start | bytes 393224 | tf_op jit(solution)/shard_map/ppermute | solution.py:362
  (16 other events, 204.2 us)

commit v4 on v3

--- a/solution.py
+++ b/solution.py
@@ -463,7 +463,7 @@
         [shape(4 * vis_here, 2 * head_dim)],
         name="kv_turn",
     )[0]
-    kv_last, o_early, q_far = lax.optimization_barrier((across(turn, 2), o_early, q_far))
+    kv_last, o_early, _ = lax.optimization_barrier((across(turn, 2), o_early, q_far))
     kv_first = call(
         kv_join_kernel,
         (here, kv_z, kv_last),

time: 106 us -> 106 us (level)
    ppermute x8, waiting for transfers between devices: 15.2 us -> 13.8 us  [across(): return lax.ppermute(x, 'img', [(k, k ^ t) for k in range(CHIPS)])]
where the time goes in v4:
time: 106 us
  waiting for transfers between devices  46.7 us (44%)
  starting transfers between devices  37.6 us (35%)
  Pallas kernels  18.9 us (18%)
  other arithmetic  1.07 us (1%)
    ppermute x18, waiting for transfers between devices, peer(): return lax.ppermute(x, 'ctx', [(k, k ^ 2 * s) for k in range(ctx_count)])  31.1 us
    ppermute x18, starting transfers between devices, peer(): return lax.ppermute(x, 'ctx', [(k, k ^ 2 * s) for k in range(ctx_count)])  22.9 us
    pallas_call x16, Pallas kernels, call(): pl.pallas_call(kernel, out_shape=outs, in_specs=specs, out_specs=[VMEM] *...  18.9 us
    ppermute x8, waiting for transfers between devices, across(): return lax.ppermute(x, 'img', [(k, k ^ t) for k in range(CHIPS)])  13.8 us
    ppermute x8, starting transfers between devices, across(): return lax.ppermute(x, 'img', [(k, k ^ t) for k in range(CHIPS)])  13.1 us
  transfers between devices with their start and end apart: 36, of which 14 were waited for; matrix products, arithmetic and copies ran while one was open for 2% of the time, Pallas kernels for 17%

profile of v4, /device:TPU:0, one launch (start us, length us, event | category | flops | bytes accessed | tf_op | source)
XLA Modules:
  0.0 106.2 jit_solution(8266052630011339762)
XLA Ops:
  1.1 4.2 %start.1 = (bf16[16,1024]{1,0:T(8,128)(2,1)}, bf16[16,1024]{1,0:T(8,128)(2,1)}, bf16[16,1024]{1,0:T(8,128)(2,1)}, bf16[16,1024]{1,0:T(8,128)(2,1)}, bf16[128,204...) custom-call(s32[3]{0:T(128)} %pad_add_fusion.1.where, ...), custom_call_target="tpu_custom_call" | custom-call | flops 4194304 | bytes 4194304 | tf_op jit(solution)/shard_map/start/pallas_call | solution.py:122
  5.3 2.6 %collective-permute-start.2 = (bf16[16,1024]{1,0:T(8,128)(2,1)}, bf16[16,1024]{1,0:T(8,128)(2,1)S(1)}, u32[]{:S(2)}, u32[]{:S(2)}) collective-permute-start(bf16[16,1024]{1,0:T(8,128)(2,1)} %get-tuple-element.50), channel_id=1, source_target_pairs={{0,8},{4,12},{8,0},{12,4},{16,24},{20,28},{24,16},{28,20},{1,9},{5... | collective-permute-start | bytes 98312 | tf_op jit(solution)/shard_map/ppermute | solution.py:365
  7.9 1.5 %collective-permute-start.3 = (bf16[16,1024]{1,0:T(8,128)(2,1)}, bf16[16,1024]{1,0:T(8,128)(2,1)S(1)}, u32[]{:S(2)}, u32[]{:S(2)}) collective-permute-start(bf16[16,1024]{1,0:T(8,128)(2,1)} %get-tuple-element.51), channel_id=1, source_target_pairs={{0,16},{4,20},{8,24},{12,28},{16,0},{20,4},{24,8},{28,12},{1,17},{... | collective-permute-start | bytes 98312 | tf_op jit(solution)/shard_map/ppermute | solution.py:365
  9.4 1.9 %collective-permute-start.10 = (bf16[512,512]{1,0:T(8,128)(2,1)}, bf16[512,512]{1,0:T(8,128)(2,1)S(1)}, u32[]{:S(2)}, u32[]{:S(2)}) collective-permute-start(bf16[512,512]{1,0:T(8,128)(2,1)} %get-tuple-element.57.q_keep), channel_id=1, source_target_pairs={{0,8},{4,12},{8,0},{12,4},{16,24},{20,28},{24,16},{28,20},{1,9},{5... | collective-permute-start | bytes 1572872 | tf_op jit(solution)/shard_map/ppermute | solution.py:365
  12.1 1.5 %collective-permute-start.11 = (bf16[128,2048]{1,0:T(8,128)(2,1)}, bf16[128,2048]{1,0:T(8,128)(2,1)S(1)}, u32[]{:S(2)}, u32[]{:S(2)}) collective-permute-start(bf16[128,2048]{1,0:T(8,128)(2,1)} %get-tuple-element.58), channel_id=1, source_target_pairs={{0,16},{4,20},{8,24},{12,28},{16,0},{20,4},{24,8},{28,12},{1,17},{... | collective-permute-start | bytes 1572872 | tf_op jit(solution)/shard_map/ppermute | solution.py:365
  16.1 2.6 %kv_shares.1 = (f32[32,1024]{1,0:T(8,128)S(1)}, f32[32,1024]{1,0:T(8,128)S(1)}, f32[32,1024]{1,0:T(8,128)S(1)}, f32[32,1024]{1,0:T(8,128)S(1)}) custom-call(s32[3]{0:T(128)S(1)} %copy-done.5, bf16[64,1024]{1,0:T(8,128)(2,1)S(1)} %constant_dynamic-update-slice_fusion.vis, bf16[64,1024]{1,0:T(8,128)(2,1)S(1)} %collective-permute-done.5.vis_other, ...), custom_call_target="tpu_custom_call" | custom-call | flops 536870912 | bytes 4194304 | tf_op jit(solution)/shard_map/kv_shares/pallas_call | solution.py:122
  19.4 5.7 %collective-permute-done.10.q_side = bf16[512,512]{1,0:T(8,128)(2,1)S(1)} collective-permute-done((bf16[512,512]{1,0:T(8,128)(2,1)}, bf16[512,512]{1,0:T(8,128)(2,1)S(1)}, u32[]{:S(2)}, u32[]{:S(2)}) %collective-permute-start.10) | collective-permute-done | bytes 524320 | tf_op jit(solution)/shard_map/ppermute | solution.py:365
  25.1 2.3 %collective-permute-start.9 = (f32[32,1024]{1,0:T(8,128)S(1)}, f32[32,1024]{1,0:T(8,128)S(1)}, u32[]{:S(2)}, u32[]{:S(2)}) collective-permute-start(f32[32,1024]{1,0:T(8,128)S(1)} %get-tuple-element.56), channel_id=1, source_target_pairs={{0,24},{4,28},{8,16},{12,20},{16,8},{20,12},{24,0},{28,4},{1,25},{... | collective-permute-start | bytes 393224 | tf_op jit(solution)/shard_map/ppermute | solution.py:365
  28.7 2.7 %collective-permute-done.8.refs_2_ = f32[32,1024]{1,0:T(8,128)S(1)} collective-permute-done((f32[32,1024]{1,0:T(8,128)S(1)}, f32[32,1024]{1,0:T(8,128)S(1)}, u32[]{:S(2)}, u32[]{:S(2)}) %collective-permute-start.8) | collective-permute-done | bytes 131104 | tf_op jit(solution)/shard_map/ppermute | solution.py:365
  32.2 1.6 %collective-permute-start.16 = (bf16[64,256]{1,0:T(8,128)(2,1)S(1)}, bf16[64,256]{1,0:T(8,128)(2,1)S(1)}, u32[]{:S(2)}, u32[]{:S(2)}) collective-permute-start(bf16[64,256]{1,0:T(8,128)(2,1)S(1)} %get-tuple-element.68), channel_id=1, source_target_pairs={{0,1},{1,0},{2,3},{3,2},{4,5},{5,4},{6,7},{7,6},{8,9},{9,8},{10,11... | collective-permute-start | bytes 98312 | tf_op jit(solution)/shard_map/ppermute | solution.py:374
  35.0 1.4 %collective-permute-start.18 = (bf16[512,512]{1,0:T(8,128)(2,1)S(1)}, bf16[512,512]{1,0:T(8,128)(2,1)S(1)}, u32[]{:S(2)}, u32[]{:S(2)}) collective-permute-start(bf16[512,512]{1,0:T(8,128)(2,1)S(1)} %get-tuple-element.70), channel_id=1, source_target_pairs={{0,16},{4,20},{8,24},{12,28},{16,0},{20,4},{24,8},{28,12},{1,17},{... | collective-permute-start | bytes 1572872 | tf_op jit(solution)/shard_map/ppermute | solution.py:365
  36.4 2.6 %collective-permute-start.17 = (bf16[64,256]{1,0:T(8,128)(2,1)S(1)}, bf16[64,256]{1,0:T(8,128)(2,1)S(1)}, u32[]{:S(2)}, u32[]{:S(2)}) collective-permute-start(bf16[64,256]{1,0:T(8,128)(2,1)S(1)} %kv_turn.1), channel_id=1, source_target_pairs={{0,2},{1,3},{2,0},{3,1},{4,6},{5,7},{6,4},{7,5},{8,10},{9,11},{10,... | collective-permute-start | bytes 98312 | tf_op jit(solution)/shard_map/ppermute | solution.py:374
  40.0 2.3 %collective-permute-done.13.q_corner = bf16[512,512]{1,0:T(8,128)(2,1)S(1)} collective-permute-done((bf16[512,512]{1,0:T(8,128)(2,1)S(1)}, bf16[512,512]{1,0:T(8,128)(2,1)S(1)}, u32[]{:S(2)}, u32[]{:S(2)}) %collective-permute-start.13) | collective-permute-done | bytes 524320 | tf_op jit(solution)/shard_map/ppermute | solution.py:365
  43.2 2.0 %collective-permute-start.15 = (bf16[256,512]{1,0:T(8,128)(2,1)S(1)}, bf16[256,512]{1,0:T(8,128)(2,1)S(1)}, u32[]{:S(2)}, u32[]{:S(2)}) collective-permute-start(bf16[256,512]{1,0:T(8,128)(2,1)S(1)} %q_late.3), channel_id=1, source_target_pairs={{0,16},{4,20},{8,24},{12,28},{16,0},{20,4},{24,8},{28,12},{1,17},{... | collective-permute-start | bytes 786440 | tf_op jit(solution)/shard_map/ppermute | solution.py:365
  46.3 3.6 %collective-permute-done.18.o_early = bf16[512,512]{1,0:T(8,128)(2,1)S(1)} collective-permute-done((bf16[512,512]{1,0:T(8,128)(2,1)S(1)}, bf16[512,512]{1,0:T(8,128)(2,1)S(1)}, u32[]{:S(2)}, u32[]{:S(2)}) %collective-permute-start.18) | collective-permute-done | bytes 524320 | tf_op jit(solution)/shard_map/ppermute | solution.py:365
  49.9 1.3 %collective-permute-start.19 = (bf16[128,256]{1,0:T(8,128)(2,1)S(1)}, bf16[128,256]{1,0:T(8,128)(2,1)S(1)}, u32[]{:S(2)}, u32[]{:S(2)}) collective-permute-start(bf16[128,256]{1,0:T(8,128)(2,1)S(1)} %kv_join.1.refs_0_), channel_id=1, source_target_pairs={{0,8},{4,12},{8,0},{12,4},{16,24},{20,28},{24,16},{28,20},{1,9},{5... | collective-permute-start | bytes 196616 | tf_op jit(solution)/shard_map/ppermute | solution.py:365
  51.2 2.1 %collective-permute-start.20 = (bf16[128,256]{1,0:T(8,128)(2,1)S(1)}, bf16[128,256]{1,0:T(8,128)(2,1)S(1)}, u32[]{:S(2)}, u32[]{:S(2)}) collective-permute-start(bf16[128,256]{1,0:T(8,128)(2,1)S(1)} %kv_join.1.refs_0_), channel_id=1, source_target_pairs={{0,16},{4,20},{8,24},{12,28},{16,0},{20,4},{24,8},{28,12},{1,17},{... | collective-permute-start | bytes 196616 | tf_op jit(solution)/shard_map/ppermute | solution.py:365
  53.4 1.5 %collective-permute-start.24 = (bf16[512,512]{1,0:T(8,128)(2,1)S(1)}, bf16[512,512]{1,0:T(8,128)(2,1)S(1)}, u32[]{:S(2)}, u32[]{:S(2)}) collective-permute-start(bf16[512,512]{1,0:T(8,128)(2,1)S(1)} %get-tuple-element.74), channel_id=1, source_target_pairs={{0,16},{4,20},{8,24},{12,28},{16,0},{20,4},{24,8},{28,12},{1,17},{... | collective-permute-start | bytes 1572872 | tf_op jit(solution)/shard_map/ppermute | solution.py:365
  54.9 2.7 %collective-permute-done.20.refs_2_ = bf16[128,256]{1,0:T(8,128)(2,1)S(1)} collective-permute-done((bf16[128,256]{1,0:T(8,128)(2,1)S(1)}, bf16[128,256]{1,0:T(8,128)(2,1)S(1)}, u32[]{:S(2)}, u32[]{:S(2)}) %collective-permute-start.20) | collective-permute-done | bytes 65568 | tf_op jit(solution)/shard_map/ppermute | solution.py:365
  58.5 2.4 %attend.1.near = bf16[256,512]{1,0:T(8,128)(2,1)S(1)} custom-call(f32[1,128]{1,0:T(1,128)S(1)} %bitcast.8, f32[256,512]{1,0:T(8,128)S(1)} %q_late.2.first, bf16[256,512]{1,0:T(8,128)(2,1)S(1)} %collective-permute-done.15.landed, bf16[128,256]{1,0:T(8,128)(2,1)S(1)} %kv_join.1.refs_0_, bf16[128,256]{1,0:T(8,128)(2,1)S(1)} %collective-permute-done.19.refs_1_, ...), custom_call_target="tpu_custom_call" | custom-call | flops 268435456 | bytes 2097152 | tf_op jit(solution)/shard_map/attend/pallas_call | solution.py:122
  62.1 5.8 %collective-permute-done.25.near = bf16[256,512]{1,0:T(8,128)(2,1)S(1)} collective-permute-done((bf16[256,512]{1,0:T(8,128)(2,1)S(1)}, bf16[256,512]{1,0:T(8,128)(2,1)S(1)}, u32[]{:S(2)}, u32[]{:S(2)}) %collective-permute-start.25) | collective-permute-done | bytes 262176 | tf_op jit(solution)/shard_map/ppermute | solution.py:365
  69.4 1.3 %o_share.3 = (bf16[128,1024]{1,0:T(8,128)(2,1)S(1)}, bf16[128,1024]{1,0:T(8,128)(2,1)S(1)}) custom-call(s32[3]{0:T(128)S(1)} %copy-done.5, bf16[256,512]{1,0:T(8,128)(2,1)S(1)} %collective-permute-done.25.near, bf16[256,512]{1,0:T(8,128)(2,1)S(1)} %collective-permute-done.26.far, bf16[1024,512]{1,0:T(8,128)(2,1)S(1)} %copy-done, ...), custom_call_target="tpu_custom_call" | custom-call | flops 536870912 | bytes 2097152 | tf_op jit(solution)/shard_map/o_share/pallas_call | solution.py:122
  70.7 1.8 %collective-permute-start.27 = (bf16[128,1024]{1,0:T(8,128)(2,1)S(1)}, bf16[128,1024]{1,0:T(8,128)(2,1)S(1)}, u32[]{:S(2)}, u32[]{:S(2)}) collective-permute-start(bf16[128,1024]{1,0:T(8,128)(2,1)S(1)} %get-tuple-element.76), channel_id=1, source_target_pairs={{0,8},{4,12},{8,0},{12,4},{16,24},{20,28},{24,16},{28,20},{1,9},{5... | collective-permute-start | bytes 786440 | tf_op jit(solution)/shard_map/ppermute | solution.py:365
  72.8 1.3 %o_share.2 = (bf16[128,1024]{1,0:T(8,128)(2,1)S(1)}, bf16[128,1024]{1,0:T(8,128)(2,1)S(1)}) custom-call(s32[3]{0:T(128)S(1)} %copy-done.5, bf16[256,512]{1,0:T(8,128)(2,1)S(1)} %attend.1.near, bf16[256,512]{1,0:T(8,128)(2,1)S(1)} %collective-permute-done.23.far, bf16[1024,512]{1,0:T(8,128)(2,1)S(1)} %copy-done, ...), custom_call_target="tpu_custom_call" | custom-call | flops 536870912 | bytes 2097152 | tf_op jit(solution)/shard_map/o_share/pallas_call | solution.py:122
  74.0 5.8 %collective-permute-done.27.landed = bf16[128,1024]{1,0:T(8,128)(2,1)S(1)} collective-permute-done((bf16[128,1024]{1,0:T(8,128)(2,1)S(1)}, bf16[128,1024]{1,0:T(8,128)(2,1)S(1)}, u32[]{:S(2)}, u32[]{:S(2)}) %collective-permute-start.27) | collective-permute-done | bytes 262176 | tf_op jit(solution)/shard_map/ppermute | solution.py:365
  81.0 2.6 %collective-permute-start.29 = (bf16[128,512]{1,0:T(8,128)(2,1)S(1)}, bf16[128,512]{1,0:T(8,128)(2,1)S(1)}, u32[]{:S(2)}, u32[]{:S(2)}) collective-permute-start(bf16[128,512]{1,0:T(8,128)(2,1)S(1)} %get-tuple-element.79), channel_id=1, source_target_pairs={{0,2},{1,3},{2,0},{3,1},{4,6},{5,7},{6,4},{7,5},{8,10},{9,11},{10,... | collective-permute-start | bytes 393224 | tf_op jit(solution)/shard_map/ppermute | solution.py:374
  83.6 1.3 %collective-permute-start.30 = (bf16[128,512]{1,0:T(8,128)(2,1)S(1)}, bf16[128,512]{1,0:T(8,128)(2,1)S(1)}, u32[]{:S(2)}, u32[]{:S(2)}) collective-permute-start(bf16[128,512]{1,0:T(8,128)(2,1)S(1)} %get-tuple-element.80), channel_id=1, source_target_pairs={{0,3},{1,2},{2,1},{3,0},{4,7},{5,6},{6,5},{7,4},{8,11},{9,10},{10,... | collective-permute-start | bytes 393224 | tf_op jit(solution)/shard_map/ppermute | solution.py:374
  86.6 2.8 %collective-permute-start.34 = (bf16[128,512]{1,0:T(8,128)(2,1)S(1)}, bf16[128,512]{1,0:T(8,128)(2,1)S(1)}, u32[]{:S(2)}, u32[]{:S(2)}) collective-permute-start(bf16[128,512]{1,0:T(8,128)(2,1)S(1)} %get-tuple-element.85), channel_id=1, source_target_pairs={{0,2},{1,3},{2,0},{3,1},{4,6},{5,7},{6,4},{7,5},{8,10},{9,11},{10,... | collective-permute-start | bytes 393224 | tf_op jit(solution)/shard_map/ppermute | solution.py:374
  89.4 1.3 %collective-permute-start.35 = (bf16[128,512]{1,0:T(8,128)(2,1)S(1)}, bf16[128,512]{1,0:T(8,128)(2,1)S(1)}, u32[]{:S(2)}, u32[]{:S(2)}) collective-permute-start(bf16[128,512]{1,0:T(8,128)(2,1)S(1)} %get-tuple-element.86), channel_id=1, source_target_pairs={{0,3},{1,2},{2,1},{3,0},{4,7},{5,6},{6,5},{7,4},{8,11},{9,10},{10,... | collective-permute-start | bytes 393224 | tf_op jit(solution)/shard_map/ppermute | solution.py:374
  90.8 3.9 %collective-permute-done.29.refs_2_ = bf16[128,512]{1,0:T(8,128)(2,1)S(1)} collective-permute-done((bf16[128,512]{1,0:T(8,128)(2,1)S(1)}, bf16[128,512]{1,0:T(8,128)(2,1)S(1)}, u32[]{:S(2)}, u32[]{:S(2)}) %collective-permute-start.29) | collective-permute-done | bytes 131104 | tf_op jit(solution)/shard_map/ppermute | solution.py:374
  94.9 9.9 %collective-permute-done.34.refs_2_ = bf16[128,512]{1,0:T(8,128)(2,1)S(1)} collective-permute-done((bf16[128,512]{1,0:T(8,128)(2,1)S(1)}, bf16[128,512]{1,0:T(8,128)(2,1)S(1)}, u32[]{:S(2)}, u32[]{:S(2)}) %collective-permute-start.34) | collective-permute-done | bytes 131104 | tf_op jit(solution)/shard_map/ppermute | solution.py:374
  104.8 1.4 %mix_keep.1 = bf16[128,1024]{1,0:T(8,128)(2,1)} custom-call(s32[3]{0:T(128)S(1)} %copy-done.5, f32[1]{0:T(128)S(6)} %tanh.3.gate, bf16[128,512]{1,0:T(8,128)(2,1)S(1)} %copy-done.4, bf16[128,512]{1,0:T(8,128)(2,1)S(1)} %collective-permute-done.31.back, bf16[128,512]{1,0:T(8,128)(2,1)S(1)} %get-tuple-element.83.refs_0_, ...), custom_call_target="tpu_custom_call" | custom-call | flops 1048576 | bytes 1048576 | tf_op jit(solution)/shard_map/mix_keep/pallas_call | solution.py:122
  (93 shorter events, 17.5 us)
Async XLA Ops:
  0.0 16.1 %collective-permute-start.6 = (bf16[512,2048]{1,0:T(8,128)(2,1)}, bf16[512,2048]{1,0:T(8,128)(2,1)}, u32[]{:S(2)}, u32[]{:S(2)}) collective-permute-start(bf16[512,2048]{1,0:T(8,128)(2,1)} %kv_own.1), channel_id=1, source_target_pairs={{0,4},{4,0},{8,12},{12,8},{16,20},{20,16},{24,28},{28,24},{1,5},{5... | collective-permute-start | bytes 6291464 | tf_op jit(solution)/shard_map/ppermute | solution.py:362
  5.3 6.8 %collective-permute-start.2 = (bf16[16,1024]{1,0:T(8,128)(2,1)}, bf16[16,1024]{1,0:T(8,128)(2,1)S(1)}, u32[]{:S(2)}, u32[]{:S(2)}) collective-permute-start(bf16[16,1024]{1,0:T(8,128)(2,1)} %get-tuple-element.50), channel_id=1, source_target_pairs={{0,8},{4,12},{8,0},{12,4},{16,24},{20,28},{24,16},{28,20},{1,9},{5... | collective-permute-start | bytes 98312 | tf_op jit(solution)/shard_map/ppermute | solution.py:365
  7.9 5.8 %collective-permute-start.3 = (bf16[16,1024]{1,0:T(8,128)(2,1)}, bf16[16,1024]{1,0:T(8,128)(2,1)S(1)}, u32[]{:S(2)}, u32[]{:S(2)}) collective-permute-start(bf16[16,1024]{1,0:T(8,128)(2,1)} %get-tuple-element.51), channel_id=1, source_target_pairs={{0,16},{4,20},{8,24},{12,28},{16,0},{20,4},{24,8},{28,12},{1,17},{... | collective-permute-start | bytes 98312 | tf_op jit(solution)/shard_map/ppermute | solution.py:365
  9.4 5.4 %collective-permute-start.4 = (bf16[16,1024]{1,0:T(8,128)(2,1)}, bf16[16,1024]{1,0:T(8,128)(2,1)S(1)}, u32[]{:S(2)}, u32[]{:S(2)}) collective-permute-start(bf16[16,1024]{1,0:T(8,128)(2,1)} %get-tuple-element.52), channel_id=1, source_target_pairs={{0,24},{4,28},{8,16},{12,20},{16,8},{20,12},{24,0},{28,4},{1,25},{... | collective-permute-start | bytes 98312 | tf_op jit(solution)/shard_map/ppermute | solution.py:365
  9.4 15.6 %collective-permute-start.10 = (bf16[512,512]{1,0:T(8,128)(2,1)}, bf16[512,512]{1,0:T(8,128)(2,1)S(1)}, u32[]{:S(2)}, u32[]{:S(2)}) collective-permute-start(bf16[512,512]{1,0:T(8,128)(2,1)} %get-tuple-element.57.q_keep), channel_id=1, source_target_pairs={{0,8},{4,12},{8,0},{12,4},{16,24},{20,28},{24,16},{28,20},{1,9},{5... | collective-permute-start | bytes 1572872 | tf_op jit(solution)/shard_map/ppermute | solution.py:365
  12.1 15.5 %collective-permute-start.11 = (bf16[128,2048]{1,0:T(8,128)(2,1)}, bf16[128,2048]{1,0:T(8,128)(2,1)S(1)}, u32[]{:S(2)}, u32[]{:S(2)}) collective-permute-start(bf16[128,2048]{1,0:T(8,128)(2,1)} %get-tuple-element.58), channel_id=1, source_target_pairs={{0,16},{4,20},{8,24},{12,28},{16,0},{20,4},{24,8},{28,12},{1,17},{... | collective-permute-start | bytes 1572872 | tf_op jit(solution)/shard_map/ppermute | solution.py:365
  13.7 13.8 %collective-permute-start.12 = (bf16[512,512]{1,0:T(8,128)(2,1)}, bf16[512,512]{1,0:T(8,128)(2,1)S(1)}, u32[]{:S(2)}, u32[]{:S(2)}) collective-permute-start(bf16[512,512]{1,0:T(8,128)(2,1)} %get-tuple-element.60), channel_id=1, source_target_pairs={{0,4},{4,0},{8,12},{12,8},{16,20},{20,16},{24,28},{28,24},{1,5},{5... | collective-permute-start | bytes 1572872 | tf_op jit(solution)/shard_map/ppermute | solution.py:362
  18.7 9.4 %collective-permute-start.7 = (f32[32,1024]{1,0:T(8,128)S(1)}, f32[32,1024]{1,0:T(8,128)S(1)}, u32[]{:S(2)}, u32[]{:S(2)}) collective-permute-start(f32[32,1024]{1,0:T(8,128)S(1)} %get-tuple-element.54), channel_id=1, source_target_pairs={{0,8},{4,12},{8,0},{12,4},{16,24},{20,28},{24,16},{28,20},{1,9},{5... | collective-permute-start | bytes 393224 | tf_op jit(solution)/shard_map/ppermute | solution.py:365
  19.1 12.3 %collective-permute-start.8 = (f32[32,1024]{1,0:T(8,128)S(1)}, f32[32,1024]{1,0:T(8,128)S(1)}, u32[]{:S(2)}, u32[]{:S(2)}) collective-permute-start(f32[32,1024]{1,0:T(8,128)S(1)} %get-tuple-element.55), channel_id=1, source_target_pairs={{0,16},{4,20},{8,24},{12,28},{16,0},{20,4},{24,8},{28,12},{1,17},{... | collective-permute-start | bytes 393224 | tf_op jit(solution)/shard_map/ppermute | solution.py:365
  25.1 6.4 %collective-permute-start.9 = (f32[32,1024]{1,0:T(8,128)S(1)}, f32[32,1024]{1,0:T(8,128)S(1)}, u32[]{:S(2)}, u32[]{:S(2)}) collective-permute-start(f32[32,1024]{1,0:T(8,128)S(1)} %get-tuple-element.56), channel_id=1, source_target_pairs={{0,24},{4,28},{8,16},{12,20},{16,8},{20,12},{24,0},{28,4},{1,25},{... | collective-permute-start | bytes 393224 | tf_op jit(solution)/shard_map/ppermute | solution.py:365
  27.6 6.4 %collective-permute-start.1 = (bf16[128,2048]{1,0:T(8,128)(2,1)S(1)}, bf16[128,2048]{1,0:T(8,128)(2,1)S(1)}, u32[]{:S(2)}, u32[]{:S(2)}) collective-permute-start(bf16[128,2048]{1,0:T(8,128)(2,1)S(1)} %copy-done.3), channel_id=1, source_target_pairs={{0,4},{4,0},{8,12},{12,8},{16,20},{20,16},{24,28},{28,24},{1,5},{5... | collective-permute-start | bytes 1572872 | tf_op jit(solution)/shard_map/ppermute | solution.py:362
  28.1 14.2 %collective-permute-start.13 = (bf16[512,512]{1,0:T(8,128)(2,1)S(1)}, bf16[512,512]{1,0:T(8,128)(2,1)S(1)}, u32[]{:S(2)}, u32[]{:S(2)}) collective-permute-start(bf16[512,512]{1,0:T(8,128)(2,1)S(1)} %collective-permute-done.12.q_other), channel_id=1, source_target_pairs={{0,8},{4,12},{8,0},{12,4},{16,24},{20,28},{24,16},{28,20},{1,9},{5... | collective-permute-start | bytes 1572872 | tf_op jit(solution)/shard_map/ppermute | solution.py:365
  31.4 7.6 %collective-permute-start.14 = (bf16[128,2048]{1,0:T(8,128)(2,1)S(1)}, bf16[128,2048]{1,0:T(8,128)(2,1)S(1)}, u32[]{:S(2)}, u32[]{:S(2)}) collective-permute-start(bf16[128,2048]{1,0:T(8,128)(2,1)S(1)} %collective-permute-done.11.own), channel_id=1, source_target_pairs={{0,4},{4,0},{8,12},{12,8},{16,20},{20,16},{24,28},{28,24},{1,5},{5... | collective-permute-start | bytes 1572872 | tf_op jit(solution)/shard_map/ppermute | solution.py:362
  35.0 14.8 %collective-permute-start.18 = (bf16[512,512]{1,0:T(8,128)(2,1)S(1)}, bf16[512,512]{1,0:T(8,128)(2,1)S(1)}, u32[]{:S(2)}, u32[]{:S(2)}) collective-permute-start(bf16[512,512]{1,0:T(8,128)(2,1)S(1)} %get-tuple-element.70), channel_id=1, source_target_pairs={{0,16},{4,20},{8,24},{12,28},{16,0},{20,4},{24,8},{28,12},{1,17},{... | collective-permute-start | bytes 1572872 | tf_op jit(solution)/shard_map/ppermute | solution.py:365
  36.4 9.9 %collective-permute-start.17 = (bf16[64,256]{1,0:T(8,128)(2,1)S(1)}, bf16[64,256]{1,0:T(8,128)(2,1)S(1)}, u32[]{:S(2)}, u32[]{:S(2)}) collective-permute-start(bf16[64,256]{1,0:T(8,128)(2,1)S(1)} %kv_turn.1), channel_id=1, source_target_pairs={{0,2},{1,3},{2,0},{3,1},{4,6},{5,7},{6,4},{7,5},{8,10},{9,11},{10,... | collective-permute-start | bytes 98312 | tf_op jit(solution)/shard_map/ppermute | solution.py:374
  43.2 15.3 %collective-permute-start.15 = (bf16[256,512]{1,0:T(8,128)(2,1)S(1)}, bf16[256,512]{1,0:T(8,128)(2,1)S(1)}, u32[]{:S(2)}, u32[]{:S(2)}) collective-permute-start(bf16[256,512]{1,0:T(8,128)(2,1)S(1)} %q_late.3), channel_id=1, source_target_pairs={{0,16},{4,20},{8,24},{12,28},{16,0},{20,4},{24,8},{28,12},{1,17},{... | collective-permute-start | bytes 786440 | tf_op jit(solution)/shard_map/ppermute | solution.py:365
  49.9 5.1 %collective-permute-start.19 = (bf16[128,256]{1,0:T(8,128)(2,1)S(1)}, bf16[128,256]{1,0:T(8,128)(2,1)S(1)}, u32[]{:S(2)}, u32[]{:S(2)}) collective-permute-start(bf16[128,256]{1,0:T(8,128)(2,1)S(1)} %kv_join.1.refs_0_), channel_id=1, source_target_pairs={{0,8},{4,12},{8,0},{12,4},{16,24},{20,28},{24,16},{28,20},{1,9},{5... | collective-permute-start | bytes 196616 | tf_op jit(solution)/shard_map/ppermute | solution.py:365
  51.2 6.4 %collective-permute-start.20 = (bf16[128,256]{1,0:T(8,128)(2,1)S(1)}, bf16[128,256]{1,0:T(8,128)(2,1)S(1)}, u32[]{:S(2)}, u32[]{:S(2)}) collective-permute-start(bf16[128,256]{1,0:T(8,128)(2,1)S(1)} %kv_join.1.refs_0_), channel_id=1, source_target_pairs={{0,16},{4,20},{8,24},{12,28},{16,0},{20,4},{24,8},{28,12},{1,17},{... | collective-permute-start | bytes 196616 | tf_op jit(solution)/shard_map/ppermute | solution.py:365
  53.2 5.3 %collective-permute-start.21 = (bf16[128,256]{1,0:T(8,128)(2,1)S(1)}, bf16[128,256]{1,0:T(8,128)(2,1)S(1)}, u32[]{:S(2)}, u32[]{:S(2)}) collective-permute-start(bf16[128,256]{1,0:T(8,128)(2,1)S(1)} %kv_join.1.refs_0_), channel_id=1, source_target_pairs={{0,24},{4,28},{8,16},{12,20},{16,8},{20,12},{24,0},{28,4},{1,25},{... | collective-permute-start | bytes 196616 | tf_op jit(solution)/shard_map/ppermute | solution.py:365
  53.4 15.4 %collective-permute-start.24 = (bf16[512,512]{1,0:T(8,128)(2,1)S(1)}, bf16[512,512]{1,0:T(8,128)(2,1)S(1)}, u32[]{:S(2)}, u32[]{:S(2)}) collective-permute-start(bf16[512,512]{1,0:T(8,128)(2,1)S(1)} %get-tuple-element.74), channel_id=1, source_target_pairs={{0,16},{4,20},{8,24},{12,28},{16,0},{20,4},{24,8},{28,12},{1,17},{... | collective-permute-start | bytes 1572872 | tf_op jit(solution)/shard_map/ppermute | solution.py:365
  60.9 7.0 %collective-permute-start.25 = (bf16[256,512]{1,0:T(8,128)(2,1)S(1)}, bf16[256,512]{1,0:T(8,128)(2,1)S(1)}, u32[]{:S(2)}, u32[]{:S(2)}) collective-permute-start(bf16[256,512]{1,0:T(8,128)(2,1)S(1)} %attend.1.near), channel_id=1, source_target_pairs={{0,8},{4,12},{8,0},{12,4},{16,24},{20,28},{24,16},{28,20},{1,9},{5... | collective-permute-start | bytes 786440 | tf_op jit(solution)/shard_map/ppermute | solution.py:365
  67.9 4.9 %collective-permute-start.23 = (bf16[256,512]{1,0:T(8,128)(2,1)S(1)}, bf16[256,512]{1,0:T(8,128)(2,1)S(1)}, u32[]{:S(2)}, u32[]{:S(2)}) collective-permute-start(bf16[256,512]{1,0:T(8,128)(2,1)S(1)} %attend.1.near), channel_id=1, source_target_pairs={{0,4},{4,0},{8,12},{12,8},{16,20},{20,16},{24,28},{28,24},{1,5},{5... | collective-permute-start | bytes 786440 | tf_op jit(solution)/shard_map/ppermute | solution.py:362
  70.7 9.2 %collective-permute-start.27 = (bf16[128,1024]{1,0:T(8,128)(2,1)S(1)}, bf16[128,1024]{1,0:T(8,128)(2,1)S(1)}, u32[]{:S(2)}, u32[]{:S(2)}) collective-permute-start(bf16[128,1024]{1,0:T(8,128)(2,1)S(1)} %get-tuple-element.76), channel_id=1, source_target_pairs={{0,8},{4,12},{8,0},{12,4},{16,24},{20,28},{24,16},{28,20},{1,9},{5... | collective-permute-start | bytes 786440 | tf_op jit(solution)/shard_map/ppermute | solution.py:365
  72.5 13.2 %collective-permute-start.32 = (bf16[128,1024]{1,0:T(8,128)(2,1)S(1)}, bf16[128,1024]{1,0:T(8,128)(2,1)S(1)}, u32[]{:S(2)}, u32[]{:S(2)}) collective-permute-start(bf16[128,1024]{1,0:T(8,128)(2,1)S(1)} %get-tuple-element.82), channel_id=1, source_target_pairs={{0,8},{4,12},{8,0},{12,4},{16,24},{20,28},{24,16},{28,20},{1,9},{5... | collective-permute-start | bytes 786440 | tf_op jit(solution)/shard_map/ppermute | solution.py:365
  72.8 13.9 %collective-permute-start = (bf16[128,512]{1,0:T(8,128)(2,1)S(1)}, bf16[128,512]{1,0:T(8,128)(2,1)S(1)}, u32[]{:S(2)}, u32[]{:S(2)}) collective-permute-start(bf16[128,512]{1,0:T(8,128)(2,1)S(1)} %copy-done.11), channel_id=1, source_target_pairs={{0,4},{4,0},{8,12},{12,8},{16,20},{20,16},{24,28},{28,24},{1,5},{5... | collective-permute-start | bytes 393224 | tf_op jit(solution)/shard_map/ppermute | solution.py:362
  80.5 8.9 %collective-permute-start.28 = (bf16[128,512]{1,0:T(8,128)(2,1)S(1)}, bf16[128,512]{1,0:T(8,128)(2,1)S(1)}, u32[]{:S(2)}, u32[]{:S(2)}) collective-permute-start(bf16[128,512]{1,0:T(8,128)(2,1)S(1)} %get-tuple-element.78), channel_id=1, source_target_pairs={{0,1},{1,0},{2,3},{3,2},{4,5},{5,4},{6,7},{7,6},{8,9},{9,8},{10,11... | collective-permute-start | bytes 393224 | tf_op jit(solution)/shard_map/ppermute | solution.py:374
  81.0 13.7 %collective-permute-start.29 = (bf16[128,512]{1,0:T(8,128)(2,1)S(1)}, bf16[128,512]{1,0:T(8,128)(2,1)S(1)}, u32[]{:S(2)}, u32[]{:S(2)}) collective-permute-start(bf16[128,512]{1,0:T(8,128)(2,1)S(1)} %get-tuple-element.79), channel_id=1, source_target_pairs={{0,2},{1,3},{2,0},{3,1},{4,6},{5,7},{6,4},{7,5},{8,10},{9,11},{10,... | collective-permute-start | bytes 393224 | tf_op jit(solution)/shard_map/ppermute | solution.py:374
  83.6 11.1 %collective-permute-start.30 = (bf16[128,512]{1,0:T(8,128)(2,1)S(1)}, bf16[128,512]{1,0:T(8,128)(2,1)S(1)}, u32[]{:S(2)}, u32[]{:S(2)}) collective-permute-start(bf16[128,512]{1,0:T(8,128)(2,1)S(1)} %get-tuple-element.80), channel_id=1, source_target_pairs={{0,3},{1,2},{2,1},{3,0},{4,7},{5,6},{6,5},{7,4},{8,11},{9,10},{10,... | collective-permute-start | bytes 393224 | tf_op jit(solution)/shard_map/ppermute | solution.py:374
  86.3 8.6 %collective-permute-start.33 = (bf16[128,512]{1,0:T(8,128)(2,1)S(1)}, bf16[128,512]{1,0:T(8,128)(2,1)S(1)}, u32[]{:S(2)}, u32[]{:S(2)}) collective-permute-start(bf16[128,512]{1,0:T(8,128)(2,1)S(1)} %get-tuple-element.84), channel_id=1, source_target_pairs={{0,1},{1,0},{2,3},{3,2},{4,5},{5,4},{6,7},{7,6},{8,9},{9,8},{10,11... | collective-permute-start | bytes 393224 | tf_op jit(solution)/shard_map/ppermute | solution.py:374
  86.6 18.2 %collective-permute-start.34 = (bf16[128,512]{1,0:T(8,128)(2,1)S(1)}, bf16[128,512]{1,0:T(8,128)(2,1)S(1)}, u32[]{:S(2)}, u32[]{:S(2)}) collective-permute-start(bf16[128,512]{1,0:T(8,128)(2,1)S(1)} %get-tuple-element.85), channel_id=1, source_target_pairs={{0,2},{1,3},{2,0},{3,1},{4,6},{5,7},{6,4},{7,5},{8,10},{9,11},{10,... | collective-permute-start | bytes 393224 | tf_op jit(solution)/shard_map/ppermute | solution.py:374
  89.4 15.4 %collective-permute-start.35 = (bf16[128,512]{1,0:T(8,128)(2,1)S(1)}, bf16[128,512]{1,0:T(8,128)(2,1)S(1)}, u32[]{:S(2)}, u32[]{:S(2)}) collective-permute-start(bf16[128,512]{1,0:T(8,128)(2,1)S(1)} %get-tuple-element.86), channel_id=1, source_target_pairs={{0,3},{1,2},{2,1},{3,0},{4,7},{5,6},{6,5},{7,4},{8,11},{9,10},{10,... | collective-permute-start | bytes 393224 | tf_op jit(solution)/shard_map/ppermute | solution.py:374
  94.8 10.0 %collective-permute-start.31 = (bf16[128,512]{1,0:T(8,128)(2,1)S(1)}, bf16[128,512]{1,0:T(8,128)(2,1)S(1)}, u32[]{:S(2)}, u32[]{:S(2)}) collective-permute-start(bf16[128,512]{1,0:T(8,128)(2,1)S(1)} %mix_give.1), channel_id=1, source_target_pairs={{0,4},{4,0},{8,12},{12,8},{16,20},{20,16},{24,28},{28,24},{1,5},{5... | collective-permute-start | bytes 393224 | tf_op jit(solution)/shard_map/ppermute | solution.py:362
  (16 other events, 203.4 us)
